TPU v7x, 512 devices: a whole 4x4x16 slice. The times are simulated.
512 devices in a mesh: row: 32 (over y, z_hi, core), chan: 16 (over z_lo, x).
Axes of the slice: x: 4, y: 4, z: 16 (z_hi: 4, z_lo: 4; z = z_hi * 4 + z_lo), core: 2. Of those that a mesh axis runs over, the one named last changes fastest.
Arguments:
- pair_rep: bfloat16 [672, 672, 128], P('row', 'chan'), may hold values from -6 to 6
- in_weights: bfloat16 [2, 128, 640], replicated, may hold values from -0.5 to 0.5
- out_weights: bfloat16 [2, 128, 128], replicated, may hold values from -0.5 to 0.5
Outputs:
- pair_out: bfloat16 [672, 672, 128], P('row', 'chan')
All inputs are finite; a program needn't handle non-finite values.
Results may differ from a plain program's by a relative error of at most 0.018.
Values may be sent and summed in bfloat16 or wider, within the bound.
No kernel may reach another device: no remote copies, remote signals or barrier semaphores. Data moves between devices by JAX's collectives and lax.ppermute only.
A program may use at most 64 MiB of HBM per device.

v0:
```python
import functools

import jax
import jax.numpy as jnp
import numpy as np
from jax import lax
from jax.experimental import pallas as pl
from jax.experimental.pallas import tpu as pltpu
from jax.sharding import Mesh, PartitionSpec as P

PARTS = (("y1", 2), ("y0", 2), ("zh", 4), ("core", 2), ("zl", 4), ("x", 4))
ROW = ("y1", "y0", "zh", "core")
CHAN = ("zl", "x")
GROUP = ("zl", "x", "y1", "zh")
SWAP = [(0, 1), (1, 0)]
ROWS, COLS, C = 21, 42, 128
T, U = 7, 3
F32, BF16 = jnp.float32, jnp.bfloat16


def spread():
    table = np.zeros((4, 128, U, 256), np.float32)
    for x in range(4):
        for u in range(U):
            for q in range(COLS):
                table[x, COLS * u + q, u, COLS * x + q] = 1
    return table.reshape(512, U * 256)


def spread_rows():
    table = np.zeros((2, 4, 128, U, 128), np.float32)
    for core in range(2):
        for x in range(4):
            for u in range(U):
                for t in range(T):
                    for w in range(U):
                        table[core, x, COLS * u + ROWS * core + U * t + w, u, 32 * w + 8 * x + t] = 1
    return table.reshape(2, 512, U * 128)


def gather_rows():
    table = np.zeros((U, 2, U, 8, 8, 8, 128), np.float32)
    for u in range(U):
        for core in range(2):
            for v in range(U):
                for t in range(T):
                    for s in range(8):
                        table[u, core, v, s, t, s, COLS * u + ROWS * core + U * t + v] = 1
    return table.reshape(U * 2 * U * 64, 8 * 128)


def dot(a, b, on_a, on_b):
    return lax.dot_general(a, b, (((on_a,), (on_b,)), ((), ())), preferred_element_type=F32)


def layer_norm(values, axis_index):
    average = jnp.mean(values, axis=axis_index, keepdims=True)
    centred = values - average
    variance = jnp.mean(centred * centred, axis=axis_index, keepdims=True)
    return centred * lax.rsqrt(variance + 1e-05)


def emit_edges(blocks, w_ref, msg_ref, gate_ref):
    lefts, rights = [], []
    for t in range(T):
        normed = layer_norm(blocks[t], 1).astype(BF16)
        projected = dot(w_ref[:, : 4 * C], normed, 0, 1)
        lefts.append(jax.nn.sigmoid(projected[C : 2 * C]) * projected[:C])
        rights.append(jax.nn.sigmoid(projected[3 * C : 4 * C]) * projected[2 * C : 3 * C])
        gate_ref[t] = jax.nn.sigmoid(dot(normed, w_ref[:, 4 * C :], 1, 0)).astype(BF16)
    none = jnp.zeros((C, 128), F32)
    both = jnp.stack(lefts + [none] + rights + [none], axis=0)
    msg_ref[...] = jnp.swapaxes(both, 0, 1).astype(BF16)


def updated(x_ref, p_ref, gate_ref, w_ref):
    product = jnp.swapaxes(x_ref[...].astype(F32), 0, 1)
    blocks = []
    for t in range(T):
        normed = layer_norm(product[t], 0).astype(BF16)
        outward = dot(normed, w_ref[...], 0, 0)
        blocks.append((p_ref[t].astype(F32) + gate_ref[t].astype(F32) * outward).astype(BF16))
    return blocks


def first_kernel(p_ref, w_ref, msg_ref, gate_ref, flat_ref):
    blocks = []
    for t in range(T):
        rows = [p_ref[U * t + u].astype(F32) for u in range(U)]
        block = jnp.concatenate(rows + [jnp.zeros((2, C), F32)], axis=0)
        flat_ref[t] = block.astype(BF16)
        blocks.append(block)
    emit_edges(blocks, w_ref, msg_ref, gate_ref)


def middle_kernel(x_ref, p_ref, gate_ref, wo_ref, w_ref, msg_ref, gate_next_ref, flat_ref):
    blocks = updated(x_ref, p_ref, gate_ref, wo_ref)
    for t in range(T):
        flat_ref[t] = blocks[t]
    emit_edges([block.astype(F32) for block in blocks], w_ref, msg_ref, gate_next_ref)


def last_kernel(x_ref, p_ref, gate_ref, wo_ref, out_ref):
    blocks = updated(x_ref, p_ref, gate_ref, wo_ref)
    for t in range(T):
        block = blocks[t].astype(F32)
        for u in range(U):
            out_ref[U * t + u] = block[COLS * u : COLS * (u + 1)].astype(BF16)


def fan(get, zl, table):
    return dot(jnp.concatenate([get(4 * zl + x) for x in range(4)], axis=1), table, 1, 0)


def outgoing_kernel(y0_ref, msg_ref, near_ref, far_ref, spread_ref, gather_ref, out_ref, left, right):
    y0 = y0_ref[0]
    table = spread_ref[...]

    def unpack(get, put):
        for zl in range(4):
            part = fan(get, zl, table)
            if part.shape[0] == 128:
                part = part.reshape(8, 2, 8, U * 256)[:, 0].reshape(64, U * 256)
            part = part.astype(BF16)
            for u in range(U):
                put(u, zl, part[:, 256 * u : 256 * (u + 1)])

    def put_left(u, zl, part):
        left[64 * u : 64 * (u + 1), 256 * zl : 256 * (zl + 1)] = part

    unpack(lambda at: msg_ref[at], put_left)
    for core in range(2):
        for ref, at in ((near_ref, y0), (far_ref, 1 - y0)):

            def put_right(v, zl, part, core=core, at=at):
                right[at, 192 * core + 64 * v : 192 * core + 64 * (v + 1), 256 * zl : 256 * (zl + 1)] = part

            unpack(lambda m, ref=ref, core=core: ref[core, m], put_right)
    for y in range(2):
        product = dot(left[...], right[y], 1, 1).astype(BF16)
        wide = jnp.concatenate([product[64 * u : 64 * (u + 1)] for u in range(U)], axis=1)
        packed = dot(wide, gather_ref[...], 1, 0).astype(BF16)
        for s in range(8):
            y1, zh = divmod(s, 4)
            out_ref[(2 * y1 + y) * 4 + zh] = packed[:, 128 * s : 128 * (s + 1)]


def incoming_kernel(at_ref, msg_ref, spread_ref, rows_ref, gather_ref, near_ref, far_ref, left, right):
    y0, mine = at_ref[0], at_ref[1]
    table, rows = spread_ref[...], rows_ref[mine]
    for core in range(2):
        for zl in range(4):
            wide = jnp.concatenate([msg_ref[core, 4 * zl + x] for x in range(4)], axis=1)
            lefts = dot(wide, rows, 1, 0).reshape(8, 2, 8, U * 128)[:, 0].reshape(64, U * 128).astype(BF16)
            rights = dot(wide, table, 1, 0).reshape(8, 2, 8, U * 256)[:, 1].reshape(64, U * 256).astype(BF16)
            y1, y = divmod(zl, 2)
            for u in range(U):
                at = 192 * core + 64 * u
                left[y, at : at + 64, 128 * y1 : 128 * (y1 + 1)] = lefts[:, 128 * u : 128 * (u + 1)]
                right[at : at + 64, 256 * zl : 256 * (zl + 1)] = rights[:, 256 * u : 256 * (u + 1)]
    for ref, at in ((far_ref, 1 - y0), (near_ref, y0)):
        product = dot(left[at], right[...], 0, 0).astype(BF16)
        wide = []
        for zl in range(4):
            for y1 in range(2):
                part = [product[128 * y1 + 32 * w : 128 * y1 + 32 * (w + 1), 256 * zl : 256 * (zl + 1)] for w in range(U)]
                wide.append(jnp.concatenate(part, axis=1))
        packed = dot(jnp.concatenate(wide, axis=0), gather_ref[...], 1, 0).astype(BF16)
        for zl in range(4):
            for x in range(4):
                ref[4 * zl + x] = packed[64 * zl : 64 * (zl + 1), 128 * x : 128 * (x + 1)]


VMEM = pl.BlockSpec(memory_space=pltpu.VMEM)
SMEM = pl.BlockSpec(memory_space=pltpu.SMEM)


def call(kernel, outs, args, name, scratch=(), scalars=0):
    flops = 200_000_000
    moved = sum(a.size * a.dtype.itemsize for a in args) + sum(2 * int(np.prod(s)) for s in outs)
    return pl.pallas_call(
        kernel,
        out_shape=[jax.ShapeDtypeStruct(s, BF16) for s in outs],
        in_specs=[SMEM] * scalars + [VMEM] * (len(args) - scalars),
        out_specs=[VMEM] * len(outs),
        scratch_shapes=[pltpu.VMEM(s, BF16) for s in scratch],
        compiler_params=pltpu.CompilerParams(vmem_limit_bytes=48 * 1024 * 1024),
        cost_estimate=pl.CostEstimate(flops=flops, bytes_accessed=moved, transcendentals=400_000),
        name=name,
    )(*args)


FLAT = (T, 128, C)
MSG = (C, 16, 128)


def shards(pair_rep, in_weights, out_weights):
    table = jnp.asarray(spread(), BF16)
    y0, core = lax.axis_index("y0"), lax.axis_index("core")

    msg, gate, flat = call(first_kernel, [MSG, FLAT, FLAT], (pair_rep, in_weights[0]), "edges")
    msg = lax.all_to_all(msg, GROUP, 0, 0, tiled=True)
    right = msg[:, 8:]
    far = lax.ppermute(right, "y0", SWAP)
    near = lax.all_gather(right, "core", axis=0).reshape(2, 16, 64, 128)
    far = lax.all_gather(far, "core", axis=0).reshape(2, 16, 64, 128)
    (product,) = call(
        outgoing_kernel,
        [(16, 64, 128)],
        (y0[None].astype(jnp.int32), msg.reshape(16, 128, 128), near, far, table, jnp.asarray(gather_rows(), BF16)),
        "outgoing", scratch=[(192, 1024), (2, 384, 1024)], scalars=1,
    )
    product = lax.all_to_all(product.reshape(128, 8, 128), GROUP, 0, 0, tiled=True)
    msg, gate, flat = call(
        middle_kernel, [MSG, FLAT, FLAT], (product, flat, gate, out_weights[0], in_weights[1]), "update_edges"
    )
    msg = lax.all_to_all(msg, GROUP, 0, 0, tiled=True)
    both = lax.all_gather(msg, "core", axis=0).reshape(2, 16, 128, 128)
    near, far = call(
        incoming_kernel,
        [(16, 64, 128)] * 2,
        (jnp.stack([y0, core]).astype(jnp.int32), both, table, jnp.asarray(spread_rows(), BF16), jnp.asarray(spread().T, BF16)),
        "incoming", scratch=[(2, 384, 256), (384, 1024)], scalars=1,
    )
    far = lax.ppermute(far, "y0", SWAP)
    product = (near.astype(F32) + far.astype(F32)).astype(BF16)
    product = lax.all_to_all(product.reshape(128, 8, 128), GROUP, 0, 0, tiled=True)
    (out,) = call(last_kernel, [(ROWS, COLS, C)], (product, flat, gate, out_weights[1]), "update")
    return out


def solution(mesh):
    parts = Mesh(mesh.devices.reshape([size for _, size in PARTS]), [name for name, _ in PARTS])
    spec = P(ROW, CHAN, None)
    return jax.shard_map(shards, mesh=parts, in_specs=(spec, P(), P()), out_specs=spec, check_vma=False)
```

profile of v0, /device:TPU:32, one launch (start us, length us, event | category | flops | bytes accessed | tf_op | source)
XLA Modules:
  0.0 231.8 jit_solution(15808167741848129221)
XLA Ops:
  6.5 0.0 copy-start
  6.5 1.1 slice_bitcast_fusion
  7.6 0.0 copy-start.7
  7.6 0.9 copy-done.7
  8.6 1.2 edges.1
  9.8 55.5 %all_to_all.20 = bf16[128,16,128]{2,1,0:T(8,128)(2,1)S(1)} all-to-all(bf16[128,16,128]{2,1,0:T(8,128)(2,1)S(1)} %get-tuple-element.13), channel_id=1, replica_groups=mesh['y1'=2,'y0'=2,'zh'=4,'core'=2,'zl'=4,'x'=4] {'zl','x','y1','zh'}, dimensions={0} | all-to-all | bytes 1048576 | tf_op jit(solution)/shard_map/all_to_all | solution.py:202
  65.4 2.6 %collective-permute-start = (bf16[128,8,128]{2,1,0:T(8,128)(2,1)S(1)}, bf16[128,8,128]{2,1,0:T(8,128)(2,1)S(1)}, u32[]{:S(2)}, u32[]{:S(2)}) collective-permute-start(bf16[128,8,128]{2,1,0:T(8,128)(2,1)S(1)} %slice.20), channel_id=1, source_target_pairs={{0,128},{128,0},{1,129},{129,1},{2,130},{130,2},{3,131},{131,3},{4... | collective-permute-start | bytes 786440 | tf_op jit(solution)/shard_map/ppermute | solution.py:204
  68.0 2.2 all-gather
  70.1 3.5 %collective-permute-done = bf16[128,8,128]{2,1,0:T(8,128)(2,1)S(1)} collective-permute-done((bf16[128,8,128]{2,1,0:T(8,128)(2,1)S(1)}, bf16[128,8,128]{2,1,0:T(8,128)(2,1)S(1)}, u32[]{:S(2)}, u32[]{:S(2)}) %collective-permute-start) | collective-permute-done | bytes 262176 | tf_op jit(solution)/shard_map/ppermute | solution.py:204
  73.6 2.2 all-gather.1
  75.8 0.0 copy-done
  75.8 0.0 copy-start.1
  75.8 1.7 copy-done.1
  77.5 0.0 copy-start.8
  77.5 5.1 %outgoing.1 = bf16[16,64,128]{2,1,0:T(8,128)(2,1)} custom-call(s32[1]{0:T(128)} %bitcast.y0_ref, bf16[16,128,128]{2,1,0:T(8,128)(2,1)S(1)} %bitcast.16, bf16[2,16,64,128]{3,2,1,0:T(8,128)(2,1)S(1)} %bitcast.17, bf16[2,16,64,128]{3,2,1,0:T(8,128)(2,1)S(1)} %bitcast.18, bf16[512,768]{1,0:T(8,128)(2,1)S(1)} %copy-done, bf16[1152,1024]{1,0:T(8,128)(2,1)S(1)} %copy-done.1), custom_call_target="tpu_custom_call" | custom-call | flops 200000000 | bytes 4980740 | tf_op jit(solution)/shard_map/outgoing/pallas_call | solution.py:181
  82.6 0.0 copy-start.3
  82.6 0.0 copy-start.4
  82.6 8.8 %all-to-all-start.1 = ((bf16[128,8,128]{2,1,0:T(8,128)(2,1)}), bf16[128,8,128]{2,1,0:T(8,128)(2,1)S(1)}, u32[]{:S(2)}, u32[]{:S(2)}) async-start(bf16[128,8,128]{2,1,0:T(8,128)(2,1)} %bitcast.6), calls=%async_computation.1 | async-start | bytes 524288 | tf_op jit(solution)/shard_map/all_to_all | solution.py:213
  91.3 0.0 all-gather.5.cloned.1.call-start
  91.4 0.0 copy-done.8
  91.4 23.4 %all-to-all-done.1.x_ref = bf16[128,8,128]{2,1,0:T(8,128)(2,1)S(1)} async-done(((bf16[128,8,128]{2,1,0:T(8,128)(2,1)}), bf16[128,8,128]{2,1,0:T(8,128)(2,1)S(1)}, u32[]{:S(2)}, u32[]{:S(2)}) %all-to-all-start.1) | async-done | bytes 262176 | tf_op jit(solution)/shard_map/all_to_all | solution.py:213
  114.8 1.5 update_edges.1
  116.3 0.0 copy-start.5
  116.3 0.7 copy-done.5
  117.0 40.6 %all_to_all.21 = bf16[128,16,128]{2,1,0:T(8,128)(2,1)} all-to-all(bf16[128,16,128]{2,1,0:T(8,128)(2,1)S(1)} %get-tuple-element.16), channel_id=1, replica_groups=mesh['y1'=2,'y0'=2,'zh'=4,'core'=2,'zl'=4,'x'=4] {'zl','x','y1','zh'}, dimensions={0} | all-to-all | bytes 1048576 | tf_op jit(solution)/shard_map/all_to_all | solution.py:217
  157.6 0.0 all-gather.5.cloned.1.call-update
  157.7 0.1 pad_add_fusion.at_ref
  157.7 9.5 %all-gather.5.cloned.1.call-done = bf16[256,16,128]{2,1,0:T(8,128)(2,1)} async-done(((bf16[128,16,128]{2,1,0:T(8,128)(2,1)}), bf16[256,16,128]{2,1,0:T(8,128)(2,1)}) %all-gather.5.cloned.1.call-update) | async-done | bytes 1048592 | tf_op jit(solution)/shard_map/all_gather | solution.py:218
  167.2 0.0 copy-done.3
  167.2 0.0 copy-done.4
  167.2 0.0 copy-start.2
  167.2 1.2 copy-done.2
  168.5 0.0 copy-start.6
  168.5 3.3 %incoming.1 = (bf16[16,64,128]{2,1,0:T(8,128)(2,1)S(1)}, bf16[16,64,128]{2,1,0:T(8,128)(2,1)S(1)}) custom-call(s32[2]{0:T(128)S(1)} %pad_add_fusion.at_ref, bf16[2,16,128,128]{3,2,1,0:T(8,128)(2,1)S(1)} %bitcast.19, bf16[512,768]{1,0:T(8,128)(2,1)S(1)} %copy-done, bf16[2,512,384]{2,1,0:T(8,128)(2,1)S(1)} %copy-done.3, bf16[768,512]{1,0:T(8,128)(2,1)S(1)} %copy-done.4), custom_call_target="tpu_custom_call" | custom-call | flops 200000000 | bytes 3932168 | tf_op jit(solution)/shard_map/incoming/pallas_call | solution.py:181
  171.8 3.4 %collective-permute-start.1 = (bf16[16,64,128]{2,1,0:T(8,128)(2,1)S(1)}, bf16[16,64,128]{2,1,0:T(8,128)(2,1)S(1)}, u32[]{:S(2)}, u32[]{:S(2)}) collective-permute-start(bf16[16,64,128]{2,1,0:T(8,128)(2,1)S(1)} %get-tuple-element.18), channel_id=1, source_target_pairs={{0,128},{128,0},{1,129},{129,1},{2,130},{130,2},{3,131},{131,3},{4... | collective-permute-start | bytes 786440 | tf_op jit(solution)/shard_map/ppermute | solution.py:225
  175.2 7.0 %collective-permute-done.1 = bf16[16,64,128]{2,1,0:T(8,128)(2,1)S(1)} collective-permute-done((bf16[16,64,128]{2,1,0:T(8,128)(2,1)S(1)}, bf16[16,64,128]{2,1,0:T(8,128)(2,1)S(1)}, u32[]{:S(2)}, u32[]{:S(2)}) %collective-permute-start.1) | collective-permute-done | bytes 262176 | tf_op jit(solution)/shard_map/ppermute | solution.py:225
  182.2 0.1 add_convert_fusion
  182.2 41.5 %all_to_all.22.x_ref = bf16[128,8,128]{2,1,0:T(8,128)(2,1)S(1)} all-to-all(bf16[128,8,128]{2,1,0:T(8,128)(2,1)S(1)} %bitcast.20), channel_id=1, replica_groups=mesh['y1'=2,'y0'=2,'zh'=4,'core'=2,'zl'=4,'x'=4] {'zl','x','y1','zh'}, dimensions={0} | all-to-all | bytes 524288 | tf_op jit(solution)/shard_map/all_to_all | solution.py:227
  223.7 0.0 copy-done.6
  223.7 1.2 update.1
  (2 shorter events, 0.0 us)
Async XLA Ops:
  6.5 69.3 %copy-start = (bf16[512,768]{1,0:T(8,128)(2,1)S(1)}, bf16[512,768]{1,0:T(8,128)(2,1)}, u32[]{:S(2)}) copy-start(bf16[512,768]{1,0:T(8,128)(2,1)} %constant.18.clone.spread_ref) | copy-start | bytes 2359300
  7.6 1.0 copy-start.7
  65.4 8.3 %collective-permute-start = (bf16[128,8,128]{2,1,0:T(8,128)(2,1)S(1)}, bf16[128,8,128]{2,1,0:T(8,128)(2,1)S(1)}, u32[]{:S(2)}, u32[]{:S(2)}) collective-permute-start(bf16[128,8,128]{2,1,0:T(8,128)(2,1)S(1)} %slice.20), channel_id=1, source_target_pairs={{0,128},{128,0},{1,129},{129,1},{2,130},{130,2},{3,131},{131,3},{4... | collective-permute-start | bytes 786440 | tf_op jit(solution)/shard_map/ppermute | solution.py:204
  75.8 1.7 copy-start.1
  77.5 13.9 %copy-start.8 = (bf16[2,128,128]{2,1,0:T(8,128)(2,1)S(1)}, bf16[2,128,128]{2,1,0:T(8,128)(2,1)}, u32[]{:S(2)}) copy-start(bf16[2,128,128]{2,1,0:T(8,128)(2,1)} %param.9) | copy-start | bytes 196612
  82.6 84.7 %copy-start.3 = (bf16[2,512,384]{2,1,0:T(8,128)(2,1)S(1)}, bf16[2,512,384]{2,1,0:T(8,128)(2,1)}, u32[]{:S(2)}) copy-start(bf16[2,512,384]{2,1,0:T(8,128)(2,1)} %constant.20.clone.rows_ref) | copy-start | bytes 2359300
  82.6 84.7 %copy-start.4 = (bf16[768,512]{1,0:T(8,128)(2,1)S(1)}, bf16[768,512]{1,0:T(8,128)(2,1)}, u32[]{:S(2)}) copy-start(bf16[768,512]{1,0:T(8,128)(2,1)} %constant.21.clone.gather_ref) | copy-start | bytes 2359300
  82.6 32.3 %all-to-all-start.1 = ((bf16[128,8,128]{2,1,0:T(8,128)(2,1)}), bf16[128,8,128]{2,1,0:T(8,128)(2,1)S(1)}, u32[]{:S(2)}, u32[]{:S(2)}) async-start(bf16[128,8,128]{2,1,0:T(8,128)(2,1)} %bitcast.6), calls=%async_computation.1 | async-start | bytes 524288 | tf_op jit(solution)/shard_map/all_to_all | solution.py:213
  91.3 75.9 %all-gather.5.cloned.1.call-start = ((), (), s32[]{:S(2)}) async-start(), calls=%async_computation.4 | async-start | bytes 1572864 | tf_op jit(solution)/shard_map/all_gather | solution.py:218
  116.3 0.7 copy-start.5
  167.2 1.2 copy-start.2
  168.5 55.3 %copy-start.6 = (bf16[7,128,128]{2,1,0:T(8,128)(2,1)S(1)}, bf16[7,128,128]{2,1,0:T(8,128)(2,1)}, u32[]{:S(2)}) copy-start(bf16[7,128,128]{2,1,0:T(8,128)(2,1)} %copy-done.5) | copy-start | bytes 688132
  171.8 10.4 %collective-permute-start.1 = (bf16[16,64,128]{2,1,0:T(8,128)(2,1)S(1)}, bf16[16,64,128]{2,1,0:T(8,128)(2,1)S(1)}, u32[]{:S(2)}, u32[]{:S(2)}) collective-permute-start(bf16[16,64,128]{2,1,0:T(8,128)(2,1)S(1)} %get-tuple-element.18), channel_id=1, source_target_pairs={{0,128},{128,0},{1,129},{129,1},{2,130},{130,2},{3,131},{131,3},{4... | collective-permute-start | bytes 786440 | tf_op jit(solution)/shard_map/ppermute | solution.py:225
Sparse Core Ops, SparseCore 0:
  157.8 9.4 all-gather.4
where the time goes:
time: 232 us
  blocking collectives  142 us (61%)
  waiting for transfers between devices  43.4 us (19%)
  starting transfers between devices  14.8 us (6%)
  between operations  13.5 us (6%)
  Pallas kernels  12.2 us (5%)
  local copies, waits for them, and re-layouts  5.66 us (2%)
    all_to_all x2, blocking collectives, shards(): msg = lax.all_to_all(msg, GROUP, 0, 0, tiled=True)  96.2 us
    all_to_all x1, blocking collectives, shards(): lax.all_to_all(product.reshape(128, 8, 128), GROUP, 0, 0, tiled=True)  41.5 us
    all_to_all x1, waiting for transfers between devices, shards(): lax.all_to_all(product.reshape(128, 8, 128), GROUP, 0, 0, tiled=True)  23.4 us
    pallas_call x5, Pallas kernels, call(): pl.pallas_call(kernel, out_shape=[jax.ShapeDtypeStruct(s, BF16) for s in...  12.2 us
    all_gather x1, waiting for transfers between devices, shards(): both = lax.all_gather(msg, 'core', axis=0).reshape(2, 16, 128, 128)  9.49 us
    all_to_all x1, starting transfers between devices, shards(): lax.all_to_all(product.reshape(128, 8, 128), GROUP, 0, 0, tiled=True)  8.76 us
    ppermute x1, waiting for transfers between devices, shards(): far = lax.ppermute(far, 'y0', SWAP)  7.01 us
  transfers between devices with their start and end apart: 4, of which 4 were waited for; matrix products, arithmetic and copies ran while one was open for 0% of the time, Pallas kernels for 0%

commit v1 on v0

--- a/solution.py
+++ b/solution.py
@@ -60,25 +60,25 @@
     return centred * lax.rsqrt(variance + 1e-05)
 
 
-def emit_edges(blocks, w_ref, msg_ref, gate_ref):
+def emit_edges(blocks, w_ref, step, msg_ref, gate_ref):
     lefts, rights = [], []
     for t in range(T):
         normed = layer_norm(blocks[t], 1).astype(BF16)
-        projected = dot(w_ref[:, : 4 * C], normed, 0, 1)
+        projected = dot(w_ref[step, :, : 4 * C], normed, 0, 1)
         lefts.append(jax.nn.sigmoid(projected[C : 2 * C]) * projected[:C])
         rights.append(jax.nn.sigmoid(projected[3 * C : 4 * C]) * projected[2 * C : 3 * C])
-        gate_ref[t] = jax.nn.sigmoid(dot(normed, w_ref[:, 4 * C :], 1, 0)).astype(BF16)
+        gate_ref[t] = jax.nn.sigmoid(dot(normed, w_ref[step, :, 4 * C :], 1, 0)).astype(BF16)
     none = jnp.zeros((C, 128), F32)
     both = jnp.stack(lefts + [none] + rights + [none], axis=0)
     msg_ref[...] = jnp.swapaxes(both, 0, 1).astype(BF16)
 
 
-def updated(x_ref, p_ref, gate_ref, w_ref):
+def updated(x_ref, p_ref, gate_ref, w_ref, step):
     product = jnp.swapaxes(x_ref[...].astype(F32), 0, 1)
     blocks = []
     for t in range(T):
         normed = layer_norm(product[t], 0).astype(BF16)
-        outward = dot(normed, w_ref[...], 0, 0)
+        outward = dot(normed, w_ref[step], 0, 0)
         blocks.append((p_ref[t].astype(F32) + gate_ref[t].astype(F32) * outward).astype(BF16))
     return blocks
 
@@ -90,18 +90,18 @@
         block = jnp.concatenate(rows + [jnp.zeros((2, C), F32)], axis=0)
         flat_ref[t] = block.astype(BF16)
         blocks.append(block)
-    emit_edges(blocks, w_ref, msg_ref, gate_ref)
+    emit_edges(blocks, w_ref, 0, msg_ref, gate_ref)
 
 
 def middle_kernel(x_ref, p_ref, gate_ref, wo_ref, w_ref, msg_ref, gate_next_ref, flat_ref):
-    blocks = updated(x_ref, p_ref, gate_ref, wo_ref)
+    blocks = updated(x_ref, p_ref, gate_ref, wo_ref, 0)
     for t in range(T):
         flat_ref[t] = blocks[t]
-    emit_edges([block.astype(F32) for block in blocks], w_ref, msg_ref, gate_next_ref)
+    emit_edges([block.astype(F32) for block in blocks], w_ref, 1, msg_ref, gate_next_ref)
 
 
 def last_kernel(x_ref, p_ref, gate_ref, wo_ref, out_ref):
-    blocks = updated(x_ref, p_ref, gate_ref, wo_ref)
+    blocks = updated(x_ref, p_ref, gate_ref, wo_ref, 1)
     for t in range(T):
         block = blocks[t].astype(F32)
         for u in range(U):
@@ -112,7 +112,9 @@
     return dot(jnp.concatenate([get(4 * zl + x) for x in range(4)], axis=1), table, 1, 0)
 
 
-def outgoing_kernel(y0_ref, msg_ref, near_ref, far_ref, spread_ref, gather_ref, out_ref, left, right):
+def outgoing_kernel(y0_ref, msg_ref, near_ref, far_ref, spread_ref, gather_hbm, out_ref, left, right, gather_ref, done):
+    fetch = pltpu.make_async_copy(gather_hbm, gather_ref, done)
+    fetch.start()
     y0 = y0_ref[0]
     table = spread_ref[...]
 
@@ -136,6 +138,7 @@
                 right[at, 192 * core + 64 * v : 192 * core + 64 * (v + 1), 256 * zl : 256 * (zl + 1)] = part
 
             unpack(lambda m, ref=ref, core=core: ref[core, m], put_right)
+    fetch.wait()
     for y in range(2):
         product = dot(left[...], right[y], 1, 1).astype(BF16)
         wide = jnp.concatenate([product[64 * u : 64 * (u + 1)] for u in range(U)], axis=1)
@@ -145,19 +148,21 @@
             out_ref[(2 * y1 + y) * 4 + zh] = packed[:, 128 * s : 128 * (s + 1)]
 
 
-def incoming_kernel(at_ref, msg_ref, spread_ref, rows_ref, gather_ref, near_ref, far_ref, left, right):
+def incoming_kernel(at_ref, left_ref, right_ref, spread_ref, rows_ref, gather_hbm, near_ref, far_ref, left, right, gather_ref, done):
+    fetch = pltpu.make_async_copy(gather_hbm, gather_ref, done)
+    fetch.start()
     y0, mine = at_ref[0], at_ref[1]
     table, rows = spread_ref[...], rows_ref[mine]
     for core in range(2):
         for zl in range(4):
-            wide = jnp.concatenate([msg_ref[core, 4 * zl + x] for x in range(4)], axis=1)
-            lefts = dot(wide, rows, 1, 0).reshape(8, 2, 8, U * 128)[:, 0].reshape(64, U * 128).astype(BF16)
-            rights = dot(wide, table, 1, 0).reshape(8, 2, 8, U * 256)[:, 1].reshape(64, U * 256).astype(BF16)
+            lefts = fan(lambda m: left_ref[core, m], zl, rows).astype(BF16)
+            rights = fan(lambda m: right_ref[core, m], zl, table).astype(BF16)
             y1, y = divmod(zl, 2)
             for u in range(U):
                 at = 192 * core + 64 * u
                 left[y, at : at + 64, 128 * y1 : 128 * (y1 + 1)] = lefts[:, 128 * u : 128 * (u + 1)]
                 right[at : at + 64, 256 * zl : 256 * (zl + 1)] = rights[:, 256 * u : 256 * (u + 1)]
+    fetch.wait()
     for ref, at in ((far_ref, 1 - y0), (near_ref, y0)):
         product = dot(left[at], right[...], 0, 0).astype(BF16)
         wide = []
@@ -175,19 +180,23 @@
 SMEM = pl.BlockSpec(memory_space=pltpu.SMEM)
 
 
-def call(kernel, outs, args, name, scratch=(), scalars=0):
+HBM = pl.BlockSpec(memory_space=pl.ANY)
+
+
+def call(kernel, outs, args, name, scratch=(), scalars=0, fetched=None):
     flops = 200_000_000
     moved = sum(a.size * a.dtype.itemsize for a in args) + sum(2 * int(np.prod(s)) for s in outs)
     return pl.pallas_call(
         kernel,
         out_shape=[jax.ShapeDtypeStruct(s, BF16) for s in outs],
-        in_specs=[SMEM] * scalars + [VMEM] * (len(args) - scalars),
+        in_specs=[SMEM] * scalars + [VMEM] * (len(args) - scalars) + [HBM] * (fetched is not None),
         out_specs=[VMEM] * len(outs),
-        scratch_shapes=[pltpu.VMEM(s, BF16) for s in scratch],
+        scratch_shapes=[pltpu.VMEM(s, BF16) for s in scratch]
+        + ([] if fetched is None else [pltpu.VMEM(fetched.shape, BF16), pltpu.SemaphoreType.DMA]),
         compiler_params=pltpu.CompilerParams(vmem_limit_bytes=48 * 1024 * 1024),
         cost_estimate=pl.CostEstimate(flops=flops, bytes_accessed=moved, transcendentals=400_000),
         name=name,
-    )(*args)
+    )(*args, *([] if fetched is None else [fetched]))
 
 
 FLAT = (T, 128, C)
@@ -198,7 +207,7 @@
     table = jnp.asarray(spread(), BF16)
     y0, core = lax.axis_index("y0"), lax.axis_index("core")
 
-    msg, gate, flat = call(first_kernel, [MSG, FLAT, FLAT], (pair_rep, in_weights[0]), "edges")
+    msg, gate, flat = call(first_kernel, [MSG, FLAT, FLAT], (pair_rep, in_weights), "edges")
     msg = lax.all_to_all(msg, GROUP, 0, 0, tiled=True)
     right = msg[:, 8:]
     far = lax.ppermute(right, "y0", SWAP)
@@ -207,25 +216,26 @@
     (product,) = call(
         outgoing_kernel,
         [(16, 64, 128)],
-        (y0[None].astype(jnp.int32), msg.reshape(16, 128, 128), near, far, table, jnp.asarray(gather_rows(), BF16)),
-        "outgoing", scratch=[(192, 1024), (2, 384, 1024)], scalars=1,
+        (y0[None].astype(jnp.int32), msg.reshape(16, 128, 128), near, far, table),
+        "outgoing", scratch=[(192, 1024), (2, 384, 1024)], scalars=1, fetched=jnp.asarray(gather_rows(), BF16),
     )
     product = lax.all_to_all(product.reshape(128, 8, 128), GROUP, 0, 0, tiled=True)
     msg, gate, flat = call(
-        middle_kernel, [MSG, FLAT, FLAT], (product, flat, gate, out_weights[0], in_weights[1]), "update_edges"
+        middle_kernel, [MSG, FLAT, FLAT], (product, flat, gate, out_weights, in_weights), "update_edges"
     )
     msg = lax.all_to_all(msg, GROUP, 0, 0, tiled=True)
-    both = lax.all_gather(msg, "core", axis=0).reshape(2, 16, 128, 128)
+    left = lax.all_gather(msg[:, :8], "core", axis=0).reshape(2, 16, 64, 128)
+    right = lax.all_gather(msg[:, 8:], "core", axis=0).reshape(2, 16, 64, 128)
     near, far = call(
         incoming_kernel,
         [(16, 64, 128)] * 2,
-        (jnp.stack([y0, core]).astype(jnp.int32), both, table, jnp.asarray(spread_rows(), BF16), jnp.asarray(spread().T, BF16)),
-        "incoming", scratch=[(2, 384, 256), (384, 1024)], scalars=1,
+        (jnp.stack([y0, core]).astype(jnp.int32), left, right, table, jnp.asarray(spread_rows(), BF16)),
+        "incoming", scratch=[(2, 384, 256), (384, 1024)], scalars=1, fetched=jnp.asarray(spread().T, BF16),
     )
     far = lax.ppermute(far, "y0", SWAP)
     product = (near.astype(F32) + far.astype(F32)).astype(BF16)
     product = lax.all_to_all(product.reshape(128, 8, 128), GROUP, 0, 0, tiled=True)
-    (out,) = call(last_kernel, [(ROWS, COLS, C)], (product, flat, gate, out_weights[1]), "update")
+    (out,) = call(last_kernel, [(ROWS, COLS, C)], (product, flat, gate, out_weights), "update")
     return out
 
 

time: 232 us -> 200 us (0.86)
  blocking collectives: 142 us -> 126 us
  between operations: 13.5 us -> 0.09 us
  starting transfers between devices: 14.8 us -> 12.3 us
    all_to_all x2 -> x1, blocking collectives: 96.2 us -> 55.5 us  [shards(): msg = lax.all_to_all(msg, GROUP, 0, 0, tiled=True)]
    all_to_all x1 -> x2, blocking collectives: 41.5 us -> 61.9 us  [shards(): lax.all_to_all(product.reshape(128, 8, 128), GROUP, 0, 0, tiled=True)]
    all_to_all x1, waiting for transfers between devices: 23.4 us -> 33.5 us  [shards(): msg = lax.all_to_all(msg, GROUP, 0, 0, tiled=True)]
    all_gather x1 -> x0, waiting for transfers between devices: 9.49 us -> none  [shards(): both = lax.all_gather(msg, 'core', axis=0).reshape(2, 16, 128, 128)]
    all_gather x0 -> x2, blocking collectives: none -> 4.53 us  [the longest x1 2.35 us: shards(): left = lax.all_gather(msg[:, :8], 'core', axis=0).reshape(2, 16, 64, 128)]
  transfers between devices with their start and end apart: 4 -> 3, of which waited for: 4 -> 3; matrix products, arithmetic and copies ran while one was open for 0% -> 0% of each run, Pallas kernels for 0% -> 0%
where the time goes in v1:
time: 200 us
  blocking collectives  126 us (63%)
  waiting for transfers between devices  44.6 us (22%)
  Pallas kernels  12.7 us (6%)
  starting transfers between devices  12.3 us (6%)
  local copies, waits for them, and re-layouts  3.73 us (2%)
    all_to_all x2, blocking collectives, shards(): lax.all_to_all(product.reshape(128, 8, 128), GROUP, 0, 0, tiled=True)  61.9 us
    all_to_all x1, blocking collectives, shards(): msg = lax.all_to_all(msg, GROUP, 0, 0, tiled=True)  55.5 us
    all_to_all x1, waiting for transfers between devices, shards(): msg = lax.all_to_all(msg, GROUP, 0, 0, tiled=True)  33.5 us
    pallas_call x5, Pallas kernels, call(): pl.pallas_call(kernel, out_shape=[jax.ShapeDtypeStruct(s, BF16) for s in...  12.7 us
    ppermute x1, waiting for transfers between devices, shards(): far = lax.ppermute(far, 'y0', SWAP)  7.64 us
    all_to_all x1, starting transfers between devices, shards(): msg = lax.all_to_all(msg, GROUP, 0, 0, tiled=True)  7.13 us
  transfers between devices with their start and end apart: 3, of which 3 were waited for; matrix products, arithmetic and copies ran while one was open for 0% of the time, Pallas kernels for 0%

profile of v1, /device:TPU:32, one launch (start us, length us, event | category | flops | bytes accessed | tf_op | source)
XLA Modules:
  0.0 199.9 jit_solution(291783861300904607)
XLA Ops:
  0.0 0.0 copy-start
  0.0 0.0 copy-start.4
  0.0 1.0 copy-done.4
  1.0 0.0 copy-start.7
  1.1 0.9 copy-done.7
  2.0 1.2 edges.1
  3.2 55.5 %all_to_all.20 = bf16[128,16,128]{2,1,0:T(8,128)(2,1)S(1)} all-to-all(bf16[128,16,128]{2,1,0:T(8,128)(2,1)S(1)} %get-tuple-element.13), channel_id=1, replica_groups=mesh['y1'=2,'y0'=2,'zh'=4,'core'=2,'zl'=4,'x'=4] {'zl','x','y1','zh'}, dimensions={0} | all-to-all | bytes 1048576 | tf_op jit(solution)/shard_map/all_to_all | solution.py:211
  58.8 2.6 %collective-permute-start = (bf16[128,8,128]{2,1,0:T(8,128)(2,1)S(1)}, bf16[128,8,128]{2,1,0:T(8,128)(2,1)S(1)}, u32[]{:S(2)}, u32[]{:S(2)}) collective-permute-start(bf16[128,8,128]{2,1,0:T(8,128)(2,1)S(1)} %slice.12), channel_id=1, source_target_pairs={{0,128},{128,0},{1,129},{129,1},{2,130},{130,2},{3,131},{131,3},{4... | collective-permute-start | bytes 786440 | tf_op jit(solution)/shard_map/ppermute | solution.py:213
  61.4 2.2 %all-gather = bf16[256,8,128]{2,1,0:T(8,128)(2,1)S(1)} all-gather(bf16[128,8,128]{2,1,0:T(8,128)(2,1)S(1)} %slice.12), channel_id=2, replica_groups=mesh['y1'=2,'y0'=2,'zh'=4,'core'=2,'zl'=4,'x'=4] {'core'}, dimensions={0}, use_global_device_ids=true | all-gather | bytes 786432 | tf_op jit(solution)/shard_map/all_gather | solution.py:214
  63.5 3.5 %collective-permute-done = bf16[128,8,128]{2,1,0:T(8,128)(2,1)S(1)} collective-permute-done((bf16[128,8,128]{2,1,0:T(8,128)(2,1)S(1)}, bf16[128,8,128]{2,1,0:T(8,128)(2,1)S(1)}, u32[]{:S(2)}, u32[]{:S(2)}) %collective-permute-start) | collective-permute-done | bytes 262176 | tf_op jit(solution)/shard_map/ppermute | solution.py:213
  67.0 2.2 %all-gather.1 = bf16[256,8,128]{2,1,0:T(8,128)(2,1)S(1)} all-gather(bf16[128,8,128]{2,1,0:T(8,128)(2,1)S(1)} %collective-permute-done), channel_id=3, replica_groups=mesh['y1'=2,'y0'=2,'zh'=4,'core'=2,'zl'=4,'x'=4] {'core'}, dimensions={0}, use_global_device_ids=true | all-gather | bytes 786432 | tf_op jit(solution)/shard_map/all_gather | solution.py:215
  69.2 0.0 copy-done
  69.2 0.0 copy-start.1
  69.2 1.7 copy-done.1
  70.9 0.0 copy-start.5
  70.9 0.0 copy-start.6
  70.9 4.6 %outgoing.1 = bf16[16,64,128]{2,1,0:T(8,128)(2,1)S(1)} custom-call(s32[1]{0:T(128)} %bitcast.y0_ref, bf16[16,128,128]{2,1,0:T(8,128)(2,1)S(1)} %bitcast.9, bf16[2,16,64,128]{3,2,1,0:T(8,128)(2,1)S(1)} %bitcast.10, bf16[2,16,64,128]{3,2,1,0:T(8,128)(2,1)S(1)} %bitcast.11, bf16[512,768]{1,0:T(8,128)(2,1)S(1)} %copy-done, bf16[1152,1024]{1,0:T(8,128)(2,1)S(1)} %copy-done.1), custom_call_target="tpu_custom_call" | custom-call | flops 200000000 | bytes 2621444 | tf_op jit(solution)/shard_map/outgoing/pallas_call | solution.py:189
  75.5 31.9 %all_to_all.21.x_ref = bf16[128,8,128]{2,1,0:T(8,128)(2,1)S(1)} all-to-all(bf16[128,8,128]{2,1,0:T(8,128)(2,1)S(1)} %bitcast.14), channel_id=1, replica_groups=mesh['y1'=2,'y0'=2,'zh'=4,'core'=2,'zl'=4,'x'=4] {'zl','x','y1','zh'}, dimensions={0} | all-to-all | bytes 524288 | tf_op jit(solution)/shard_map/all_to_all | solution.py:222
  107.4 0.0 copy-done.5
  107.4 0.0 copy-done.6
  107.4 0.0 copy-start.2
  107.4 0.0 copy-start.3
  107.4 2.2 %update_edges.1 = (bf16[128,16,128]{2,1,0:T(8,128)(2,1)}, bf16[7,128,128]{2,1,0:T(8,128)(2,1)S(1)}, bf16[7,128,128]{2,1,0:T(8,128)(2,1)S(1)}) custom-call(bf16[128,8,128]{2,1,0:T(8,128)(2,1)S(1)} %all_to_all.21.x_ref, bf16[7,128,128]{2,1,0:T(8,128)(2,1)S(1)} %get-tuple-element.14.p_ref, bf16[7,128,128]{2,1,0:T(8,128)(2,1)S(1)} %get-tuple-element.15.gate_ref, ...), custom_call_target="tpu_custom_call" | custom-call | flops 200000000 | bytes 2097152 | tf_op jit(solution)/shard_map/update_edges/pallas_call | solution.py:189
  109.6 7.1 %all-to-all-start.2 = ((bf16[128,16,128]{2,1,0:T(8,128)(2,1)}), bf16[128,16,128]{2,1,0:T(8,128)(2,1)S(1)}, u32[]{:S(2)}, u32[]{:S(2)}) async-start(bf16[128,16,128]{2,1,0:T(8,128)(2,1)} %get-tuple-element.16), calls=%async_computation.2 | async-start | bytes 1048576 | tf_op jit(solution)/shard_map/all_to_all | solution.py:226
  116.8 0.1 pad_add_fusion.at_ref
  116.8 33.5 %all-to-all-done.2 = bf16[128,16,128]{2,1,0:T(8,128)(2,1)S(1)} async-done(((bf16[128,16,128]{2,1,0:T(8,128)(2,1)}), bf16[128,16,128]{2,1,0:T(8,128)(2,1)S(1)}, u32[]{:S(2)}, u32[]{:S(2)}) %all-to-all-start.2) | async-done | bytes 524320 | tf_op jit(solution)/shard_map/all_to_all | solution.py:226
  150.4 2.2 %all-gather.3 = bf16[256,8,128]{2,1,0:T(8,128)(2,1)S(1)} all-gather(bf16[128,8,128]{2,1,0:T(8,128)(2,1)S(1)} %get-tuple-element.21), channel_id=5, replica_groups=mesh['y1'=2,'y0'=2,'zh'=4,'core'=2,'zl'=4,'x'=4] {'core'}, dimensions={0}, use_global_device_ids=true | all-gather | bytes 786432 | tf_op jit(solution)/shard_map/all_gather | solution.py:228
  152.6 2.3 %all-gather.2 = bf16[256,8,128]{2,1,0:T(8,128)(2,1)S(1)} all-gather(bf16[128,8,128]{2,1,0:T(8,128)(2,1)S(1)} %get-tuple-element.22), channel_id=4, replica_groups=mesh['y1'=2,'y0'=2,'zh'=4,'core'=2,'zl'=4,'x'=4] {'core'}, dimensions={0}, use_global_device_ids=true | all-gather | bytes 786432 | tf_op jit(solution)/shard_map/all_gather | solution.py:227
  154.9 0.0 copy-done.2
  154.9 0.0 copy-done.3
  154.9 3.5 %incoming.1 = (bf16[16,64,128]{2,1,0:T(8,128)(2,1)S(1)}, bf16[16,64,128]{2,1,0:T(8,128)(2,1)S(1)}) custom-call(s32[2]{0:T(128)S(1)} %pad_add_fusion.at_ref, bf16[2,16,64,128]{3,2,1,0:T(8,128)(2,1)S(1)} %bitcast.13, bf16[2,16,64,128]{3,2,1,0:T(8,128)(2,1)S(1)} %bitcast.12, bf16[512,768]{1,0:T(8,128)(2,1)S(1)} %copy-done, bf16[2,512,384]{2,1,0:T(8,128)(2,1)S(1)} %copy-done.3, ...), custom_call_target="tpu_custom_call" | custom-call | flops 200000000 | bytes 3145736 | tf_op jit(solution)/shard_map/incoming/pallas_call | solution.py:189
  158.4 2.6 %collective-permute-start.1 = (bf16[16,64,128]{2,1,0:T(8,128)(2,1)S(1)}, bf16[16,64,128]{2,1,0:T(8,128)(2,1)S(1)}, u32[]{:S(2)}, u32[]{:S(2)}) collective-permute-start(bf16[16,64,128]{2,1,0:T(8,128)(2,1)S(1)} %get-tuple-element.18), channel_id=1, source_target_pairs={{0,128},{128,0},{1,129},{129,1},{2,130},{130,2},{3,131},{131,3},{4... | collective-permute-start | bytes 786440 | tf_op jit(solution)/shard_map/ppermute | solution.py:235
  161.0 7.6 %collective-permute-done.1 = bf16[16,64,128]{2,1,0:T(8,128)(2,1)S(1)} collective-permute-done((bf16[16,64,128]{2,1,0:T(8,128)(2,1)S(1)}, bf16[16,64,128]{2,1,0:T(8,128)(2,1)S(1)}, u32[]{:S(2)}, u32[]{:S(2)}) %collective-permute-start.1) | collective-permute-done | bytes 262176 | tf_op jit(solution)/shard_map/ppermute | solution.py:235
  168.7 0.1 add_convert_fusion
  168.8 30.0 %all_to_all.22.x_ref = bf16[128,8,128]{2,1,0:T(8,128)(2,1)S(1)} all-to-all(bf16[128,8,128]{2,1,0:T(8,128)(2,1)S(1)} %bitcast.15), channel_id=1, replica_groups=mesh['y1'=2,'y0'=2,'zh'=4,'core'=2,'zl'=4,'x'=4] {'zl','x','y1','zh'}, dimensions={0} | all-to-all | bytes 524288 | tf_op jit(solution)/shard_map/all_to_all | solution.py:237
  198.7 1.2 update.1
  (2 shorter events, 0.1 us)
Async XLA Ops:
  0.0 69.2 %copy-start = (bf16[512,768]{1,0:T(8,128)(2,1)S(1)}, bf16[512,768]{1,0:T(8,128)(2,1)}, u32[]{:S(2)}) copy-start(bf16[512,768]{1,0:T(8,128)(2,1)} %constant.18.clone.spread_ref) | copy-start | bytes 2359300
  0.0 1.0 copy-start.4
  1.0 0.9 copy-start.7
  58.8 8.3 %collective-permute-start = (bf16[128,8,128]{2,1,0:T(8,128)(2,1)S(1)}, bf16[128,8,128]{2,1,0:T(8,128)(2,1)S(1)}, u32[]{:S(2)}, u32[]{:S(2)}) collective-permute-start(bf16[128,8,128]{2,1,0:T(8,128)(2,1)S(1)} %slice.12), channel_id=1, source_target_pairs={{0,128},{128,0},{1,129},{129,1},{2,130},{130,2},{3,131},{131,3},{4... | collective-permute-start | bytes 786440 | tf_op jit(solution)/shard_map/ppermute | solution.py:213
  69.2 1.7 copy-start.1
  70.9 36.5 %copy-start.5 = (bf16[2,128,640]{2,1,0:T(8,128)(2,1)S(1)}, bf16[2,128,640]{2,1,0:T(8,128)(2,1)}, u32[]{:S(2)}) copy-start(bf16[2,128,640]{2,1,0:T(8,128)(2,1)} %w_ref.3) | copy-start | bytes 983044
  70.9 36.5 %copy-start.6 = (bf16[2,128,128]{2,1,0:T(8,128)(2,1)S(1)}, bf16[2,128,128]{2,1,0:T(8,128)(2,1)}, u32[]{:S(2)}) copy-start(bf16[2,128,128]{2,1,0:T(8,128)(2,1)} %wo_ref.3) | copy-start | bytes 196612
  107.4 47.5 %copy-start.2 = (bf16[768,512]{1,0:T(8,128)(2,1)S(1)}, bf16[768,512]{1,0:T(8,128)(2,1)}, u32[]{:S(2)}) copy-start(bf16[768,512]{1,0:T(8,128)(2,1)} %constant.21.clone.gather_hbm) | copy-start | bytes 2359300
  107.4 47.5 %copy-start.3 = (bf16[2,512,384]{2,1,0:T(8,128)(2,1)S(1)}, bf16[2,512,384]{2,1,0:T(8,128)(2,1)}, u32[]{:S(2)}) copy-start(bf16[2,512,384]{2,1,0:T(8,128)(2,1)} %constant.20.clone.rows_ref) | copy-start | bytes 2359300
  109.6 40.7 %all-to-all-start.2 = ((bf16[128,16,128]{2,1,0:T(8,128)(2,1)}), bf16[128,16,128]{2,1,0:T(8,128)(2,1)S(1)}, u32[]{:S(2)}, u32[]{:S(2)}) async-start(bf16[128,16,128]{2,1,0:T(8,128)(2,1)} %get-tuple-element.16), calls=%async_computation.2 | async-start | bytes 1048576 | tf_op jit(solution)/shard_map/all_to_all | solution.py:226
  158.4 10.2 %collective-permute-start.1 = (bf16[16,64,128]{2,1,0:T(8,128)(2,1)S(1)}, bf16[16,64,128]{2,1,0:T(8,128)(2,1)S(1)}, u32[]{:S(2)}, u32[]{:S(2)}) collective-permute-start(bf16[16,64,128]{2,1,0:T(8,128)(2,1)S(1)} %get-tuple-element.18), channel_id=1, source_target_pairs={{0,128},{128,0},{1,129},{129,1},{2,130},{130,2},{3,131},{131,3},{4... | collective-permute-start | bytes 786440 | tf_op jit(solution)/shard_map/ppermute | solution.py:235

commit v2 on v1

v2 whole, which is shorter than its diff:
```python
import functools

import jax
import jax.numpy as jnp
import numpy as np
from jax import lax
from jax.experimental import pallas as pl
from jax.experimental.pallas import tpu as pltpu
from jax.sharding import Mesh, PartitionSpec as P

PARTS = (("y1", 2), ("y0", 2), ("zh", 4), ("core", 2), ("zl", 4), ("x", 4))
ROW = ("y1", "y0", "zh", "core")
CHAN = ("zl", "x")
GROUP = ("zl", "x", "y1", "zh")
SWAP = [(0, 1), (1, 0)]
ROWS, COLS, C = 21, 42, 128
T, U = 7, 3
F32, BF16 = jnp.float32, jnp.bfloat16


def spread():
    table = np.zeros((2, 128, U, 128), np.float32)
    for x in range(2):
        for u in range(U):
            for q in range(COLS):
                table[x, COLS * u + q, u, COLS * x + q] = 1
    return table.reshape(256, U * 128)


def spread_rows():
    table = np.zeros((2, 4, 128, U, 128), np.float32)
    for core in range(2):
        for x in range(4):
            for u in range(U):
                for t in range(T):
                    for w in range(U):
                        table[core, x, COLS * u + ROWS * core + U * t + w, u, 32 * w + 8 * x + t] = 1
    return table.reshape(2, 512, U * 128)


def gather_rows():
    table = np.zeros((U, 128, 2, 128), np.float32)
    for u in range(U):
        for core in range(2):
            for v in range(U):
                for s in range(2):
                    for t in range(T):
                        table[u, 48 * core + 16 * v + 8 * s + t, s, COLS * u + ROWS * core + U * t + v] = 1
    return table.reshape(U * 128, 256)


def dot(a, b, on_a, on_b):
    return lax.dot_general(a, b, (((on_a,), (on_b,)), ((), ())), preferred_element_type=F32)


def layer_norm(values, axis_index):
    average = jnp.mean(values, axis=axis_index, keepdims=True)
    centred = values - average
    variance = jnp.mean(centred * centred, axis=axis_index, keepdims=True)
    return centred * lax.rsqrt(variance + 1e-05)


def emit_edges(blocks, w_ref, step, msg_ref, gate_ref):
    lefts, rights = [], []
    for t in range(T):
        normed = layer_norm(blocks[t], 1).astype(BF16)
        projected = dot(w_ref[step, :, : 4 * C], normed, 0, 1)
        lefts.append(jax.nn.sigmoid(projected[C : 2 * C]) * projected[:C])
        rights.append(jax.nn.sigmoid(projected[3 * C : 4 * C]) * projected[2 * C : 3 * C])
        gate_ref[t] = jax.nn.sigmoid(dot(normed, w_ref[step, :, 4 * C :], 1, 0)).astype(BF16)
    none = jnp.zeros((C, 128), F32)
    both = jnp.stack(lefts + [none] + rights + [none], axis=0)
    msg_ref[...] = jnp.swapaxes(both, 0, 1).astype(BF16)


def updated(x_ref, p_ref, gate_ref, w_ref, step):
    product = jnp.swapaxes(x_ref[...].astype(F32), 0, 1)
    blocks = []
    for t in range(T):
        normed = layer_norm(product[t], 0).astype(BF16)
        outward = dot(normed, w_ref[step], 0, 0)
        blocks.append((p_ref[t].astype(F32) + gate_ref[t].astype(F32) * outward).astype(BF16))
    return blocks


def first_kernel(p_ref, w_ref, msg_ref, gate_ref, flat_ref):
    blocks = []
    for t in range(T):
        rows = [p_ref[U * t + u].astype(F32) for u in range(U)]
        block = jnp.concatenate(rows + [jnp.zeros((2, C), F32)], axis=0)
        flat_ref[t] = block.astype(BF16)
        blocks.append(block)
    emit_edges(blocks, w_ref, 0, msg_ref, gate_ref)


def middle_kernel(x_ref, p_ref, gate_ref, wo_ref, w_ref, msg_ref, gate_next_ref, flat_ref):
    blocks = updated(x_ref, p_ref, gate_ref, wo_ref, 0)
    for t in range(T):
        flat_ref[t] = blocks[t]
    emit_edges([block.astype(F32) for block in blocks], w_ref, 1, msg_ref, gate_next_ref)


def last_kernel(x_ref, p_ref, gate_ref, wo_ref, out_ref):
    blocks = updated(x_ref, p_ref, gate_ref, wo_ref, 1)
    for t in range(T):
        block = blocks[t].astype(F32)
        for u in range(U):
            out_ref[U * t + u] = block[COLS * u : COLS * (u + 1)].astype(BF16)


def fan(get, count, table):
    wide = [jnp.concatenate([get(count * at + x) for x in range(count)], axis=1) for at in range(16 // count)]
    return dot(jnp.concatenate(wide, axis=0), table, 1, 0)


def fill_right(right, core, get, table):
    part = fan(get, 2, table).astype(BF16)
    for pair in range(8):
        for v in range(U):
            for high in range(4):
                rows = 64 * pair + 16 * high
                at = 128 * high + 48 * core + 16 * v
                right[at : at + 16, 128 * pair : 128 * (pair + 1)] = part[rows : rows + 16, 128 * v : 128 * (v + 1)]


def outgoing_products(left, right, gather_ref):
    product = dot(left[...], right[...], 1, 1).astype(BF16)
    wide = [
        jnp.concatenate([product[64 * u : 64 * (u + 1), 128 * high : 128 * (high + 1)] for u in range(U)], axis=1)
        for high in range(4)
    ]
    return dot(jnp.concatenate(wide, axis=0), gather_ref[...], 1, 0).astype(BF16)


def outgoing_near_kernel(msg_ref, near_ref, spread_ref, gather_ref, left, out_ref, right):
    table = spread_ref[...]
    part = fan(lambda at: msg_ref[at], 2, table).reshape(64, 2, 8, U * 128)[:, 0].reshape(512, U * 128).astype(BF16)
    for pair in range(8):
        for u in range(U):
            left[64 * u : 64 * (u + 1), 128 * pair : 128 * (pair + 1)] = part[
                64 * pair : 64 * (pair + 1), 128 * u : 128 * (u + 1)
            ]
    for high in range(4):
        right[128 * high + 96 : 128 * (high + 1)] = jnp.zeros((32, 1024), BF16)
    for core in range(2):
        fill_right(right, core, lambda m, core=core: near_ref[core, m], table)
    packed = outgoing_products(left, right, gather_ref)
    for s in range(8):
        high, low = divmod(s, 2)
        out_ref[s] = packed[64 * high : 64 * (high + 1), 128 * low : 128 * (low + 1)]


def outgoing_far_kernel(y0_ref, left, near_ref, far_ref, spread_ref, gather_ref, out_ref, right):
    y0 = y0_ref[0]
    table = spread_ref[...]
    for high in range(4):
        right[128 * high + 96 : 128 * (high + 1)] = jnp.zeros((32, 1024), BF16)
    for core in range(2):
        fill_right(right, core, lambda m, core=core: far_ref[core, m], table)
    packed = outgoing_products(left, right, gather_ref)
    for s in range(8):
        high, low = divmod(s, 2)
        y1, zh = divmod(s, 4)
        out_ref[(2 * y1 + y0) * 4 + zh] = near_ref[s]
        out_ref[(2 * y1 + 1 - y0) * 4 + zh] = packed[64 * high : 64 * (high + 1), 128 * low : 128 * (low + 1)]


def incoming_products(left, right, gather_ref, out_ref):
    product = dot(left, right, 0, 0).astype(BF16)
    wide = []
    for pair in range(8):
        for y1 in range(2):
            part = [
                product[128 * y1 + 32 * w : 128 * y1 + 32 * (w + 1), 128 * pair : 128 * (pair + 1)] for w in range(U)
            ]
            wide.append(jnp.concatenate(part, axis=1))
    packed = dot(jnp.concatenate(wide, axis=0), gather_ref[...], 1, 0).astype(BF16)
    for pair in range(8):
        for x in range(2):
            out_ref[2 * pair + x] = packed[64 * pair : 64 * (pair + 1), 128 * x : 128 * (x + 1)]


def incoming_far_kernel(
    at_ref, left_ref, right_ref, spread_ref, rows_ref, gather_ref, far_ref, left_near, right, left
):
    y0, mine = at_ref[0], at_ref[1]
    table, rows = spread_ref[...], rows_ref[mine]
    for core in range(2):
        lefts = fan(lambda m: left_ref[core, m], 4, rows).astype(BF16)
        rights = fan(lambda m: right_ref[core, m], 2, table).astype(BF16)
        for u in range(U):
            at = 192 * core + 64 * u
            for zl in range(4):
                y1, y = divmod(zl, 2)
                left[y, at : at + 64, 128 * y1 : 128 * (y1 + 1)] = lefts[64 * zl : 64 * (zl + 1), 128 * u : 128 * (u + 1)]
            for pair in range(8):
                right[at : at + 64, 128 * pair : 128 * (pair + 1)] = rights[
                    64 * pair : 64 * (pair + 1), 128 * u : 128 * (u + 1)
                ]
    left_near[...] = left[y0]
    incoming_products(left[1 - y0], right[...], gather_ref, far_ref)


def incoming_near_kernel(left, right, gather_ref, near_ref):
    incoming_products(left[...], right[...], gather_ref, near_ref)


VMEM = pl.BlockSpec(memory_space=pltpu.VMEM)
SMEM = pl.BlockSpec(memory_space=pltpu.SMEM)


def call(kernel, outs, args, name, scratch=(), scalars=0):
    moved = sum(a.size * a.dtype.itemsize for a in args) + sum(2 * int(np.prod(s)) for s in outs)
    return pl.pallas_call(
        kernel,
        out_shape=[jax.ShapeDtypeStruct(s, BF16) for s in outs],
        in_specs=[SMEM] * scalars + [VMEM] * (len(args) - scalars),
        out_specs=[VMEM] * len(outs),
        scratch_shapes=[pltpu.VMEM(s, BF16) for s in scratch],
        compiler_params=pltpu.CompilerParams(vmem_limit_bytes=48 * 1024 * 1024),
        cost_estimate=pl.CostEstimate(flops=2_000_000_000, bytes_accessed=moved, transcendentals=0),
        name=name,
    )(*args)


FLAT = (T, 128, C)
MSG = (C, 16, 128)


def shards(pair_rep, in_weights, out_weights):
    table, back = jnp.asarray(spread(), BF16), jnp.asarray(spread().T, BF16)
    gather = jnp.asarray(gather_rows(), BF16)
    y0, core = lax.axis_index("y0").astype(jnp.int32), lax.axis_index("core").astype(jnp.int32)

    msg, gate, flat = call(first_kernel, [MSG, FLAT, FLAT], (pair_rep, in_weights), "edges")
    msg = lax.all_to_all(msg, GROUP, 0, 0, tiled=True)
    right = msg[:, 8:]
    far = lax.ppermute(right, "y0", SWAP)
    near = lax.all_gather(right, "core", axis=0).reshape(2, 16, 64, 128)
    left, near = call(
        outgoing_near_kernel, [(192, 1024), (8, 64, 128)], (msg.reshape(16, 128, 128), near, table, gather),
        "outgoing_near", scratch=[(512, 1024)],
    )
    far = lax.all_gather(far, "core", axis=0).reshape(2, 16, 64, 128)
    (product,) = call(
        outgoing_far_kernel, [(16, 64, 128)], (y0[None], left, near, far, table, gather),
        "outgoing_far", scratch=[(512, 1024)], scalars=1,
    )
    product = lax.all_to_all(product.reshape(128, 8, 128), GROUP, 0, 0, tiled=True)
    msg, gate, flat = call(
        middle_kernel, [MSG, FLAT, FLAT], (product, flat, gate, out_weights, in_weights), "update_edges"
    )
    msg = lax.all_to_all(msg, GROUP, 0, 0, tiled=True)
    left = lax.all_gather(msg[:, :8], "core", axis=0).reshape(2, 16, 64, 128)
    right = lax.all_gather(msg[:, 8:], "core", axis=0).reshape(2, 16, 64, 128)
    far, left, right = call(
        incoming_far_kernel, [(16, 64, 128), (384, 256), (384, 1024)],
        (jnp.stack([y0, core]), left, right, table, jnp.asarray(spread_rows(), BF16), back),
        "incoming_far", scratch=[(2, 384, 256)], scalars=1,
    )
    far = lax.ppermute(far, "y0", SWAP)
    (near,) = call(incoming_near_kernel, [(16, 64, 128)], (left, right, back), "incoming_near")
    product = (near.astype(F32) + far.astype(F32)).astype(BF16)
    product = lax.all_to_all(product.reshape(128, 8, 128), GROUP, 0, 0, tiled=True)
    (out,) = call(last_kernel, [(ROWS, COLS, C)], (product, flat, gate, out_weights), "update")
    return out


def solution(mesh):
    parts = Mesh(mesh.devices.reshape([size for _, size in PARTS]), [name for name, _ in PARTS])
    spec = P(ROW, CHAN, None)
    return jax.shard_map(shards, mesh=parts, in_specs=(spec, P(), P()), out_specs=spec, check_vma=False)
```

time: 200 us -> 195 us (0.975)
  blocking collectives: 126 us -> 71 us
  waiting for transfers between devices: 44.6 us -> 76.4 us
  starting transfers between devices: 12.3 us -> 34.3 us
  Pallas kernels: 12.7 us -> 10.3 us
    all_to_all x1 -> x0, blocking collectives: 55.5 us -> none  [shards(): msg = lax.all_to_all(msg, GROUP, 0, 0, tiled=True)]
    all_to_all x1 -> x2, waiting for transfers between devices: 33.5 us -> 67.5 us  [shards(): msg = lax.all_to_all(msg, GROUP, 0, 0, tiled=True)]
    all_to_all x1 -> x2, starting transfers between devices: 7.13 us -> 28.9 us  [shards(): msg = lax.all_to_all(msg, GROUP, 0, 0, tiled=True)]
    pallas_call x5 -> x7, Pallas kernels: 12.7 us -> 10.3 us  [call(): pl.pallas_call(kernel, out_shape=[jax.ShapeDtypeStruct(s, BF16) for s in...]
  transfers between devices with their start and end apart: 3 -> 4, of which waited for: 3 -> 4; matrix products, arithmetic and copies ran while one was open for 0% -> 0% of each run, Pallas kernels for 0% -> 1%
where the time goes in v2:
time: 195 us; the launch traced here: 194 us
  waiting for transfers between devices  76.4 us (39%)
  blocking collectives  71 us (36%)
  starting transfers between devices  34.3 us (18%)
  Pallas kernels  10.3 us (5%)
  local copies, waits for them, and re-layouts  2.01 us (1%)
    all_to_all x2, waiting for transfers between devices, shards(): msg = lax.all_to_all(msg, GROUP, 0, 0, tiled=True)  67.5 us
    all_to_all x2, blocking collectives, shards(): lax.all_to_all(product.reshape(128, 8, 128), GROUP, 0, 0, tiled=True)  62.1 us
    all_to_all x2, starting transfers between devices, shards(): msg = lax.all_to_all(msg, GROUP, 0, 0, tiled=True)  28.9 us
    pallas_call x7, Pallas kernels, call(): pl.pallas_call(kernel, out_shape=[jax.ShapeDtypeStruct(s, BF16) for s in...  10.3 us
    ppermute x1, waiting for transfers between devices, shards(): far = lax.ppermute(far, 'y0', SWAP)  6.83 us
  transfers between devices with their start and end apart: 4, of which 4 were waited for; matrix products, arithmetic and copies ran while one was open for 0% of the time, Pallas kernels for 1%

profile of v2, /device:TPU:32, one launch (start us, length us, event | category | flops | bytes accessed | tf_op | source)
XLA Modules:
  0.0 194.4 jit_solution(8787343802784068858)
XLA Ops:
  0.0 0.0 copy-start
  0.0 1.0 copy-done
  1.0 0.0 copy-start.2
  1.0 0.9 copy-done.2
  1.9 2.0 %edges.1 = (bf16[128,16,128]{2,1,0:T(8,128)(2,1)}, bf16[7,128,128]{2,1,0:T(8,128)(2,1)S(1)}, bf16[7,128,128]{2,1,0:T(8,128)(2,1)S(1)}) custom-call(bf16[21,42,128]{2,1,0:T(8,128)(2,1)S(1)} %copy-done.2, bf16[2,128,640]{2,1,0:T(8,128)(2,1)S(1)} %copy-done), custom_call_target="tpu_custom_call" | custom-call | flops 2000000000 | bytes 1536512 | tf_op jit(solution)/shard_map/edges/pallas_call | solution.py:214
  3.9 21.7 %all-to-all-start = ((bf16[128,16,128]{2,1,0:T(8,128)(2,1)}), bf16[128,16,128]{2,1,0:T(8,128)(2,1)S(1)}, u32[]{:S(2)}, u32[]{:S(2)}) async-start(bf16[128,16,128]{2,1,0:T(8,128)(2,1)} %get-tuple-element.16), calls=%async_computation | async-start | bytes 1048576 | tf_op jit(solution)/shard_map/all_to_all | solution.py:236
  25.6 34.0 %all-to-all-done = bf16[128,16,128]{2,1,0:T(8,128)(2,1)S(1)} async-done(((bf16[128,16,128]{2,1,0:T(8,128)(2,1)}), bf16[128,16,128]{2,1,0:T(8,128)(2,1)S(1)}, u32[]{:S(2)}, u32[]{:S(2)}) %all-to-all-start) | async-done | bytes 524320 | tf_op jit(solution)/shard_map/all_to_all | solution.py:236
  59.7 0.0 copy-start.6
  59.7 0.0 copy-start.7
  59.7 2.7 %collective-permute-start = (bf16[128,8,128]{2,1,0:T(8,128)(2,1)S(1)}, bf16[128,8,128]{2,1,0:T(8,128)(2,1)S(1)}, u32[]{:S(2)}, u32[]{:S(2)}) collective-permute-start(bf16[128,8,128]{2,1,0:T(8,128)(2,1)S(1)} %slice.12), channel_id=1, source_target_pairs={{0,128},{128,0},{1,129},{129,1},{2,130},{130,2},{3,131},{131,3},{4... | collective-permute-start | bytes 786440 | tf_op jit(solution)/shard_map/ppermute | solution.py:238
  62.4 2.2 %all-gather = bf16[256,8,128]{2,1,0:T(8,128)(2,1)S(1)} all-gather(bf16[128,8,128]{2,1,0:T(8,128)(2,1)S(1)} %slice.12), channel_id=2, replica_groups=mesh['y1'=2,'y0'=2,'zh'=4,'core'=2,'zl'=4,'x'=4] {'core'}, dimensions={0}, use_global_device_ids=true | all-gather | bytes 786432 | tf_op jit(solution)/shard_map/all_gather | solution.py:239
  64.6 0.0 copy-done.6
  64.6 0.0 copy-done.7
  64.6 1.4 outgoing_near.1
  66.0 2.1 %collective-permute-done = bf16[128,8,128]{2,1,0:T(8,128)(2,1)S(1)} collective-permute-done((bf16[128,8,128]{2,1,0:T(8,128)(2,1)S(1)}, bf16[128,8,128]{2,1,0:T(8,128)(2,1)S(1)}, u32[]{:S(2)}, u32[]{:S(2)}) %collective-permute-start) | collective-permute-done | bytes 262176 | tf_op jit(solution)/shard_map/ppermute | solution.py:238
  68.1 2.2 %all-gather.1 = bf16[256,8,128]{2,1,0:T(8,128)(2,1)S(1)} all-gather(bf16[128,8,128]{2,1,0:T(8,128)(2,1)S(1)} %collective-permute-done), channel_id=3, replica_groups=mesh['y1'=2,'y0'=2,'zh'=4,'core'=2,'zl'=4,'x'=4] {'core'}, dimensions={0}, use_global_device_ids=true | all-gather | bytes 786432 | tf_op jit(solution)/shard_map/all_gather | solution.py:244
  70.3 1.1 outgoing_far.1
  71.4 0.0 copy-start.1
  71.4 0.0 copy-start.3
  71.4 32.1 %all_to_all.20.x_ref = bf16[128,8,128]{2,1,0:T(8,128)(2,1)S(1)} all-to-all(bf16[128,8,128]{2,1,0:T(8,128)(2,1)S(1)} %bitcast.14), channel_id=1, replica_groups=mesh['y1'=2,'y0'=2,'zh'=4,'core'=2,'zl'=4,'x'=4] {'zl','x','y1','zh'}, dimensions={0} | all-to-all | bytes 524288 | tf_op jit(solution)/shard_map/all_to_all | solution.py:249
  103.5 0.0 copy-done.1
  103.5 0.0 copy-done.3
  103.5 2.2 %update_edges.1 = (bf16[128,16,128]{2,1,0:T(8,128)(2,1)}, bf16[7,128,128]{2,1,0:T(8,128)(2,1)S(1)}, bf16[7,128,128]{2,1,0:T(8,128)(2,1)S(1)}) custom-call(bf16[128,8,128]{2,1,0:T(8,128)(2,1)S(1)} %all_to_all.20.x_ref, bf16[7,128,128]{2,1,0:T(8,128)(2,1)S(1)} %get-tuple-element.19.p_ref, bf16[7,128,128]{2,1,0:T(8,128)(2,1)S(1)} %get-tuple-element.20.gate_ref, ...), custom_call_target="tpu_custom_call" | custom-call | flops 2000000000 | bytes 2097152 | tf_op jit(solution)/shard_map/update_edges/pallas_call | solution.py:214
  105.7 7.1 %all-to-all-start.2 = ((bf16[128,16,128]{2,1,0:T(8,128)(2,1)}), bf16[128,16,128]{2,1,0:T(8,128)(2,1)S(1)}, u32[]{:S(2)}, u32[]{:S(2)}) async-start(bf16[128,16,128]{2,1,0:T(8,128)(2,1)} %get-tuple-element.21), calls=%async_computation.2 | async-start | bytes 1048576 | tf_op jit(solution)/shard_map/all_to_all | solution.py:253
  112.9 0.1 pad_add_fusion.at_ref
  112.9 33.5 %all-to-all-done.2 = bf16[128,16,128]{2,1,0:T(8,128)(2,1)S(1)} async-done(((bf16[128,16,128]{2,1,0:T(8,128)(2,1)}), bf16[128,16,128]{2,1,0:T(8,128)(2,1)S(1)}, u32[]{:S(2)}, u32[]{:S(2)}) %all-to-all-start.2) | async-done | bytes 524320 | tf_op jit(solution)/shard_map/all_to_all | solution.py:253
  146.5 0.0 copy-start.4
  146.5 2.3 %all-gather.3 = bf16[256,8,128]{2,1,0:T(8,128)(2,1)S(1)} all-gather(bf16[128,8,128]{2,1,0:T(8,128)(2,1)S(1)} %get-tuple-element.27), channel_id=5, replica_groups=mesh['y1'=2,'y0'=2,'zh'=4,'core'=2,'zl'=4,'x'=4] {'core'}, dimensions={0}, use_global_device_ids=true | all-gather | bytes 786432 | tf_op jit(solution)/shard_map/all_gather | solution.py:255
  148.8 0.0 copy-start.5
  148.8 2.3 %all-gather.2 = bf16[256,8,128]{2,1,0:T(8,128)(2,1)S(1)} all-gather(bf16[128,8,128]{2,1,0:T(8,128)(2,1)S(1)} %get-tuple-element.28), channel_id=4, replica_groups=mesh['y1'=2,'y0'=2,'zh'=4,'core'=2,'zl'=4,'x'=4] {'core'}, dimensions={0}, use_global_device_ids=true | all-gather | bytes 786432 | tf_op jit(solution)/shard_map/all_gather | solution.py:254
  151.1 0.0 copy-done.4
  151.1 0.0 copy-done.5
  151.1 1.8 incoming_far.1
  152.9 2.8 %collective-permute-start.1 = (bf16[16,64,128]{2,1,0:T(8,128)(2,1)S(1)}, bf16[16,64,128]{2,1,0:T(8,128)(2,1)S(1)}, u32[]{:S(2)}, u32[]{:S(2)}) collective-permute-start(bf16[16,64,128]{2,1,0:T(8,128)(2,1)S(1)} %get-tuple-element.24), channel_id=1, source_target_pairs={{0,128},{128,0},{1,129},{129,1},{2,130},{130,2},{3,131},{131,3},{4... | collective-permute-start | bytes 786440 | tf_op jit(solution)/shard_map/ppermute | solution.py:261
  155.7 0.6 incoming_near.1
  156.3 6.8 %collective-permute-done.1 = bf16[16,64,128]{2,1,0:T(8,128)(2,1)S(1)} collective-permute-done((bf16[16,64,128]{2,1,0:T(8,128)(2,1)S(1)}, bf16[16,64,128]{2,1,0:T(8,128)(2,1)S(1)}, u32[]{:S(2)}, u32[]{:S(2)}) %collective-permute-start.1) | collective-permute-done | bytes 262176 | tf_op jit(solution)/shard_map/ppermute | solution.py:261
  163.2 0.1 add_convert_fusion
  163.2 30.0 %all_to_all.21.x_ref = bf16[128,8,128]{2,1,0:T(8,128)(2,1)S(1)} all-to-all(bf16[128,8,128]{2,1,0:T(8,128)(2,1)S(1)} %bitcast.15), channel_id=1, replica_groups=mesh['y1'=2,'y0'=2,'zh'=4,'core'=2,'zl'=4,'x'=4] {'zl','x','y1','zh'}, dimensions={0} | all-to-all | bytes 524288 | tf_op jit(solution)/shard_map/all_to_all | solution.py:264
  193.2 1.2 update.1
  (2 shorter events, 0.1 us)
Async XLA Ops:
  0.0 1.0 copy-start
  1.0 0.9 copy-start.2
  3.9 55.7 %all-to-all-start = ((bf16[128,16,128]{2,1,0:T(8,128)(2,1)}), bf16[128,16,128]{2,1,0:T(8,128)(2,1)S(1)}, u32[]{:S(2)}, u32[]{:S(2)}) async-start(bf16[128,16,128]{2,1,0:T(8,128)(2,1)} %get-tuple-element.16), calls=%async_computation | async-start | bytes 1048576 | tf_op jit(solution)/shard_map/all_to_all | solution.py:236
  59.7 4.9 %copy-start.6 = (bf16[256,384]{1,0:T(8,128)(2,1)S(1)}, bf16[256,384]{1,0:T(8,128)(2,1)}, u32[]{:S(2)}) copy-start(bf16[256,384]{1,0:T(8,128)(2,1)} %constant.18.clone.spread_ref) | copy-start | bytes 589828
  59.7 4.9 %copy-start.7 = (bf16[384,256]{1,0:T(8,128)(2,1)S(1)}, bf16[384,256]{1,0:T(8,128)(2,1)}, u32[]{:S(2)}) copy-start(bf16[384,256]{1,0:T(8,128)(2,1)} %constant.20.clone.gather_ref) | copy-start | bytes 589828
  59.7 8.4 %collective-permute-start = (bf16[128,8,128]{2,1,0:T(8,128)(2,1)S(1)}, bf16[128,8,128]{2,1,0:T(8,128)(2,1)S(1)}, u32[]{:S(2)}, u32[]{:S(2)}) collective-permute-start(bf16[128,8,128]{2,1,0:T(8,128)(2,1)S(1)} %slice.12), channel_id=1, source_target_pairs={{0,128},{128,0},{1,129},{129,1},{2,130},{130,2},{3,131},{131,3},{4... | collective-permute-start | bytes 786440 | tf_op jit(solution)/shard_map/ppermute | solution.py:238
  71.4 32.1 %copy-start.1 = (bf16[2,128,640]{2,1,0:T(8,128)(2,1)S(1)}, bf16[2,128,640]{2,1,0:T(8,128)(2,1)}, u32[]{:S(2)}) copy-start(bf16[2,128,640]{2,1,0:T(8,128)(2,1)} %w_ref.3) | copy-start | bytes 983044
  71.4 32.1 %copy-start.3 = (bf16[2,128,128]{2,1,0:T(8,128)(2,1)S(1)}, bf16[2,128,128]{2,1,0:T(8,128)(2,1)}, u32[]{:S(2)}) copy-start(bf16[2,128,128]{2,1,0:T(8,128)(2,1)} %wo_ref.3) | copy-start | bytes 196612
  105.7 40.7 %all-to-all-start.2 = ((bf16[128,16,128]{2,1,0:T(8,128)(2,1)}), bf16[128,16,128]{2,1,0:T(8,128)(2,1)S(1)}, u32[]{:S(2)}, u32[]{:S(2)}) async-start(bf16[128,16,128]{2,1,0:T(8,128)(2,1)} %get-tuple-element.21), calls=%async_computation.2 | async-start | bytes 1048576 | tf_op jit(solution)/shard_map/all_to_all | solution.py:253
  146.5 4.6 %copy-start.4 = (bf16[2,512,384]{2,1,0:T(8,128)(2,1)S(1)}, bf16[2,512,384]{2,1,0:T(8,128)(2,1)}, u32[]{:S(2)}) copy-start(bf16[2,512,384]{2,1,0:T(8,128)(2,1)} %constant.21.clone.rows_ref) | copy-start | bytes 2359300
  148.8 2.3 %copy-start.5 = (bf16[384,256]{1,0:T(8,128)(2,1)S(1)}, bf16[384,256]{1,0:T(8,128)(2,1)}, u32[]{:S(2)}) copy-start(bf16[384,256]{1,0:T(8,128)(2,1)} %constant.19.clone.gather_ref) | copy-start | bytes 589828
  152.9 10.2 %collective-permute-start.1 = (bf16[16,64,128]{2,1,0:T(8,128)(2,1)S(1)}, bf16[16,64,128]{2,1,0:T(8,128)(2,1)S(1)}, u32[]{:S(2)}, u32[]{:S(2)}) collective-permute-start(bf16[16,64,128]{2,1,0:T(8,128)(2,1)S(1)} %get-tuple-element.24), channel_id=1, source_target_pairs={{0,128},{128,0},{1,129},{129,1},{2,130},{130,2},{3,131},{131,3},{4... | collective-permute-start | bytes 786440 | tf_op jit(solution)/shard_map/ppermute | solution.py:261

commit v3 on v2

--- a/solution.py
+++ b/solution.py
@@ -11,7 +11,8 @@
 PARTS = (("y1", 2), ("y0", 2), ("zh", 4), ("core", 2), ("zl", 4), ("x", 4))
 ROW = ("y1", "y0", "zh", "core")
 CHAN = ("zl", "x")
-GROUP = ("zl", "x", "y1", "zh")
+TO_CHANNELS = ("x", "zl", "zh", "y1")
+TO_POSITIONS = ("zl", "x", "zh", "y1")
 SWAP = [(0, 1), (1, 0)]
 ROWS, COLS, C = 21, 42, 128
 T, U = 7, 3
@@ -109,7 +110,10 @@
 
 
 def fan(get, count, table):
-    wide = [jnp.concatenate([get(count * at + x) for x in range(count)], axis=1) for at in range(16 // count)]
+    wide = []
+    for zl in range(4):
+        for first in range(0, 4, count):
+            wide.append(jnp.concatenate([get(4 * x + zl) for x in range(first, first + count)], axis=1))
     return dot(jnp.concatenate(wide, axis=0), table, 1, 0)
 
 
@@ -160,21 +164,21 @@
     packed = outgoing_products(left, right, gather_ref)
     for s in range(8):
         high, low = divmod(s, 2)
-        y1, zh = divmod(s, 4)
+        zh, y1 = divmod(s, 2)
         out_ref[(2 * y1 + y0) * 4 + zh] = near_ref[s]
         out_ref[(2 * y1 + 1 - y0) * 4 + zh] = packed[64 * high : 64 * (high + 1), 128 * low : 128 * (low + 1)]
 
 
 def incoming_products(left, right, gather_ref, out_ref):
-    product = dot(left, right, 0, 0).astype(BF16)
+    product = dot(left, right, 0, 0)
     wide = []
     for pair in range(8):
-        for y1 in range(2):
-            part = [
-                product[128 * y1 + 32 * w : 128 * y1 + 32 * (w + 1), 128 * pair : 128 * (pair + 1)] for w in range(U)
-            ]
-            wide.append(jnp.concatenate(part, axis=1))
-    packed = dot(jnp.concatenate(wide, axis=0), gather_ref[...], 1, 0).astype(BF16)
+        for zh in range(4):
+            for y1 in range(2):
+                at = 128 * y1 + 8 * zh
+                part = [product[at + 32 * w : at + 32 * w + 8, 128 * pair : 128 * (pair + 1)] for w in range(U)]
+                wide.append(jnp.concatenate(part, axis=1))
+    packed = dot(jnp.concatenate(wide, axis=0).astype(BF16), gather_ref[...], 1, 0).astype(BF16)
     for pair in range(8):
         for x in range(2):
             out_ref[2 * pair + x] = packed[64 * pair : 64 * (pair + 1), 128 * x : 128 * (x + 1)]
@@ -230,10 +234,11 @@
 def shards(pair_rep, in_weights, out_weights):
     table, back = jnp.asarray(spread(), BF16), jnp.asarray(spread().T, BF16)
     gather = jnp.asarray(gather_rows(), BF16)
+    out_weights = jnp.swapaxes(out_weights.reshape(2, 4, 4, 8, C), 1, 2).reshape(2, C, C)
     y0, core = lax.axis_index("y0").astype(jnp.int32), lax.axis_index("core").astype(jnp.int32)
 
     msg, gate, flat = call(first_kernel, [MSG, FLAT, FLAT], (pair_rep, in_weights), "edges")
-    msg = lax.all_to_all(msg, GROUP, 0, 0, tiled=True)
+    msg = lax.all_to_all(msg, TO_CHANNELS, 0, 0, tiled=True)
     right = msg[:, 8:]
     far = lax.ppermute(right, "y0", SWAP)
     near = lax.all_gather(right, "core", axis=0).reshape(2, 16, 64, 128)
@@ -246,11 +251,11 @@
         outgoing_far_kernel, [(16, 64, 128)], (y0[None], left, near, far, table, gather),
         "outgoing_far", scratch=[(512, 1024)], scalars=1,
     )
-    product = lax.all_to_all(product.reshape(128, 8, 128), GROUP, 0, 0, tiled=True)
+    product = lax.all_to_all(product.reshape(128, 8, 128), TO_POSITIONS, 0, 0, tiled=True)
     msg, gate, flat = call(
         middle_kernel, [MSG, FLAT, FLAT], (product, flat, gate, out_weights, in_weights), "update_edges"
     )
-    msg = lax.all_to_all(msg, GROUP, 0, 0, tiled=True)
+    msg = lax.all_to_all(msg, TO_CHANNELS, 0, 0, tiled=True)
     left = lax.all_gather(msg[:, :8], "core", axis=0).reshape(2, 16, 64, 128)
     right = lax.all_gather(msg[:, 8:], "core", axis=0).reshape(2, 16, 64, 128)
     far, left, right = call(
@@ -261,7 +266,7 @@
     far = lax.ppermute(far, "y0", SWAP)
     (near,) = call(incoming_near_kernel, [(16, 64, 128)], (left, right, back), "incoming_near")
     product = (near.astype(F32) + far.astype(F32)).astype(BF16)
-    product = lax.all_to_all(product.reshape(128, 8, 128), GROUP, 0, 0, tiled=True)
+    product = lax.all_to_all(product.reshape(128, 8, 128), TO_POSITIONS, 0, 0, tiled=True)
     (out,) = call(last_kernel, [(ROWS, COLS, C)], (product, flat, gate, out_weights), "update")
     return out
 

time: 195 us -> 196 us (level)
  blocking collectives: 71 us -> 37.5 us
  waiting for transfers between devices: 76.4 us -> 103 us
  starting transfers between devices: 34.3 us -> 41.5 us
    all_to_all x2 -> x1, blocking collectives: 62.1 us -> 28.5 us  [shards(): lax.all_to_all(product.reshape(128, 8, 128), TO_POSITIONS, 0, 0, tiled=True)]
    all_to_all x2 -> x3, waiting for transfers between devices: 67.5 us -> 94.2 us  [the longest x2 70.7 us: shards(): msg = lax.all_to_all(msg, TO_CHANNELS, 0, 0, tiled=True)]
    all_to_all x2 -> x3, starting transfers between devices: 28.9 us -> 36 us  [the longest x2 28.7 us: shards(): msg = lax.all_to_all(msg, TO_CHANNELS, 0, 0, tiled=True)]
  transfers between devices with their start and end apart: 4 -> 5, of which waited for: 4 -> 5; matrix products, arithmetic and copies ran while one was open for 0% -> 0% of each run, Pallas kernels for 1% -> 1%
where the time goes in v3:
time: 196 us; the launch traced here: 195 us
  waiting for transfers between devices  103 us (53%)
  starting transfers between devices  41.5 us (21%)
  blocking collectives  37.5 us (19%)
  Pallas kernels  11 us (6%)
  local copies, waits for them, and re-layouts  2.02 us (1%)
    all_to_all x2, waiting for transfers between devices, shards(): msg = lax.all_to_all(msg, TO_CHANNELS, 0, 0, tiled=True)  70.7 us
    all_to_all x2, starting transfers between devices, shards(): msg = lax.all_to_all(msg, TO_CHANNELS, 0, 0, tiled=True)  28.7 us
    all_to_all x1, blocking collectives, shards(): lax.all_to_all(product.reshape(128, 8, 128), TO_POSITIONS, 0, 0, tiled=True)  28.5 us
    all_to_all x1, waiting for transfers between devices, shards(): lax.all_to_all(product.reshape(128, 8, 128), TO_POSITIONS, 0, 0, tiled=True)  23.4 us
    pallas_call x7, Pallas kernels, call(): pl.pallas_call(kernel, out_shape=[jax.ShapeDtypeStruct(s, BF16) for s in...  11 us
    all_to_all x1, starting transfers between devices, shards(): lax.all_to_all(product.reshape(128, 8, 128), TO_POSITIONS, 0, 0, tiled=True)  7.25 us
    ppermute x1, waiting for transfers between devices, shards(): far = lax.ppermute(far, 'y0', SWAP)  6.82 us
  transfers between devices with their start and end apart: 5, of which 5 were waited for; matrix products, arithmetic and copies ran while one was open for 0% of the time, Pallas kernels for 1%

profile of v3, /device:TPU:32, one launch (start us, length us, event | category | flops | bytes accessed | tf_op | source)
XLA Modules:
  0.0 195.4 jit_solution(15584398711406060116)
XLA Ops:
  0.0 0.0 copy-start
  0.0 1.0 copy-done
  1.0 0.0 copy-start.2
  1.0 0.9 copy-done.2
  1.9 2.0 %edges.1 = (bf16[128,16,128]{2,1,0:T(8,128)(2,1)}, bf16[7,128,128]{2,1,0:T(8,128)(2,1)S(1)}, bf16[7,128,128]{2,1,0:T(8,128)(2,1)S(1)}) custom-call(bf16[21,42,128]{2,1,0:T(8,128)(2,1)S(1)} %copy-done.2, bf16[2,128,640]{2,1,0:T(8,128)(2,1)S(1)} %copy-done), custom_call_target="tpu_custom_call" | custom-call | flops 2000000000 | bytes 1536512 | tf_op jit(solution)/shard_map/edges/pallas_call | solution.py:218
  3.9 21.6 %all-to-all-start = ((bf16[128,16,128]{2,1,0:T(8,128)(2,1)}), bf16[128,16,128]{2,1,0:T(8,128)(2,1)S(1)}, u32[]{:S(2)}, u32[]{:S(2)}) async-start(bf16[128,16,128]{2,1,0:T(8,128)(2,1)} %get-tuple-element.16), calls=%async_computation | async-start | bytes 1048576 | tf_op jit(solution)/shard_map/all_to_all | solution.py:241
  25.5 35.6 %all-to-all-done = bf16[128,16,128]{2,1,0:T(8,128)(2,1)S(1)} async-done(((bf16[128,16,128]{2,1,0:T(8,128)(2,1)}), bf16[128,16,128]{2,1,0:T(8,128)(2,1)S(1)}, u32[]{:S(2)}, u32[]{:S(2)}) %all-to-all-start) | async-done | bytes 524320 | tf_op jit(solution)/shard_map/all_to_all | solution.py:241
  61.1 0.0 copy-start.5
  61.1 0.0 copy-start.6
  61.1 2.7 %collective-permute-start = (bf16[128,8,128]{2,1,0:T(8,128)(2,1)S(1)}, bf16[128,8,128]{2,1,0:T(8,128)(2,1)S(1)}, u32[]{:S(2)}, u32[]{:S(2)}) collective-permute-start(bf16[128,8,128]{2,1,0:T(8,128)(2,1)S(1)} %slice.12), channel_id=1, source_target_pairs={{0,128},{128,0},{1,129},{129,1},{2,130},{130,2},{3,131},{131,3},{4... | collective-permute-start | bytes 786440 | tf_op jit(solution)/shard_map/ppermute | solution.py:243
  63.9 2.2 %all-gather = bf16[256,8,128]{2,1,0:T(8,128)(2,1)S(1)} all-gather(bf16[128,8,128]{2,1,0:T(8,128)(2,1)S(1)} %slice.12), channel_id=2, replica_groups=mesh['y1'=2,'y0'=2,'zh'=4,'core'=2,'zl'=4,'x'=4] {'core'}, dimensions={0}, use_global_device_ids=true | all-gather | bytes 786432 | tf_op jit(solution)/shard_map/all_gather | solution.py:244
  66.0 0.0 copy-done.5
  66.0 0.0 copy-done.6
  66.0 1.4 outgoing_near.1
  67.4 2.1 %collective-permute-done = bf16[128,8,128]{2,1,0:T(8,128)(2,1)S(1)} collective-permute-done((bf16[128,8,128]{2,1,0:T(8,128)(2,1)S(1)}, bf16[128,8,128]{2,1,0:T(8,128)(2,1)S(1)}, u32[]{:S(2)}, u32[]{:S(2)}) %collective-permute-start) | collective-permute-done | bytes 262176 | tf_op jit(solution)/shard_map/ppermute | solution.py:243
  69.5 2.2 %all-gather.1 = bf16[256,8,128]{2,1,0:T(8,128)(2,1)S(1)} all-gather(bf16[128,8,128]{2,1,0:T(8,128)(2,1)S(1)} %collective-permute-done), channel_id=3, replica_groups=mesh['y1'=2,'y0'=2,'zh'=4,'core'=2,'zl'=4,'x'=4] {'core'}, dimensions={0}, use_global_device_ids=true | all-gather | bytes 786432 | tf_op jit(solution)/shard_map/all_gather | solution.py:249
  71.7 1.8 outgoing_far.1
  73.5 0.0 copy-start.7
  73.5 0.0 copy-start.1
  73.5 7.2 %all-to-all-start.1 = ((bf16[128,8,128]{2,1,0:T(8,128)(2,1)}), bf16[128,8,128]{2,1,0:T(8,128)(2,1)S(1)}, u32[]{:S(2)}, u32[]{:S(2)}) async-start(bf16[128,8,128]{2,1,0:T(8,128)(2,1)} %bitcast.5), calls=%async_computation.1 | async-start | bytes 524288 | tf_op jit(solution)/shard_map/all_to_all | solution.py:254
  80.8 0.0 copy-done.7
  80.8 23.4 %all-to-all-done.1.x_ref = bf16[128,8,128]{2,1,0:T(8,128)(2,1)S(1)} async-done(((bf16[128,8,128]{2,1,0:T(8,128)(2,1)}), bf16[128,8,128]{2,1,0:T(8,128)(2,1)S(1)}, u32[]{:S(2)}, u32[]{:S(2)}) %all-to-all-start.1) | async-done | bytes 262176 | tf_op jit(solution)/shard_map/all_to_all | solution.py:254
  104.3 0.0 copy-done.1
  104.3 2.2 %update_edges.1 = (bf16[128,16,128]{2,1,0:T(8,128)(2,1)}, bf16[7,128,128]{2,1,0:T(8,128)(2,1)S(1)}, bf16[7,128,128]{2,1,0:T(8,128)(2,1)S(1)}) custom-call(bf16[128,8,128]{2,1,0:T(8,128)(2,1)S(1)} %all-to-all-done.1.x_ref, bf16[7,128,128]{2,1,0:T(8,128)(2,1)S(1)} %get-tuple-element.19.p_ref, bf16[7,128,128]{2,1,0:T(8,128)(2,1)S(1)} %get-tuple-element.20.gate_ref, ...), custom_call_target="tpu_custom_call" | custom-call | flops 2000000000 | bytes 2097152 | tf_op jit(solution)/shard_map/update_edges/pallas_call | solution.py:218
  106.5 7.1 %all-to-all-start.2 = ((bf16[128,16,128]{2,1,0:T(8,128)(2,1)}), bf16[128,16,128]{2,1,0:T(8,128)(2,1)S(1)}, u32[]{:S(2)}, u32[]{:S(2)}) async-start(bf16[128,16,128]{2,1,0:T(8,128)(2,1)} %get-tuple-element.21), calls=%async_computation.2 | async-start | bytes 1048576 | tf_op jit(solution)/shard_map/all_to_all | solution.py:258
  113.6 0.1 pad_add_fusion.at_ref
  113.7 35.2 %all-to-all-done.2 = bf16[128,16,128]{2,1,0:T(8,128)(2,1)S(1)} async-done(((bf16[128,16,128]{2,1,0:T(8,128)(2,1)}), bf16[128,16,128]{2,1,0:T(8,128)(2,1)S(1)}, u32[]{:S(2)}, u32[]{:S(2)}) %all-to-all-start.2) | async-done | bytes 524320 | tf_op jit(solution)/shard_map/all_to_all | solution.py:258
  148.9 0.0 copy-start.3
  148.9 2.3 %all-gather.3 = bf16[256,8,128]{2,1,0:T(8,128)(2,1)S(1)} all-gather(bf16[128,8,128]{2,1,0:T(8,128)(2,1)S(1)} %get-tuple-element.27), channel_id=5, replica_groups=mesh['y1'=2,'y0'=2,'zh'=4,'core'=2,'zl'=4,'x'=4] {'core'}, dimensions={0}, use_global_device_ids=true | all-gather | bytes 786432 | tf_op jit(solution)/shard_map/all_gather | solution.py:260
  151.2 0.0 copy-start.4
  151.2 2.3 %all-gather.2 = bf16[256,8,128]{2,1,0:T(8,128)(2,1)S(1)} all-gather(bf16[128,8,128]{2,1,0:T(8,128)(2,1)S(1)} %get-tuple-element.28), channel_id=4, replica_groups=mesh['y1'=2,'y0'=2,'zh'=4,'core'=2,'zl'=4,'x'=4] {'core'}, dimensions={0}, use_global_device_ids=true | all-gather | bytes 786432 | tf_op jit(solution)/shard_map/all_gather | solution.py:259
  153.5 0.0 copy-done.3
  153.5 0.0 copy-done.4
  153.5 1.8 incoming_far.1
  155.3 2.8 %collective-permute-start.1 = (bf16[16,64,128]{2,1,0:T(8,128)(2,1)S(1)}, bf16[16,64,128]{2,1,0:T(8,128)(2,1)S(1)}, u32[]{:S(2)}, u32[]{:S(2)}) collective-permute-start(bf16[16,64,128]{2,1,0:T(8,128)(2,1)S(1)} %get-tuple-element.24), channel_id=1, source_target_pairs={{0,128},{128,0},{1,129},{129,1},{2,130},{130,2},{3,131},{131,3},{4... | collective-permute-start | bytes 786440 | tf_op jit(solution)/shard_map/ppermute | solution.py:266
  158.1 0.6 incoming_near.1
  158.7 6.8 %collective-permute-done.1 = bf16[16,64,128]{2,1,0:T(8,128)(2,1)S(1)} collective-permute-done((bf16[16,64,128]{2,1,0:T(8,128)(2,1)S(1)}, bf16[16,64,128]{2,1,0:T(8,128)(2,1)S(1)}, u32[]{:S(2)}, u32[]{:S(2)}) %collective-permute-start.1) | collective-permute-done | bytes 262176 | tf_op jit(solution)/shard_map/ppermute | solution.py:266
  165.6 0.1 add_convert_fusion
  165.6 28.5 %all_to_all.20.x_ref = bf16[128,8,128]{2,1,0:T(8,128)(2,1)S(1)} all-to-all(bf16[128,8,128]{2,1,0:T(8,128)(2,1)S(1)} %bitcast.20), channel_id=1, replica_groups=mesh['y1'=2,'y0'=2,'zh'=4,'core'=2,'zl'=4,'x'=4] {'zl','x','zh','y1'}, dimensions={0} | all-to-all | bytes 524288 | tf_op jit(solution)/shard_map/all_to_all | solution.py:269
  194.2 1.2 update.1
  (3 shorter events, 0.1 us)
Async XLA Ops:
  0.0 1.0 copy-start
  1.0 0.9 copy-start.2
  3.9 57.2 %all-to-all-start = ((bf16[128,16,128]{2,1,0:T(8,128)(2,1)}), bf16[128,16,128]{2,1,0:T(8,128)(2,1)S(1)}, u32[]{:S(2)}, u32[]{:S(2)}) async-start(bf16[128,16,128]{2,1,0:T(8,128)(2,1)} %get-tuple-element.16), calls=%async_computation | async-start | bytes 1048576 | tf_op jit(solution)/shard_map/all_to_all | solution.py:241
  61.1 4.9 %copy-start.5 = (bf16[256,384]{1,0:T(8,128)(2,1)S(1)}, bf16[256,384]{1,0:T(8,128)(2,1)}, u32[]{:S(2)}) copy-start(bf16[256,384]{1,0:T(8,128)(2,1)} %constant.18.clone.spread_ref) | copy-start | bytes 589828
  61.1 4.9 %copy-start.6 = (bf16[384,256]{1,0:T(8,128)(2,1)S(1)}, bf16[384,256]{1,0:T(8,128)(2,1)}, u32[]{:S(2)}) copy-start(bf16[384,256]{1,0:T(8,128)(2,1)} %constant.20.clone.gather_ref) | copy-start | bytes 589828
  61.1 8.4 %collective-permute-start = (bf16[128,8,128]{2,1,0:T(8,128)(2,1)S(1)}, bf16[128,8,128]{2,1,0:T(8,128)(2,1)S(1)}, u32[]{:S(2)}, u32[]{:S(2)}) collective-permute-start(bf16[128,8,128]{2,1,0:T(8,128)(2,1)S(1)} %slice.12), channel_id=1, source_target_pairs={{0,128},{128,0},{1,129},{129,1},{2,130},{130,2},{3,131},{131,3},{4... | collective-permute-start | bytes 786440 | tf_op jit(solution)/shard_map/ppermute | solution.py:243
  73.5 7.3 %copy-start.7 = (bf16[2,128,128]{2,1,0:T(8,128)(2,1)S(1)}, bf16[2,128,128]{2,1,0:T(8,128)(2,1)}, u32[]{:S(2)}) copy-start(bf16[2,128,128]{2,1,0:T(8,128)(2,1)} %param.9) | copy-start | bytes 196612
  73.5 30.7 %copy-start.1 = (bf16[2,128,640]{2,1,0:T(8,128)(2,1)S(1)}, bf16[2,128,640]{2,1,0:T(8,128)(2,1)}, u32[]{:S(2)}) copy-start(bf16[2,128,640]{2,1,0:T(8,128)(2,1)} %w_ref.3) | copy-start | bytes 983044
  73.5 30.7 %all-to-all-start.1 = ((bf16[128,8,128]{2,1,0:T(8,128)(2,1)}), bf16[128,8,128]{2,1,0:T(8,128)(2,1)S(1)}, u32[]{:S(2)}, u32[]{:S(2)}) async-start(bf16[128,8,128]{2,1,0:T(8,128)(2,1)} %bitcast.5), calls=%async_computation.1 | async-start | bytes 524288 | tf_op jit(solution)/shard_map/all_to_all | solution.py:254
  106.5 42.4 %all-to-all-start.2 = ((bf16[128,16,128]{2,1,0:T(8,128)(2,1)}), bf16[128,16,128]{2,1,0:T(8,128)(2,1)S(1)}, u32[]{:S(2)}, u32[]{:S(2)}) async-start(bf16[128,16,128]{2,1,0:T(8,128)(2,1)} %get-tuple-element.21), calls=%async_computation.2 | async-start | bytes 1048576 | tf_op jit(solution)/shard_map/all_to_all | solution.py:258
  148.9 4.6 %copy-start.3 = (bf16[2,512,384]{2,1,0:T(8,128)(2,1)S(1)}, bf16[2,512,384]{2,1,0:T(8,128)(2,1)}, u32[]{:S(2)}) copy-start(bf16[2,512,384]{2,1,0:T(8,128)(2,1)} %constant.21.clone.rows_ref) | copy-start | bytes 2359300
  151.2 2.3 %copy-start.4 = (bf16[384,256]{1,0:T(8,128)(2,1)S(1)}, bf16[384,256]{1,0:T(8,128)(2,1)}, u32[]{:S(2)}) copy-start(bf16[384,256]{1,0:T(8,128)(2,1)} %constant.19.clone.gather_ref) | copy-start | bytes 589828
  155.3 10.2 %collective-permute-start.1 = (bf16[16,64,128]{2,1,0:T(8,128)(2,1)S(1)}, bf16[16,64,128]{2,1,0:T(8,128)(2,1)S(1)}, u32[]{:S(2)}, u32[]{:S(2)}) collective-permute-start(bf16[16,64,128]{2,1,0:T(8,128)(2,1)S(1)} %get-tuple-element.24), channel_id=1, source_target_pairs={{0,128},{128,0},{1,129},{129,1},{2,130},{130,2},{3,131},{131,3},{4... | collective-permute-start | bytes 786440 | tf_op jit(solution)/shard_map/ppermute | solution.py:266

commit v4 on v3

--- a/solution.py
+++ b/solution.py
@@ -12,7 +12,7 @@
 ROW = ("y1", "y0", "zh", "core")
 CHAN = ("zl", "x")
 TO_CHANNELS = ("x", "zl", "zh", "y1")
-TO_POSITIONS = ("zl", "x", "zh", "y1")
+TO_POSITIONS = ("zl", "x", "y1", "zh")
 SWAP = [(0, 1), (1, 0)]
 ROWS, COLS, C = 21, 42, 128
 T, U = 7, 3
@@ -35,7 +35,7 @@
             for u in range(U):
                 for t in range(T):
                     for w in range(U):
-                        table[core, x, COLS * u + ROWS * core + U * t + w, u, 32 * w + 8 * x + t] = 1
+                        table[core, x, COLS * u + ROWS * core + U * t + w, u, 32 * w + 8 * x + t + 1] = 1
     return table.reshape(2, 512, U * 128)
 
 
@@ -69,16 +69,15 @@
         lefts.append(jax.nn.sigmoid(projected[C : 2 * C]) * projected[:C])
         rights.append(jax.nn.sigmoid(projected[3 * C : 4 * C]) * projected[2 * C : 3 * C])
         gate_ref[t] = jax.nn.sigmoid(dot(normed, w_ref[step, :, 4 * C :], 1, 0)).astype(BF16)
-    none = jnp.zeros((C, 128), F32)
-    both = jnp.stack(lefts + [none] + rights + [none], axis=0)
-    msg_ref[...] = jnp.swapaxes(both, 0, 1).astype(BF16)
+    both = jnp.stack(rights + lefts, axis=0)
+    msg_ref[...] = jnp.swapaxes(both, 0, 1).astype(BF16).reshape(C, T, 2, 128)
 
 
 def updated(x_ref, p_ref, gate_ref, w_ref, step):
     product = jnp.swapaxes(x_ref[...].astype(F32), 0, 1)
     blocks = []
     for t in range(T):
-        normed = layer_norm(product[t], 0).astype(BF16)
+        normed = layer_norm(product[t + 1], 0).astype(BF16)
         outward = dot(normed, w_ref[step], 0, 0)
         blocks.append((p_ref[t].astype(F32) + gate_ref[t].astype(F32) * outward).astype(BF16))
     return blocks
@@ -133,12 +132,13 @@
         jnp.concatenate([product[64 * u : 64 * (u + 1), 128 * high : 128 * (high + 1)] for u in range(U)], axis=1)
         for high in range(4)
     ]
-    return dot(jnp.concatenate(wide, axis=0), gather_ref[...], 1, 0).astype(BF16)
-
-
-def outgoing_near_kernel(msg_ref, near_ref, spread_ref, gather_ref, left, out_ref, right):
+    packed = dot(jnp.concatenate(wide, axis=0), gather_ref[...], 1, 0)
+    return jnp.swapaxes(packed.reshape(4, 4, 2, 8, 256), 1, 2).reshape(256, 256).astype(BF16)
+
+
+def outgoing_near_kernel(left_ref, near_ref, spread_ref, gather_ref, left, out_ref, right):
     table = spread_ref[...]
-    part = fan(lambda at: msg_ref[at], 2, table).reshape(64, 2, 8, U * 128)[:, 0].reshape(512, U * 128).astype(BF16)
+    part = fan(lambda at: left_ref[at], 2, table).astype(BF16)
     for pair in range(8):
         for u in range(U):
             left[64 * u : 64 * (u + 1), 128 * pair : 128 * (pair + 1)] = part[
@@ -170,15 +170,15 @@
 
 
 def incoming_products(left, right, gather_ref, out_ref):
-    product = dot(left, right, 0, 0)
+    product = dot(left, right, 0, 0).astype(BF16)
     wide = []
     for pair in range(8):
-        for zh in range(4):
-            for y1 in range(2):
-                at = 128 * y1 + 8 * zh
-                part = [product[at + 32 * w : at + 32 * w + 8, 128 * pair : 128 * (pair + 1)] for w in range(U)]
-                wide.append(jnp.concatenate(part, axis=1))
-    packed = dot(jnp.concatenate(wide, axis=0).astype(BF16), gather_ref[...], 1, 0).astype(BF16)
+        for y1 in range(2):
+            part = [
+                product[128 * y1 + 32 * w : 128 * y1 + 32 * (w + 1), 128 * pair : 128 * (pair + 1)] for w in range(U)
+            ]
+            wide.append(jnp.concatenate(part, axis=1))
+    packed = dot(jnp.concatenate(wide, axis=0), gather_ref[...], 1, 0).astype(BF16)
     for pair in range(8):
         for x in range(2):
             out_ref[2 * pair + x] = packed[64 * pair : 64 * (pair + 1), 128 * x : 128 * (x + 1)]
@@ -190,7 +190,9 @@
     y0, mine = at_ref[0], at_ref[1]
     table, rows = spread_ref[...], rows_ref[mine]
     for core in range(2):
-        lefts = fan(lambda m: left_ref[core, m], 4, rows).astype(BF16)
+        lefts = pltpu.roll(fan(lambda m: left_ref[core, m], 4, rows).reshape(32, 8, U * 128), 7, 1)
+        at_t = lax.broadcasted_iota(jnp.int32, lefts.shape, 1)
+        lefts = jnp.where(at_t < T, lefts, 0).reshape(256, U * 128).astype(BF16)
         rights = fan(lambda m: right_ref[core, m], 2, table).astype(BF16)
         for u in range(U):
             at = 192 * core + 64 * u
@@ -228,25 +230,25 @@
 
 
 FLAT = (T, 128, C)
-MSG = (C, 16, 128)
+MSG = (C, T, 2, 128)
 
 
 def shards(pair_rep, in_weights, out_weights):
     table, back = jnp.asarray(spread(), BF16), jnp.asarray(spread().T, BF16)
     gather = jnp.asarray(gather_rows(), BF16)
-    out_weights = jnp.swapaxes(out_weights.reshape(2, 4, 4, 8, C), 1, 2).reshape(2, C, C)
+    out_weights = out_weights.reshape(2, 4, 4, 4, 2, C).transpose(0, 2, 1, 4, 3, 5).reshape(2, C, C)
     y0, core = lax.axis_index("y0").astype(jnp.int32), lax.axis_index("core").astype(jnp.int32)
 
     msg, gate, flat = call(first_kernel, [MSG, FLAT, FLAT], (pair_rep, in_weights), "edges")
     msg = lax.all_to_all(msg, TO_CHANNELS, 0, 0, tiled=True)
-    right = msg[:, 8:]
+    right = msg[:, :4].reshape(C, 8, 128)
     far = lax.ppermute(right, "y0", SWAP)
-    near = lax.all_gather(right, "core", axis=0).reshape(2, 16, 64, 128)
+    near = lax.all_gather(right, "core", axis=0, tiled=True).reshape(2, 16, 64, 128)
     left, near = call(
-        outgoing_near_kernel, [(192, 1024), (8, 64, 128)], (msg.reshape(16, 128, 128), near, table, gather),
+        outgoing_near_kernel, [(192, 1024), (8, 64, 128)], (msg[:, 3:].reshape(16, 64, 128), near, table, gather),
         "outgoing_near", scratch=[(512, 1024)],
     )
-    far = lax.all_gather(far, "core", axis=0).reshape(2, 16, 64, 128)
+    far = lax.all_gather(far, "core", axis=0, tiled=True).reshape(2, 16, 64, 128)
     (product,) = call(
         outgoing_far_kernel, [(16, 64, 128)], (y0[None], left, near, far, table, gather),
         "outgoing_far", scratch=[(512, 1024)], scalars=1,
@@ -256,8 +258,8 @@
         middle_kernel, [MSG, FLAT, FLAT], (product, flat, gate, out_weights, in_weights), "update_edges"
     )
     msg = lax.all_to_all(msg, TO_CHANNELS, 0, 0, tiled=True)
-    left = lax.all_gather(msg[:, :8], "core", axis=0).reshape(2, 16, 64, 128)
-    right = lax.all_gather(msg[:, 8:], "core", axis=0).reshape(2, 16, 64, 128)
+    left = lax.all_gather(msg[:, 3:].reshape(C, 8, 128), "core", axis=0, tiled=True).reshape(2, 16, 64, 128)
+    right = lax.all_gather(msg[:, :4].reshape(C, 8, 128), "core", axis=0, tiled=True).reshape(2, 16, 64, 128)
     far, left, right = call(
         incoming_far_kernel, [(16, 64, 128), (384, 256), (384, 1024)],
         (jnp.stack([y0, core]), left, right, table, jnp.asarray(spread_rows(), BF16), back),

time: 196 us -> 192 us (0.980)
  waiting for transfers between devices: 103 us -> 97.9 us
    all_to_all x2, waiting for transfers between devices: 70.7 us -> 65.2 us  [shards(): msg = lax.all_to_all(msg, TO_CHANNELS, 0, 0, tiled=True)]
where the time goes in v4:
time: 192 us; the launch traced here: 191 us
  waiting for transfers between devices  97.9 us (51%)
  starting transfers between devices  41 us (21%)
  blocking collectives  37.7 us (20%)
  Pallas kernels  11.3 us (6%)
  local copies, waits for them, and re-layouts  2.7 us (1%)
    all_to_all x2, waiting for transfers between devices, shards(): msg = lax.all_to_all(msg, TO_CHANNELS, 0, 0, tiled=True)  65.2 us
    all_to_all x2, starting transfers between devices, shards(): msg = lax.all_to_all(msg, TO_CHANNELS, 0, 0, tiled=True)  28.7 us
    all_to_all x1, blocking collectives, shards(): lax.all_to_all(product.reshape(128, 8, 128), TO_POSITIONS, 0, 0, tiled=True)  28.6 us
    all_to_all x1, waiting for transfers between devices, shards(): lax.all_to_all(product.reshape(128, 8, 128), TO_POSITIONS, 0, 0, tiled=True)  23.5 us
    pallas_call x7, Pallas kernels, call(): pl.pallas_call(kernel, out_shape=[jax.ShapeDtypeStruct(s, BF16) for s in...  11.3 us
    all_to_all x1, starting transfers between devices, shards(): lax.all_to_all(product.reshape(128, 8, 128), TO_POSITIONS, 0, 0, tiled=True)  7.09 us
    ppermute x1, waiting for transfers between devices, shards(): far = lax.ppermute(far, 'y0', SWAP)  7.01 us
  transfers between devices with their start and end apart: 5, of which 5 were waited for; matrix products, arithmetic and copies ran while one was open for 0% of the time, Pallas kernels for 1%

profile of v4, /device:TPU:32, one launch (start us, length us, event | category | flops | bytes accessed | tf_op | source)
XLA Modules:
  0.0 191.0 jit_solution(14409143836382052896)
XLA Ops:
  0.0 0.0 copy-start
  0.0 1.0 copy-done
  1.0 0.0 copy-start.2
  1.0 0.9 copy-done.2
  1.9 2.2 %edges.1 = (bf16[128,7,2,128]{3,2,1,0:T(2,128)(2,1)}, bf16[7,128,128]{2,1,0:T(8,128)(2,1)S(1)}, bf16[7,128,128]{2,1,0:T(8,128)(2,1)S(1)}) custom-call(bf16[21,42,128]{2,1,0:T(8,128)(2,1)S(1)} %copy-done.2, bf16[2,128,640]{2,1,0:T(8,128)(2,1)S(1)} %copy-done), custom_call_target="tpu_custom_call" | custom-call | flops 2000000000 | bytes 1470976 | tf_op jit(solution)/shard_map/edges/pallas_call | solution.py:220
  4.2 21.6 %all-to-all-start = ((bf16[128,7,2,128]{3,2,1,0:T(2,128)(2,1)}), bf16[128,7,2,128]{3,2,1,0:T(2,128)(2,1)S(1)}, u32[]{:S(2)}, u32[]{:S(2)}) async-start(bf16[128,7,2,128]{3,2,1,0:T(2,128)(2,1)} %get-tuple-element.16), calls=%async_computation | async-start | bytes 917504 | tf_op jit(solution)/shard_map/all_to_all | solution.py:243
  25.8 32.8 %all-to-all-done = bf16[128,7,2,128]{3,2,1,0:T(2,128)(2,1)S(1)} async-done(((bf16[128,7,2,128]{3,2,1,0:T(2,128)(2,1)}), bf16[128,7,2,128]{3,2,1,0:T(2,128)(2,1)S(1)}, u32[]{:S(2)}, u32[]{:S(2)}) %all-to-all-start) | async-done | bytes 458784 | tf_op jit(solution)/shard_map/all_to_all | solution.py:243
  58.6 0.4 fusion.1
  59.0 0.0 copy-start.5
  59.0 0.0 copy-start.6
  59.0 2.7 %collective-permute-start = (bf16[128,8,128]{2,1,0:T(8,128)(2,1)S(1)}, bf16[128,8,128]{2,1,0:T(8,128)(2,1)S(1)}, u32[]{:S(2)}, u32[]{:S(2)}) collective-permute-start(bf16[128,8,128]{2,1,0:T(8,128)(2,1)S(1)} %bitcast.24), channel_id=1, source_target_pairs={{0,128},{128,0},{1,129},{129,1},{2,130},{130,2},{3,131},{131,3},{4... | collective-permute-start | bytes 786440 | tf_op jit(solution)/shard_map/ppermute | solution.py:245
  61.7 2.2 %all_gather.12 = bf16[256,8,128]{2,1,0:T(8,128)(2,1)S(1)} all-gather(bf16[128,8,128]{2,1,0:T(8,128)(2,1)S(1)} %bitcast.25), channel_id=1, replica_groups=mesh['y1'=2,'y0'=2,'zh'=4,'core'=2,'zl'=4,'x'=4] {'core'}, dimensions={0}, use_global_device_ids=true | all-gather | bytes 786432 | tf_op jit(solution)/shard_map/all_gather | solution.py:246
  63.9 0.0 copy-done.5
  63.9 0.0 copy-done.6
  63.9 1.2 outgoing_near.1
  65.2 2.2 %collective-permute-done = bf16[128,8,128]{2,1,0:T(8,128)(2,1)S(1)} collective-permute-done((bf16[128,8,128]{2,1,0:T(8,128)(2,1)S(1)}, bf16[128,8,128]{2,1,0:T(8,128)(2,1)S(1)}, u32[]{:S(2)}, u32[]{:S(2)}) %collective-permute-start) | collective-permute-done | bytes 262176 | tf_op jit(solution)/shard_map/ppermute | solution.py:245
  67.4 2.2 %all_gather.13 = bf16[256,8,128]{2,1,0:T(8,128)(2,1)S(1)} all-gather(bf16[128,8,128]{2,1,0:T(8,128)(2,1)S(1)} %collective-permute-done), channel_id=1, replica_groups=mesh['y1'=2,'y0'=2,'zh'=4,'core'=2,'zl'=4,'x'=4] {'core'}, dimensions={0}, use_global_device_ids=true | all-gather | bytes 786432 | tf_op jit(solution)/shard_map/all_gather | solution.py:251
  69.6 1.8 outgoing_far.1
  71.4 0.0 copy-start.7
  71.4 0.0 copy-start.1
  71.4 7.1 %all-to-all-start.1 = ((bf16[128,8,128]{2,1,0:T(8,128)(2,1)}), bf16[128,8,128]{2,1,0:T(8,128)(2,1)S(1)}, u32[]{:S(2)}, u32[]{:S(2)}) async-start(bf16[128,8,128]{2,1,0:T(8,128)(2,1)} %bitcast.6), calls=%async_computation.1 | async-start | bytes 524288 | tf_op jit(solution)/shard_map/all_to_all | solution.py:256
  78.5 0.0 copy-done.7
  78.5 23.5 %all-to-all-done.1.x_ref = bf16[128,8,128]{2,1,0:T(8,128)(2,1)S(1)} async-done(((bf16[128,8,128]{2,1,0:T(8,128)(2,1)}), bf16[128,8,128]{2,1,0:T(8,128)(2,1)S(1)}, u32[]{:S(2)}, u32[]{:S(2)}) %all-to-all-start.1) | async-done | bytes 262176 | tf_op jit(solution)/shard_map/all_to_all | solution.py:256
  102.0 0.0 copy-done.1
  102.0 2.4 %update_edges.1 = (bf16[128,7,2,128]{3,2,1,0:T(2,128)(2,1)}, bf16[7,128,128]{2,1,0:T(8,128)(2,1)S(1)}, bf16[7,128,128]{2,1,0:T(8,128)(2,1)S(1)}) custom-call(bf16[128,8,128]{2,1,0:T(8,128)(2,1)S(1)} %all-to-all-done.1.x_ref, bf16[7,128,128]{2,1,0:T(8,128)(2,1)S(1)} %get-tuple-element.19.p_ref, bf16[7,128,128]{2,1,0:T(8,128)(2,1)S(1)} %get-tuple-element.20.gate_ref, ...), custom_call_target="tpu_custom_call" | custom-call | flops 2000000000 | bytes 2031616 | tf_op jit(solution)/shard_map/update_edges/pallas_call | solution.py:220
  104.4 7.0 %all-to-all-start.2 = ((bf16[128,7,2,128]{3,2,1,0:T(2,128)(2,1)}), bf16[128,7,2,128]{3,2,1,0:T(2,128)(2,1)S(1)}, u32[]{:S(2)}, u32[]{:S(2)}) async-start(bf16[128,7,2,128]{3,2,1,0:T(2,128)(2,1)} %get-tuple-element.21), calls=%async_computation.2 | async-start | bytes 917504 | tf_op jit(solution)/shard_map/all_to_all | solution.py:260
  111.5 0.1 pad_add_fusion.at_ref
  111.6 32.4 %all-to-all-done.2 = bf16[128,7,2,128]{3,2,1,0:T(2,128)(2,1)S(1)} async-done(((bf16[128,7,2,128]{3,2,1,0:T(2,128)(2,1)}), bf16[128,7,2,128]{3,2,1,0:T(2,128)(2,1)S(1)}, u32[]{:S(2)}, u32[]{:S(2)}) %all-to-all-start.2) | async-done | bytes 458784 | tf_op jit(solution)/shard_map/all_to_all | solution.py:260
  144.0 0.4 fusion
  144.3 0.0 copy-start.3
  144.3 2.3 %all_gather.14 = bf16[256,8,128]{2,1,0:T(8,128)(2,1)S(1)} all-gather(bf16[128,8,128]{2,1,0:T(8,128)(2,1)S(1)} %bitcast.27), channel_id=1, replica_groups=mesh['y1'=2,'y0'=2,'zh'=4,'core'=2,'zl'=4,'x'=4] {'core'}, dimensions={0}, use_global_device_ids=true | all-gather | bytes 786432 | tf_op jit(solution)/shard_map/all_gather | solution.py:261
  146.6 0.0 copy-start.4
  146.6 2.5 %all_gather.15 = bf16[256,8,128]{2,1,0:T(8,128)(2,1)S(1)} all-gather(bf16[128,8,128]{2,1,0:T(8,128)(2,1)S(1)} %bitcast.26), channel_id=1, replica_groups=mesh['y1'=2,'y0'=2,'zh'=4,'core'=2,'zl'=4,'x'=4] {'core'}, dimensions={0}, use_global_device_ids=true | all-gather | bytes 786432 | tf_op jit(solution)/shard_map/all_gather | solution.py:262
  149.1 0.0 copy-done.3
  149.1 0.0 copy-done.4
  149.1 1.8 incoming_far.1
  150.9 2.6 %collective-permute-start.1 = (bf16[16,64,128]{2,1,0:T(8,128)(2,1)S(1)}, bf16[16,64,128]{2,1,0:T(8,128)(2,1)S(1)}, u32[]{:S(2)}, u32[]{:S(2)}) collective-permute-start(bf16[16,64,128]{2,1,0:T(8,128)(2,1)S(1)} %get-tuple-element.24), channel_id=1, source_target_pairs={{0,128},{128,0},{1,129},{129,1},{2,130},{130,2},{3,131},{131,3},{4... | collective-permute-start | bytes 786440 | tf_op jit(solution)/shard_map/ppermute | solution.py:268
  153.5 0.6 incoming_near.1
  154.2 7.0 %collective-permute-done.1 = bf16[16,64,128]{2,1,0:T(8,128)(2,1)S(1)} collective-permute-done((bf16[16,64,128]{2,1,0:T(8,128)(2,1)S(1)}, bf16[16,64,128]{2,1,0:T(8,128)(2,1)S(1)}, u32[]{:S(2)}, u32[]{:S(2)}) %collective-permute-start.1) | collective-permute-done | bytes 262176 | tf_op jit(solution)/shard_map/ppermute | solution.py:268
  161.2 0.1 add_convert_fusion
  161.3 28.6 %all_to_all.20.x_ref = bf16[128,8,128]{2,1,0:T(8,128)(2,1)S(1)} all-to-all(bf16[128,8,128]{2,1,0:T(8,128)(2,1)S(1)} %bitcast.23), channel_id=1, replica_groups=mesh['y1'=2,'y0'=2,'zh'=4,'core'=2,'zl'=4,'x'=4] {'zl','x','y1','zh'}, dimensions={0} | all-to-all | bytes 524288 | tf_op jit(solution)/shard_map/all_to_all | solution.py:271
  189.9 1.2 update.1
  (1 shorter events, 0.0 us)
Async XLA Ops:
  0.0 1.0 copy-start
  1.0 0.9 copy-start.2
  4.2 54.4 %all-to-all-start = ((bf16[128,7,2,128]{3,2,1,0:T(2,128)(2,1)}), bf16[128,7,2,128]{3,2,1,0:T(2,128)(2,1)S(1)}, u32[]{:S(2)}, u32[]{:S(2)}) async-start(bf16[128,7,2,128]{3,2,1,0:T(2,128)(2,1)} %get-tuple-element.16), calls=%async_computation | async-start | bytes 917504 | tf_op jit(solution)/shard_map/all_to_all | solution.py:243
  59.0 4.9 %copy-start.5 = (bf16[256,384]{1,0:T(8,128)(2,1)S(1)}, bf16[256,384]{1,0:T(8,128)(2,1)}, u32[]{:S(2)}) copy-start(bf16[256,384]{1,0:T(8,128)(2,1)} %constant.18.clone.spread_ref) | copy-start | bytes 589828
  59.0 4.9 %copy-start.6 = (bf16[384,256]{1,0:T(8,128)(2,1)S(1)}, bf16[384,256]{1,0:T(8,128)(2,1)}, u32[]{:S(2)}) copy-start(bf16[384,256]{1,0:T(8,128)(2,1)} %constant.20.clone.gather_ref) | copy-start | bytes 589828
  59.0 8.4 %collective-permute-start = (bf16[128,8,128]{2,1,0:T(8,128)(2,1)S(1)}, bf16[128,8,128]{2,1,0:T(8,128)(2,1)S(1)}, u32[]{:S(2)}, u32[]{:S(2)}) collective-permute-start(bf16[128,8,128]{2,1,0:T(8,128)(2,1)S(1)} %bitcast.24), channel_id=1, source_target_pairs={{0,128},{128,0},{1,129},{129,1},{2,130},{130,2},{3,131},{131,3},{4... | collective-permute-start | bytes 786440 | tf_op jit(solution)/shard_map/ppermute | solution.py:245
  71.4 7.1 %copy-start.7 = (bf16[2,128,128]{2,1,0:T(8,128)(2,1)S(1)}, bf16[2,128,128]{2,1,0:T(8,128)(2,1)}, u32[]{:S(2)}) copy-start(bf16[2,128,128]{2,1,0:T(8,128)(2,1)} %param.9) | copy-start | bytes 196612
  71.4 30.6 %copy-start.1 = (bf16[2,128,640]{2,1,0:T(8,128)(2,1)S(1)}, bf16[2,128,640]{2,1,0:T(8,128)(2,1)}, u32[]{:S(2)}) copy-start(bf16[2,128,640]{2,1,0:T(8,128)(2,1)} %w_ref.3) | copy-start | bytes 983044
  71.4 30.6 %all-to-all-start.1 = ((bf16[128,8,128]{2,1,0:T(8,128)(2,1)}), bf16[128,8,128]{2,1,0:T(8,128)(2,1)S(1)}, u32[]{:S(2)}, u32[]{:S(2)}) async-start(bf16[128,8,128]{2,1,0:T(8,128)(2,1)} %bitcast.6), calls=%async_computation.1 | async-start | bytes 524288 | tf_op jit(solution)/shard_map/all_to_all | solution.py:256
  104.4 39.5 %all-to-all-start.2 = ((bf16[128,7,2,128]{3,2,1,0:T(2,128)(2,1)}), bf16[128,7,2,128]{3,2,1,0:T(2,128)(2,1)S(1)}, u32[]{:S(2)}, u32[]{:S(2)}) async-start(bf16[128,7,2,128]{3,2,1,0:T(2,128)(2,1)} %get-tuple-element.21), calls=%async_computation.2 | async-start | bytes 917504 | tf_op jit(solution)/shard_map/all_to_all | solution.py:260
  144.3 4.8 %copy-start.3 = (bf16[2,512,384]{2,1,0:T(8,128)(2,1)S(1)}, bf16[2,512,384]{2,1,0:T(8,128)(2,1)}, u32[]{:S(2)}) copy-start(bf16[2,512,384]{2,1,0:T(8,128)(2,1)} %constant.21.clone.rows_ref) | copy-start | bytes 2359300
  146.6 2.5 %copy-start.4 = (bf16[384,256]{1,0:T(8,128)(2,1)S(1)}, bf16[384,256]{1,0:T(8,128)(2,1)}, u32[]{:S(2)}) copy-start(bf16[384,256]{1,0:T(8,128)(2,1)} %constant.19.clone.gather_ref) | copy-start | bytes 589828
  150.9 10.2 %collective-permute-start.1 = (bf16[16,64,128]{2,1,0:T(8,128)(2,1)S(1)}, bf16[16,64,128]{2,1,0:T(8,128)(2,1)S(1)}, u32[]{:S(2)}, u32[]{:S(2)}) collective-permute-start(bf16[16,64,128]{2,1,0:T(8,128)(2,1)S(1)} %get-tuple-element.24), channel_id=1, source_target_pairs={{0,128},{128,0},{1,129},{129,1},{2,130},{130,2},{3,131},{131,3},{4... | collective-permute-start | bytes 786440 | tf_op jit(solution)/shard_map/ppermute | solution.py:268

commit v5 on v4

--- a/solution.py
+++ b/solution.py
@@ -74,7 +74,8 @@
 
 
 def updated(x_ref, p_ref, gate_ref, w_ref, step):
-    product = jnp.swapaxes(x_ref[...].astype(F32), 0, 1)
+    owners = [((zl * 4 + x) * 2 + y1) * 4 + zh for x in range(4) for zl in range(4) for zh in range(4) for y1 in range(2)]
+    product = jnp.swapaxes(jnp.stack([x_ref[owner].astype(F32) for owner in owners], axis=0), 0, 1)
     blocks = []
     for t in range(T):
         normed = layer_norm(product[t + 1], 0).astype(BF16)
@@ -83,13 +84,18 @@
     return blocks
 
 
-def first_kernel(p_ref, w_ref, msg_ref, gate_ref, flat_ref):
+def first_kernel(p_hbm, w_hbm, msg_ref, gate_ref, flat_ref, p_ref, w_ref, done):
+    copies = [pltpu.make_async_copy(p_hbm, p_ref, done.at[0]), pltpu.make_async_copy(w_hbm, w_ref, done.at[1])]
+    for copy in copies:
+        copy.start()
     blocks = []
+    copies[0].wait()
     for t in range(T):
         rows = [p_ref[U * t + u].astype(F32) for u in range(U)]
         block = jnp.concatenate(rows + [jnp.zeros((2, C), F32)], axis=0)
         flat_ref[t] = block.astype(BF16)
         blocks.append(block)
+    copies[1].wait()
     emit_edges(blocks, w_ref, 0, msg_ref, gate_ref)
 
 
@@ -114,6 +120,14 @@
         for first in range(0, 4, count):
             wide.append(jnp.concatenate([get(4 * x + zl) for x in range(first, first + count)], axis=1))
     return dot(jnp.concatenate(wide, axis=0), table, 1, 0)
+
+
+def right_of(ref, at):
+    return ref[at, :, :4].reshape(64, 128)
+
+
+def left_of(ref, at):
+    return ref[at, :, 3:].reshape(64, 128)
 
 
 def fill_right(right, core, get, table):
@@ -136,9 +150,9 @@
     return jnp.swapaxes(packed.reshape(4, 4, 2, 8, 256), 1, 2).reshape(256, 256).astype(BF16)
 
 
-def outgoing_near_kernel(left_ref, near_ref, spread_ref, gather_ref, left, out_ref, right):
+def outgoing_near_kernel(msg_ref, near_ref, spread_ref, gather_ref, left, out_ref, right):
     table = spread_ref[...]
-    part = fan(lambda at: left_ref[at], 2, table).astype(BF16)
+    part = fan(lambda at: left_of(msg_ref, at), 2, table).astype(BF16)
     for pair in range(8):
         for u in range(U):
             left[64 * u : 64 * (u + 1), 128 * pair : 128 * (pair + 1)] = part[
@@ -184,27 +198,44 @@
             out_ref[2 * pair + x] = packed[64 * pair : 64 * (pair + 1), 128 * x : 128 * (x + 1)]
 
 
+def incoming_part(mine, msg_ref, spread_ref, rows_ref, put_left, put_right):
+    lefts = pltpu.roll(fan(lambda m: left_of(msg_ref, m), 4, rows_ref[mine]).reshape(32, 8, U * 128), 7, 1)
+    at_t = lax.broadcasted_iota(jnp.int32, lefts.shape, 1)
+    lefts = jnp.where(at_t < T, lefts, 0).reshape(256, U * 128).astype(BF16)
+    rights = fan(lambda m: right_of(msg_ref, m), 2, spread_ref[...]).astype(BF16)
+    for u in range(U):
+        for zl in range(4):
+            put_left(u, zl, lefts[64 * zl : 64 * (zl + 1), 128 * u : 128 * (u + 1)])
+        for pair in range(8):
+            put_right(u, pair, rights[64 * pair : 64 * (pair + 1), 128 * u : 128 * (u + 1)])
+
+
+def incoming_own_kernel(core_ref, msg_ref, spread_ref, rows_ref, left, right):
+    def put_left(u, zl, part):
+        y1, y = divmod(zl, 2)
+        left[y, 64 * u : 64 * (u + 1), 128 * y1 : 128 * (y1 + 1)] = part
+
+    def put_right(u, pair, part):
+        right[64 * u : 64 * (u + 1), 128 * pair : 128 * (pair + 1)] = part
+
+    incoming_part(core_ref[0], msg_ref, spread_ref, rows_ref, put_left, put_right)
+
+
 def incoming_far_kernel(
-    at_ref, left_ref, right_ref, spread_ref, rows_ref, gather_ref, far_ref, left_near, right, left
+    y0_ref, core_ref, msg_ref, left_own, right_own, spread_ref, rows_ref, gather_ref, far_ref, left_near, right, left
 ):
-    y0, mine = at_ref[0], at_ref[1]
-    table, rows = spread_ref[...], rows_ref[mine]
-    for core in range(2):
-        lefts = pltpu.roll(fan(lambda m: left_ref[core, m], 4, rows).reshape(32, 8, U * 128), 7, 1)
-        at_t = lax.broadcasted_iota(jnp.int32, lefts.shape, 1)
-        lefts = jnp.where(at_t < T, lefts, 0).reshape(256, U * 128).astype(BF16)
-        rights = fan(lambda m: right_ref[core, m], 2, table).astype(BF16)
-        for u in range(U):
-            at = 192 * core + 64 * u
-            for zl in range(4):
-                y1, y = divmod(zl, 2)
-                left[y, at : at + 64, 128 * y1 : 128 * (y1 + 1)] = lefts[64 * zl : 64 * (zl + 1), 128 * u : 128 * (u + 1)]
-            for pair in range(8):
-                right[at : at + 64, 128 * pair : 128 * (pair + 1)] = rights[
-                    64 * pair : 64 * (pair + 1), 128 * u : 128 * (u + 1)
-                ]
-    left_near[...] = left[y0]
-    incoming_products(left[1 - y0], right[...], gather_ref, far_ref)
+    def put_left(u, zl, part):
+        y1, y = divmod(zl, 2)
+        left[y, 192 + 64 * u : 192 + 64 * (u + 1), 128 * y1 : 128 * (y1 + 1)] = part
+
+    def put_right(u, pair, part):
+        right[192 + 64 * u : 192 + 64 * (u + 1), 128 * pair : 128 * (pair + 1)] = part
+
+    incoming_part(core_ref[0], msg_ref, spread_ref, rows_ref, put_left, put_right)
+    left[:, :192] = left_own[...]
+    right[:192] = right_own[...]
+    left_near[...] = left[y0_ref[0]]
+    incoming_products(left[1 - y0_ref[0]], right[...], gather_ref, far_ref)
 
 
 def incoming_near_kernel(left, right, gather_ref, near_ref):
@@ -215,15 +246,19 @@
 SMEM = pl.BlockSpec(memory_space=pltpu.SMEM)
 
 
-def call(kernel, outs, args, name, scratch=(), scalars=0):
+HBM = pl.BlockSpec(memory_space=pl.ANY)
+
+
+def call(kernel, outs, args, name, scratch=(), scalars=0, fetched=0):
     moved = sum(a.size * a.dtype.itemsize for a in args) + sum(2 * int(np.prod(s)) for s in outs)
     return pl.pallas_call(
         kernel,
         out_shape=[jax.ShapeDtypeStruct(s, BF16) for s in outs],
-        in_specs=[SMEM] * scalars + [VMEM] * (len(args) - scalars),
+        in_specs=[SMEM] * scalars + [VMEM] * (len(args) - scalars - fetched) + [HBM] * fetched,
         out_specs=[VMEM] * len(outs),
-        scratch_shapes=[pltpu.VMEM(s, BF16) for s in scratch],
-        compiler_params=pltpu.CompilerParams(vmem_limit_bytes=48 * 1024 * 1024),
+        scratch_shapes=[pltpu.VMEM(s, BF16) for s in scratch]
+        + ([pltpu.SemaphoreType.DMA((fetched,))] if fetched else []),
+        compiler_params=pltpu.CompilerParams(vmem_limit_bytes=(60 if fetched else 48) * 1024 * 1024),
         cost_estimate=pl.CostEstimate(flops=2_000_000_000, bytes_accessed=moved, transcendentals=0),
         name=name,
     )(*args)
@@ -236,21 +271,23 @@
 def shards(pair_rep, in_weights, out_weights):
     table, back = jnp.asarray(spread(), BF16), jnp.asarray(spread().T, BF16)
     gather = jnp.asarray(gather_rows(), BF16)
-    out_weights = out_weights.reshape(2, 4, 4, 4, 2, C).transpose(0, 2, 1, 4, 3, 5).reshape(2, C, C)
-    y0, core = lax.axis_index("y0").astype(jnp.int32), lax.axis_index("core").astype(jnp.int32)
-
-    msg, gate, flat = call(first_kernel, [MSG, FLAT, FLAT], (pair_rep, in_weights), "edges")
+    y0, core = (lax.axis_index(name).astype(jnp.int32)[None] for name in ("y0", "core"))
+
+    msg, gate, flat = call(
+        first_kernel, [MSG, FLAT, FLAT], (pair_rep, in_weights), "edges",
+        scratch=[pair_rep.shape, in_weights.shape], fetched=2,
+    )
     msg = lax.all_to_all(msg, TO_CHANNELS, 0, 0, tiled=True)
     right = msg[:, :4].reshape(C, 8, 128)
     far = lax.ppermute(right, "y0", SWAP)
     near = lax.all_gather(right, "core", axis=0, tiled=True).reshape(2, 16, 64, 128)
     left, near = call(
-        outgoing_near_kernel, [(192, 1024), (8, 64, 128)], (msg[:, 3:].reshape(16, 64, 128), near, table, gather),
+        outgoing_near_kernel, [(192, 1024), (8, 64, 128)], (msg.reshape(16, 8, T, 2, 128), near, table, gather),
         "outgoing_near", scratch=[(512, 1024)],
     )
     far = lax.all_gather(far, "core", axis=0, tiled=True).reshape(2, 16, 64, 128)
     (product,) = call(
-        outgoing_far_kernel, [(16, 64, 128)], (y0[None], left, near, far, table, gather),
+        outgoing_far_kernel, [(16, 64, 128)], (y0, left, near, far, table, gather),
         "outgoing_far", scratch=[(512, 1024)], scalars=1,
     )
     product = lax.all_to_all(product.reshape(128, 8, 128), TO_POSITIONS, 0, 0, tiled=True)
@@ -258,12 +295,16 @@
         middle_kernel, [MSG, FLAT, FLAT], (product, flat, gate, out_weights, in_weights), "update_edges"
     )
     msg = lax.all_to_all(msg, TO_CHANNELS, 0, 0, tiled=True)
-    left = lax.all_gather(msg[:, 3:].reshape(C, 8, 128), "core", axis=0, tiled=True).reshape(2, 16, 64, 128)
-    right = lax.all_gather(msg[:, :4].reshape(C, 8, 128), "core", axis=0, tiled=True).reshape(2, 16, 64, 128)
+    rows = jnp.asarray(spread_rows(), BF16)
+    other = lax.ppermute(msg, "core", SWAP)
+    left, right = call(
+        incoming_own_kernel, [(2, 192, 256), (192, 1024)], (core, msg.reshape(16, 8, T, 2, 128), table, rows),
+        "incoming_own", scalars=1,
+    )
     far, left, right = call(
         incoming_far_kernel, [(16, 64, 128), (384, 256), (384, 1024)],
-        (jnp.stack([y0, core]), left, right, table, jnp.asarray(spread_rows(), BF16), back),
-        "incoming_far", scratch=[(2, 384, 256)], scalars=1,
+        (y0, core, other.reshape(16, 8, T, 2, 128), left, right, table, rows, back),
+        "incoming_far", scratch=[(2, 384, 256)], scalars=2,
     )
     far = lax.ppermute(far, "y0", SWAP)
     (near,) = call(incoming_near_kernel, [(16, 64, 128)], (left, right, back), "incoming_near")

time: 192 us -> 187 us (0.974)
  blocking collectives: 37.7 us -> 103 us
  waiting for transfers between devices: 97.9 us -> 43.1 us
  starting transfers between devices: 41 us -> 29 us
  local copies, waits for them, and re-layouts: 2.7 us -> 0.23 us
    all_to_all x0 -> x1, blocking collectives: none -> 39.4 us  [shards(): msg = lax.all_to_all(msg, TO_CHANNELS, 0, 0, tiled=True)]
    all_to_all x2 -> x1, waiting for transfers between devices: 65.2 us -> 32.8 us  [shards(): msg = lax.all_to_all(msg, TO_CHANNELS, 0, 0, tiled=True)]
    all_to_all x1 -> x2, blocking collectives: 28.6 us -> 59 us  [shards(): lax.all_to_all(product.reshape(128, 8, 128), TO_POSITIONS, 0, 0, tiled=True)]
    all_to_all x1 -> x0, waiting for transfers between devices: 23.5 us -> none  [shards(): lax.all_to_all(product.reshape(128, 8, 128), TO_POSITIONS, 0, 0, tiled=True)]
    all_to_all x1 -> x0, starting transfers between devices: 7.09 us -> none  [shards(): lax.all_to_all(product.reshape(128, 8, 128), TO_POSITIONS, 0, 0, tiled=True)]
    all_to_all x2 -> x1, starting transfers between devices: 28.7 us -> 21.6 us  [shards(): msg = lax.all_to_all(msg, TO_CHANNELS, 0, 0, tiled=True)]
    all_gather x2 -> x0, blocking collectives: 4.79 us -> none  [the longest x1 2.48 us: shards(): lax.all_gather(msg[:, :4].reshape(C, 8, 128), 'core', axis=0, tiled=True)]
    ppermute x0 -> x1, starting transfers between devices: none -> 2.09 us  [shards(): other = lax.ppermute(msg, 'core', SWAP)]
  transfers between devices with their start and end apart: 5 -> 4, of which waited for: 5 -> 4; matrix products, arithmetic and copies ran while one was open for 0% -> 0% of each run, Pallas kernels for 1% -> 1%
where the time goes in v5:
time: 187 us; the launch traced here: 186 us
  blocking collectives  103 us (55%)
  waiting for transfers between devices  43.1 us (23%)
  starting transfers between devices  29 us (16%)
  Pallas kernels  10.8 us (6%)
    all_to_all x2, blocking collectives, shards(): lax.all_to_all(product.reshape(128, 8, 128), TO_POSITIONS, 0, 0, tiled=True)  59 us
    all_to_all x1, blocking collectives, shards(): msg = lax.all_to_all(msg, TO_CHANNELS, 0, 0, tiled=True)  39.4 us
    all_to_all x1, waiting for transfers between devices, shards(): msg = lax.all_to_all(msg, TO_CHANNELS, 0, 0, tiled=True)  32.8 us
    all_to_all x1, starting transfers between devices, shards(): msg = lax.all_to_all(msg, TO_CHANNELS, 0, 0, tiled=True)  21.6 us
    pallas_call x8, Pallas kernels, call(): pl.pallas_call(kernel, out_shape=[jax.ShapeDtypeStruct(s, BF16) for s in...  10.8 us
    ppermute x1, waiting for transfers between devices, shards(): far = lax.ppermute(far, 'y0', SWAP)  7.01 us
  transfers between devices with their start and end apart: 4, of which 4 were waited for; matrix products, arithmetic and copies ran while one was open for 0% of the time, Pallas kernels for 1%

profile of v5, /device:TPU:32, one launch (start us, length us, event | category | flops | bytes accessed | tf_op | source)
XLA Modules:
  0.0 186.2 jit_solution(5277658062089331604)
XLA Ops:
  0.0 3.5 %edges.1 = (bf16[128,7,2,128]{3,2,1,0:T(2,128)(2,1)}, bf16[7,128,128]{2,1,0:T(8,128)(2,1)}, bf16[7,128,128]{2,1,0:T(8,128)(2,1)}) custom-call(bf16[21,42,128]{2,1,0:T(8,128)(2,1)} %p_hbm.1, bf16[2,128,640]{2,1,0:T(8,128)(2,1)} %w_ref.1), custom_call_target="tpu_custom_call" | custom-call | flops 2000000000 | bytes 1470976 | tf_op jit(solution)/shard_map/edges/pallas_call | solution.py:254
  3.5 21.6 %all-to-all-start = ((bf16[128,7,2,128]{3,2,1,0:T(2,128)(2,1)}), bf16[128,7,2,128]{3,2,1,0:T(2,128)(2,1)S(1)}, u32[]{:S(2)}, u32[]{:S(2)}) async-start(bf16[128,7,2,128]{3,2,1,0:T(2,128)(2,1)} %get-tuple-element.18), calls=%async_computation | async-start | bytes 917504 | tf_op jit(solution)/shard_map/all_to_all | solution.py:280
  25.2 32.8 %all-to-all-done = bf16[128,7,2,128]{3,2,1,0:T(2,128)(2,1)S(1)} async-done(((bf16[128,7,2,128]{3,2,1,0:T(2,128)(2,1)}), bf16[128,7,2,128]{3,2,1,0:T(2,128)(2,1)S(1)}, u32[]{:S(2)}, u32[]{:S(2)}) %all-to-all-start) | async-done | bytes 458784 | tf_op jit(solution)/shard_map/all_to_all | solution.py:280
  58.0 0.2 slice.4
  58.1 0.0 copy-start.4
  58.2 0.0 copy-start.5
  58.2 2.7 %collective-permute-start = (bf16[128,8,128]{2,1,0:T(8,128)(2,1)S(1)}, bf16[128,8,128]{2,1,0:T(8,128)(2,1)S(1)}, u32[]{:S(2)}, u32[]{:S(2)}) collective-permute-start(bf16[128,8,128]{2,1,0:T(8,128)(2,1)S(1)} %bitcast.16), channel_id=1, source_target_pairs={{0,128},{128,0},{1,129},{129,1},{2,130},{130,2},{3,131},{131,3},{4... | collective-permute-start | bytes 786440 | tf_op jit(solution)/shard_map/ppermute | solution.py:282
  60.9 2.2 %all_gather.6 = bf16[256,8,128]{2,1,0:T(8,128)(2,1)S(1)} all-gather(bf16[128,8,128]{2,1,0:T(8,128)(2,1)S(1)} %bitcast.17), channel_id=1, replica_groups=mesh['y1'=2,'y0'=2,'zh'=4,'core'=2,'zl'=4,'x'=4] {'core'}, dimensions={0}, use_global_device_ids=true | all-gather | bytes 786432 | tf_op jit(solution)/shard_map/all_gather | solution.py:283
  63.1 0.0 copy-done.4
  63.1 0.0 copy-done.5
  63.1 1.3 outgoing_near.1
  64.4 2.2 %collective-permute-done = bf16[128,8,128]{2,1,0:T(8,128)(2,1)S(1)} collective-permute-done((bf16[128,8,128]{2,1,0:T(8,128)(2,1)S(1)}, bf16[128,8,128]{2,1,0:T(8,128)(2,1)S(1)}, u32[]{:S(2)}, u32[]{:S(2)}) %collective-permute-start) | collective-permute-done | bytes 262176 | tf_op jit(solution)/shard_map/ppermute | solution.py:282
  66.6 2.2 %all_gather.7 = bf16[256,8,128]{2,1,0:T(8,128)(2,1)S(1)} all-gather(bf16[128,8,128]{2,1,0:T(8,128)(2,1)S(1)} %collective-permute-done), channel_id=1, replica_groups=mesh['y1'=2,'y0'=2,'zh'=4,'core'=2,'zl'=4,'x'=4] {'core'}, dimensions={0}, use_global_device_ids=true | all-gather | bytes 786432 | tf_op jit(solution)/shard_map/all_gather | solution.py:288
  68.7 0.0 copy-start.6
  68.7 0.0 copy-start.7
  68.7 1.1 outgoing_far.1
  69.9 0.0 copy-start
  69.9 0.0 copy-start.1
  69.9 30.4 %all_to_all.20.x_ref = bf16[128,8,128]{2,1,0:T(8,128)(2,1)S(1)} all-to-all(bf16[128,8,128]{2,1,0:T(8,128)(2,1)S(1)} %bitcast.14), channel_id=1, replica_groups=mesh['y1'=2,'y0'=2,'zh'=4,'core'=2,'zl'=4,'x'=4] {'zl','x','y1','zh'}, dimensions={0} | all-to-all | bytes 524288 | tf_op jit(solution)/shard_map/all_to_all | solution.py:293
  100.3 0.0 copy-done.6
  100.3 0.0 copy-done.7
  100.3 0.0 copy-done
  100.3 0.0 copy-done.1
  100.3 1.6 update_edges.1
  102.0 0.0 copy-start.2
  102.0 39.4 %all_to_all.21 = bf16[128,7,2,128]{3,2,1,0:T(2,128)(2,1)S(1)} all-to-all(bf16[128,7,2,128]{3,2,1,0:T(2,128)(2,1)S(1)} %get-tuple-element.23), channel_id=1, replica_groups=mesh['y1'=2,'y0'=2,'zh'=4,'core'=2,'zl'=4,'x'=4] {'x','zl','zh','y1'}, dimensions={0} | all-to-all | bytes 917504 | tf_op jit(solution)/shard_map/all_to_all | solution.py:297
  141.4 2.1 %collective-permute-start.1 = (bf16[128,7,2,128]{3,2,1,0:T(2,128)(2,1)S(1)}, bf16[128,7,2,128]{3,2,1,0:T(2,128)(2,1)S(1)}, u32[]{:S(2)}, u32[]{:S(2)}) collective-permute-start(bf16[128,7,2,128]{3,2,1,0:T(2,128)(2,1)S(1)} %all_to_all.21), channel_id=1, source_target_pairs={{0,16},{16,0},{1,17},{17,1},{2,18},{18,2},{3,19},{19,3},{4,20},{20... | collective-permute-start | bytes 1376264 | tf_op jit(solution)/shard_map/ppermute | solution.py:299
  143.5 0.0 copy-done.2
  143.5 0.0 copy-start.3
  143.5 0.5 incoming_own.1
  144.0 1.1 collective-permute-done.1
  145.1 0.0 copy-done.3
  145.1 1.0 incoming_far.1
  146.1 2.6 %collective-permute-start.2 = (bf16[16,64,128]{2,1,0:T(8,128)(2,1)S(1)}, bf16[16,64,128]{2,1,0:T(8,128)(2,1)S(1)}, u32[]{:S(2)}, u32[]{:S(2)}) collective-permute-start(bf16[16,64,128]{2,1,0:T(8,128)(2,1)S(1)} %get-tuple-element.28), channel_id=1, source_target_pairs={{0,128},{128,0},{1,129},{129,1},{2,130},{130,2},{3,131},{131,3},{4... | collective-permute-start | bytes 786440 | tf_op jit(solution)/shard_map/ppermute | solution.py:309
  148.7 0.6 incoming_near.1
  149.3 7.0 %collective-permute-done.2 = bf16[16,64,128]{2,1,0:T(8,128)(2,1)S(1)} collective-permute-done((bf16[16,64,128]{2,1,0:T(8,128)(2,1)S(1)}, bf16[16,64,128]{2,1,0:T(8,128)(2,1)S(1)}, u32[]{:S(2)}, u32[]{:S(2)}) %collective-permute-start.2) | collective-permute-done | bytes 262176 | tf_op jit(solution)/shard_map/ppermute | solution.py:309
  156.4 0.1 add_convert_fusion
  156.4 28.6 %all_to_all.22.x_ref = bf16[128,8,128]{2,1,0:T(8,128)(2,1)S(1)} all-to-all(bf16[128,8,128]{2,1,0:T(8,128)(2,1)S(1)} %bitcast.18), channel_id=1, replica_groups=mesh['y1'=2,'y0'=2,'zh'=4,'core'=2,'zl'=4,'x'=4] {'zl','x','y1','zh'}, dimensions={0} | all-to-all | bytes 524288 | tf_op jit(solution)/shard_map/all_to_all | solution.py:312
  185.0 1.2 update.1
Async XLA Ops:
  3.5 54.5 %all-to-all-start = ((bf16[128,7,2,128]{3,2,1,0:T(2,128)(2,1)}), bf16[128,7,2,128]{3,2,1,0:T(2,128)(2,1)S(1)}, u32[]{:S(2)}, u32[]{:S(2)}) async-start(bf16[128,7,2,128]{3,2,1,0:T(2,128)(2,1)} %get-tuple-element.18), calls=%async_computation | async-start | bytes 917504 | tf_op jit(solution)/shard_map/all_to_all | solution.py:280
  58.1 4.9 %copy-start.4 = (bf16[256,384]{1,0:T(8,128)(2,1)S(1)}, bf16[256,384]{1,0:T(8,128)(2,1)}, u32[]{:S(2)}) copy-start(bf16[256,384]{1,0:T(8,128)(2,1)} %constant.18.clone.spread_ref) | copy-start | bytes 589828
  58.2 4.9 %copy-start.5 = (bf16[384,256]{1,0:T(8,128)(2,1)S(1)}, bf16[384,256]{1,0:T(8,128)(2,1)}, u32[]{:S(2)}) copy-start(bf16[384,256]{1,0:T(8,128)(2,1)} %constant.20.clone.gather_ref) | copy-start | bytes 589828
  58.2 8.4 %collective-permute-start = (bf16[128,8,128]{2,1,0:T(8,128)(2,1)S(1)}, bf16[128,8,128]{2,1,0:T(8,128)(2,1)S(1)}, u32[]{:S(2)}, u32[]{:S(2)}) collective-permute-start(bf16[128,8,128]{2,1,0:T(8,128)(2,1)S(1)} %bitcast.16), channel_id=1, source_target_pairs={{0,128},{128,0},{1,129},{129,1},{2,130},{130,2},{3,131},{131,3},{4... | collective-permute-start | bytes 786440 | tf_op jit(solution)/shard_map/ppermute | solution.py:282
  68.7 31.6 %copy-start.6 = (bf16[7,128,128]{2,1,0:T(8,128)(2,1)S(1)}, bf16[7,128,128]{2,1,0:T(8,128)(2,1)}, u32[]{:S(2)}) copy-start(bf16[7,128,128]{2,1,0:T(8,128)(2,1)} %get-tuple-element.22.gate_ref) | copy-start | bytes 688132
  68.7 31.6 %copy-start.7 = (bf16[7,128,128]{2,1,0:T(8,128)(2,1)S(1)}, bf16[7,128,128]{2,1,0:T(8,128)(2,1)}, u32[]{:S(2)}) copy-start(bf16[7,128,128]{2,1,0:T(8,128)(2,1)} %get-tuple-element.21.p_ref) | copy-start | bytes 688132
  69.9 30.4 %copy-start = (bf16[2,128,640]{2,1,0:T(8,128)(2,1)S(1)}, bf16[2,128,640]{2,1,0:T(8,128)(2,1)}, u32[]{:S(2)}) copy-start(bf16[2,128,640]{2,1,0:T(8,128)(2,1)} %w_ref.1) | copy-start | bytes 983044
  69.9 30.4 %copy-start.1 = (bf16[2,128,128]{2,1,0:T(8,128)(2,1)S(1)}, bf16[2,128,128]{2,1,0:T(8,128)(2,1)}, u32[]{:S(2)}) copy-start(bf16[2,128,128]{2,1,0:T(8,128)(2,1)} %wo_ref.3) | copy-start | bytes 196612
  102.0 41.6 %copy-start.2 = (bf16[2,512,384]{2,1,0:T(8,128)(2,1)S(1)}, bf16[2,512,384]{2,1,0:T(8,128)(2,1)}, u32[]{:S(2)}) copy-start(bf16[2,512,384]{2,1,0:T(8,128)(2,1)} %constant.21.clone.rows_ref) | copy-start | bytes 2359300
  141.4 3.7 %collective-permute-start.1 = (bf16[128,7,2,128]{3,2,1,0:T(2,128)(2,1)S(1)}, bf16[128,7,2,128]{3,2,1,0:T(2,128)(2,1)S(1)}, u32[]{:S(2)}, u32[]{:S(2)}) collective-permute-start(bf16[128,7,2,128]{3,2,1,0:T(2,128)(2,1)S(1)} %all_to_all.21), channel_id=1, source_target_pairs={{0,16},{16,0},{1,17},{17,1},{2,18},{18,2},{3,19},{19,3},{4,20},{20... | collective-permute-start | bytes 1376264 | tf_op jit(solution)/shard_map/ppermute | solution.py:299
  143.5 1.6 copy-start.3
  146.1 10.2 %collective-permute-start.2 = (bf16[16,64,128]{2,1,0:T(8,128)(2,1)S(1)}, bf16[16,64,128]{2,1,0:T(8,128)(2,1)S(1)}, u32[]{:S(2)}, u32[]{:S(2)}) collective-permute-start(bf16[16,64,128]{2,1,0:T(8,128)(2,1)S(1)} %get-tuple-element.28), channel_id=1, source_target_pairs={{0,128},{128,0},{1,129},{129,1},{2,130},{130,2},{3,131},{131,3},{4... | collective-permute-start | bytes 786440 | tf_op jit(solution)/shard_map/ppermute | solution.py:309

commit v6 on v5

--- a/solution.py
+++ b/solution.py
@@ -84,7 +84,7 @@
     return blocks
 
 
-def first_kernel(p_hbm, w_hbm, msg_ref, gate_ref, flat_ref, p_ref, w_ref, done):
+def first_kernel(y0_ref, core_ref, p_hbm, w_hbm, msg_ref, gate_ref, flat_ref, p_ref, w_ref, done):
     copies = [pltpu.make_async_copy(p_hbm, p_ref, done.at[0]), pltpu.make_async_copy(w_hbm, w_ref, done.at[1])]
     for copy in copies:
         copy.start()
@@ -183,7 +183,7 @@
         out_ref[(2 * y1 + 1 - y0) * 4 + zh] = packed[64 * high : 64 * (high + 1), 128 * low : 128 * (low + 1)]
 
 
-def incoming_products(left, right, gather_ref, out_ref):
+def incoming_products(left, right, gather_ref, put):
     product = dot(left, right, 0, 0).astype(BF16)
     wide = []
     for pair in range(8):
@@ -192,10 +192,10 @@
                 product[128 * y1 + 32 * w : 128 * y1 + 32 * (w + 1), 128 * pair : 128 * (pair + 1)] for w in range(U)
             ]
             wide.append(jnp.concatenate(part, axis=1))
-    packed = dot(jnp.concatenate(wide, axis=0), gather_ref[...], 1, 0).astype(BF16)
+    packed = dot(jnp.concatenate(wide, axis=0), gather_ref[...], 1, 0)
     for pair in range(8):
         for x in range(2):
-            out_ref[2 * pair + x] = packed[64 * pair : 64 * (pair + 1), 128 * x : 128 * (x + 1)]
+            put(2 * pair + x, packed[64 * pair : 64 * (pair + 1), 128 * x : 128 * (x + 1)])
 
 
 def incoming_part(mine, msg_ref, spread_ref, rows_ref, put_left, put_right):
@@ -235,11 +235,20 @@
     left[:, :192] = left_own[...]
     right[:192] = right_own[...]
     left_near[...] = left[y0_ref[0]]
-    incoming_products(left[1 - y0_ref[0]], right[...], gather_ref, far_ref)
-
-
-def incoming_near_kernel(left, right, gather_ref, near_ref):
-    incoming_products(left[...], right[...], gather_ref, near_ref)
+
+    def put(at, part):
+        far_ref[at] = part.astype(BF16)
+
+    incoming_products(left[1 - y0_ref[0]], right[...], gather_ref, put)
+
+
+def incoming_near_kernel(y0_ref, left, right, far_ref, gather_ref, out_ref):
+    other = 1 - y0_ref[0]
+
+    def put(at, part):
+        out_ref[at] = (part + far_ref[other, at].astype(F32)).astype(BF16)
+
+    incoming_products(left[...], right[...], gather_ref, put)
 
 
 VMEM = pl.BlockSpec(memory_space=pltpu.VMEM)
@@ -258,7 +267,7 @@
         out_specs=[VMEM] * len(outs),
         scratch_shapes=[pltpu.VMEM(s, BF16) for s in scratch]
         + ([pltpu.SemaphoreType.DMA((fetched,))] if fetched else []),
-        compiler_params=pltpu.CompilerParams(vmem_limit_bytes=(60 if fetched else 48) * 1024 * 1024),
+        compiler_params=pltpu.CompilerParams(vmem_limit_bytes=(56 if fetched else 48) * 1024 * 1024),
         cost_estimate=pl.CostEstimate(flops=2_000_000_000, bytes_accessed=moved, transcendentals=0),
         name=name,
     )(*args)
@@ -274,8 +283,8 @@
     y0, core = (lax.axis_index(name).astype(jnp.int32)[None] for name in ("y0", "core"))
 
     msg, gate, flat = call(
-        first_kernel, [MSG, FLAT, FLAT], (pair_rep, in_weights), "edges",
-        scratch=[pair_rep.shape, in_weights.shape], fetched=2,
+        first_kernel, [MSG, FLAT, FLAT], (y0, core, pair_rep, in_weights), "edges",
+        scratch=[pair_rep.shape, in_weights.shape], scalars=2, fetched=2,
     )
     msg = lax.all_to_all(msg, TO_CHANNELS, 0, 0, tiled=True)
     right = msg[:, :4].reshape(C, 8, 128)
@@ -306,9 +315,10 @@
         (y0, core, other.reshape(16, 8, T, 2, 128), left, right, table, rows, back),
         "incoming_far", scratch=[(2, 384, 256)], scalars=2,
     )
-    far = lax.ppermute(far, "y0", SWAP)
-    (near,) = call(incoming_near_kernel, [(16, 64, 128)], (left, right, back), "incoming_near")
-    product = (near.astype(F32) + far.astype(F32)).astype(BF16)
+    far = lax.all_gather(far.reshape(128, 8, 128), "y0", axis=0, tiled=True).reshape(2, 16, 64, 128)
+    (product,) = call(
+        incoming_near_kernel, [(16, 64, 128)], (y0, left, right, far, back), "incoming_near", scalars=1
+    )
     product = lax.all_to_all(product.reshape(128, 8, 128), TO_POSITIONS, 0, 0, tiled=True)
     (out,) = call(last_kernel, [(ROWS, COLS, C)], (product, flat, gate, out_weights), "update")
     return out

time: 187 us -> 186 us (level)
  blocking collectives: 103 us -> 166 us
  waiting for transfers between devices: 43.1 us -> 3.3 us
  starting transfers between devices: 29 us -> 4.81 us
    all_to_all x1 -> x2, blocking collectives: 39.4 us -> 93.9 us  [shards(): msg = lax.all_to_all(msg, TO_CHANNELS, 0, 0, tiled=True)]
    all_to_all x1 -> x0, waiting for transfers between devices: 32.8 us -> none  [shards(): msg = lax.all_to_all(msg, TO_CHANNELS, 0, 0, tiled=True)]
    all_to_all x1 -> x0, starting transfers between devices: 21.6 us -> none  [shards(): msg = lax.all_to_all(msg, TO_CHANNELS, 0, 0, tiled=True)]
    all_gather x0 -> x1, blocking collectives: none -> 9.02 us  [shards(): lax.all_gather(far.reshape(128, 8, 128), 'y0', axis=0, tiled=True)]
    ppermute x1 -> x0, waiting for transfers between devices: 7.01 us -> none  [shards(): far = lax.ppermute(far, 'y0', SWAP)]
    ppermute x1 -> x0, starting transfers between devices: 2.58 us -> none  [shards(): far = lax.ppermute(far, 'y0', SWAP)]
  transfers between devices with their start and end apart: 4 -> 2, of which waited for: 4 -> 2; matrix products, arithmetic and copies ran while one was open for 0% -> 0% of each run, Pallas kernels for 1% -> 1%
where the time goes in v6:
time: 186 us
  blocking collectives  166 us (89%)
  Pallas kernels  10.8 us (6%)
  starting transfers between devices  4.81 us (3%)
  waiting for transfers between devices  3.3 us (2%)
    all_to_all x2, blocking collectives, shards(): msg = lax.all_to_all(msg, TO_CHANNELS, 0, 0, tiled=True)  93.9 us
    all_to_all x2, blocking collectives, shards(): lax.all_to_all(product.reshape(128, 8, 128), TO_POSITIONS, 0, 0, tiled=True)  59 us
    pallas_call x8, Pallas kernels, call(): pl.pallas_call(kernel, out_shape=[jax.ShapeDtypeStruct(s, BF16) for s in...  10.8 us
    all_gather x1, blocking collectives, shards(): lax.all_gather(far.reshape(128, 8, 128), 'y0', axis=0, tiled=True)  9.02 us
  transfers between devices with their start and end apart: 2, of which 2 were waited for; matrix products, arithmetic and copies ran while one was open for 0% of the time, Pallas kernels for 1%

profile of v6, /device:TPU:32, one launch (start us, length us, event | category | flops | bytes accessed | tf_op | source)
XLA Modules:
  0.0 185.6 jit_solution(10947407335445756882)
XLA Ops:
  0.0 3.5 %edges.1 = (bf16[128,7,2,128]{3,2,1,0:T(2,128)(2,1)}, bf16[7,128,128]{2,1,0:T(8,128)(2,1)}, bf16[7,128,128]{2,1,0:T(8,128)(2,1)}) custom-call(s32[1]{0:T(128)} %bitcast.y0_ref, s32[1]{0:T(128)} %bitcast.1.core_ref, bf16[21,42,128]{2,1,0:T(8,128)(2,1)} %p_hbm.1, bf16[2,128,640]{2,1,0:T(8,128)(2,1)} %w_ref.1), custom_call_target="tpu_custom_call" | custom-call | flops 2000000000 | bytes 1470984 | tf_op jit(solution)/shard_map/edges/pallas_call | solution.py:263
  3.5 54.5 %all_to_all.20 = bf16[128,7,2,128]{3,2,1,0:T(2,128)(2,1)S(1)} all-to-all(bf16[128,7,2,128]{3,2,1,0:T(2,128)(2,1)} %get-tuple-element.18), channel_id=1, replica_groups=mesh['y1'=2,'y0'=2,'zh'=4,'core'=2,'zl'=4,'x'=4] {'x','zl','zh','y1'}, dimensions={0} | all-to-all | bytes 917504 | tf_op jit(solution)/shard_map/all_to_all | solution.py:289
  58.0 0.2 slice.4
  58.1 0.0 copy-start.4
  58.2 0.0 copy-start.5
  58.2 2.7 %collective-permute-start = (bf16[128,8,128]{2,1,0:T(8,128)(2,1)S(1)}, bf16[128,8,128]{2,1,0:T(8,128)(2,1)S(1)}, u32[]{:S(2)}, u32[]{:S(2)}) collective-permute-start(bf16[128,8,128]{2,1,0:T(8,128)(2,1)S(1)} %bitcast.21), channel_id=1, source_target_pairs={{0,128},{128,0},{1,129},{129,1},{2,130},{130,2},{3,131},{131,3},{4... | collective-permute-start | bytes 786440 | tf_op jit(solution)/shard_map/ppermute | solution.py:291
  60.9 2.2 %all_gather.9 = bf16[256,8,128]{2,1,0:T(8,128)(2,1)S(1)} all-gather(bf16[128,8,128]{2,1,0:T(8,128)(2,1)S(1)} %bitcast.22), channel_id=1, replica_groups=mesh['y1'=2,'y0'=2,'zh'=4,'core'=2,'zl'=4,'x'=4] {'core'}, dimensions={0}, use_global_device_ids=true | all-gather | bytes 786432 | tf_op jit(solution)/shard_map/all_gather | solution.py:292
  63.1 0.0 copy-done.4
  63.1 0.0 copy-done.5
  63.1 1.3 outgoing_near.1
  64.4 2.2 %collective-permute-done = bf16[128,8,128]{2,1,0:T(8,128)(2,1)S(1)} collective-permute-done((bf16[128,8,128]{2,1,0:T(8,128)(2,1)S(1)}, bf16[128,8,128]{2,1,0:T(8,128)(2,1)S(1)}, u32[]{:S(2)}, u32[]{:S(2)}) %collective-permute-start) | collective-permute-done | bytes 262176 | tf_op jit(solution)/shard_map/ppermute | solution.py:291
  66.6 2.2 %all_gather.10 = bf16[256,8,128]{2,1,0:T(8,128)(2,1)S(1)} all-gather(bf16[128,8,128]{2,1,0:T(8,128)(2,1)S(1)} %collective-permute-done), channel_id=1, replica_groups=mesh['y1'=2,'y0'=2,'zh'=4,'core'=2,'zl'=4,'x'=4] {'core'}, dimensions={0}, use_global_device_ids=true | all-gather | bytes 786432 | tf_op jit(solution)/shard_map/all_gather | solution.py:297
  68.7 0.0 copy-start.6
  68.7 0.0 copy-start.7
  68.7 1.1 outgoing_far.1
  69.9 0.0 copy-start
  69.9 0.0 copy-start.1
  69.9 30.4 %all_to_all.21.x_ref = bf16[128,8,128]{2,1,0:T(8,128)(2,1)S(1)} all-to-all(bf16[128,8,128]{2,1,0:T(8,128)(2,1)S(1)} %bitcast.19), channel_id=1, replica_groups=mesh['y1'=2,'y0'=2,'zh'=4,'core'=2,'zl'=4,'x'=4] {'zl','x','y1','zh'}, dimensions={0} | all-to-all | bytes 524288 | tf_op jit(solution)/shard_map/all_to_all | solution.py:302
  100.3 0.0 copy-done.6
  100.3 0.0 copy-done.7
  100.3 0.0 copy-done
  100.3 0.0 copy-done.1
  100.3 1.6 update_edges.1
  102.0 0.0 copy-start.2
  102.0 39.4 %all_to_all.22 = bf16[128,7,2,128]{3,2,1,0:T(2,128)(2,1)S(1)} all-to-all(bf16[128,7,2,128]{3,2,1,0:T(2,128)(2,1)S(1)} %get-tuple-element.23), channel_id=1, replica_groups=mesh['y1'=2,'y0'=2,'zh'=4,'core'=2,'zl'=4,'x'=4] {'x','zl','zh','y1'}, dimensions={0} | all-to-all | bytes 917504 | tf_op jit(solution)/shard_map/all_to_all | solution.py:306
  141.4 2.1 %collective-permute-start.1 = (bf16[128,7,2,128]{3,2,1,0:T(2,128)(2,1)S(1)}, bf16[128,7,2,128]{3,2,1,0:T(2,128)(2,1)S(1)}, u32[]{:S(2)}, u32[]{:S(2)}) collective-permute-start(bf16[128,7,2,128]{3,2,1,0:T(2,128)(2,1)S(1)} %all_to_all.22), channel_id=1, source_target_pairs={{0,16},{16,0},{1,17},{17,1},{2,18},{18,2},{3,19},{19,3},{4,20},{20... | collective-permute-start | bytes 1376264 | tf_op jit(solution)/shard_map/ppermute | solution.py:308
  143.5 0.0 copy-done.2
  143.5 0.0 copy-start.3
  143.5 0.5 incoming_own.1
  144.0 1.1 collective-permute-done.1
  145.1 0.0 copy-done.3
  145.1 1.0 incoming_far.1
  146.1 9.0 %all_gather.11 = bf16[256,8,128]{2,1,0:T(8,128)(2,1)S(1)} all-gather(bf16[128,8,128]{2,1,0:T(8,128)(2,1)S(1)} %bitcast.17), channel_id=1, replica_groups=mesh['y1'=2,'y0'=2,'zh'=4,'core'=2,'zl'=4,'x'=4] {'y0'}, dimensions={0}, use_global_device_ids=true | all-gather | bytes 786432 | tf_op jit(solution)/shard_map/all_gather | solution.py:318
  155.1 0.6 incoming_near.1
  155.8 28.6 %all_to_all.23.x_ref = bf16[128,8,128]{2,1,0:T(8,128)(2,1)S(1)} all-to-all(bf16[128,8,128]{2,1,0:T(8,128)(2,1)S(1)} %bitcast.18), channel_id=1, replica_groups=mesh['y1'=2,'y0'=2,'zh'=4,'core'=2,'zl'=4,'x'=4] {'zl','x','y1','zh'}, dimensions={0} | all-to-all | bytes 524288 | tf_op jit(solution)/shard_map/all_to_all | solution.py:322
  184.4 1.2 update.1
Async XLA Ops:
  58.1 4.9 %copy-start.4 = (bf16[256,384]{1,0:T(8,128)(2,1)S(1)}, bf16[256,384]{1,0:T(8,128)(2,1)}, u32[]{:S(2)}) copy-start(bf16[256,384]{1,0:T(8,128)(2,1)} %constant.18.clone.spread_ref) | copy-start | bytes 589828
  58.2 4.9 %copy-start.5 = (bf16[384,256]{1,0:T(8,128)(2,1)S(1)}, bf16[384,256]{1,0:T(8,128)(2,1)}, u32[]{:S(2)}) copy-start(bf16[384,256]{1,0:T(8,128)(2,1)} %constant.20.clone.gather_ref) | copy-start | bytes 589828
  58.2 8.4 %collective-permute-start = (bf16[128,8,128]{2,1,0:T(8,128)(2,1)S(1)}, bf16[128,8,128]{2,1,0:T(8,128)(2,1)S(1)}, u32[]{:S(2)}, u32[]{:S(2)}) collective-permute-start(bf16[128,8,128]{2,1,0:T(8,128)(2,1)S(1)} %bitcast.21), channel_id=1, source_target_pairs={{0,128},{128,0},{1,129},{129,1},{2,130},{130,2},{3,131},{131,3},{4... | collective-permute-start | bytes 786440 | tf_op jit(solution)/shard_map/ppermute | solution.py:291
  68.7 31.6 %copy-start.6 = (bf16[7,128,128]{2,1,0:T(8,128)(2,1)S(1)}, bf16[7,128,128]{2,1,0:T(8,128)(2,1)}, u32[]{:S(2)}) copy-start(bf16[7,128,128]{2,1,0:T(8,128)(2,1)} %get-tuple-element.22.gate_ref) | copy-start | bytes 688132
  68.7 31.6 %copy-start.7 = (bf16[7,128,128]{2,1,0:T(8,128)(2,1)S(1)}, bf16[7,128,128]{2,1,0:T(8,128)(2,1)}, u32[]{:S(2)}) copy-start(bf16[7,128,128]{2,1,0:T(8,128)(2,1)} %get-tuple-element.21.p_ref) | copy-start | bytes 688132
  69.9 30.4 %copy-start = (bf16[2,128,640]{2,1,0:T(8,128)(2,1)S(1)}, bf16[2,128,640]{2,1,0:T(8,128)(2,1)}, u32[]{:S(2)}) copy-start(bf16[2,128,640]{2,1,0:T(8,128)(2,1)} %w_ref.1) | copy-start | bytes 983044
  69.9 30.4 %copy-start.1 = (bf16[2,128,128]{2,1,0:T(8,128)(2,1)S(1)}, bf16[2,128,128]{2,1,0:T(8,128)(2,1)}, u32[]{:S(2)}) copy-start(bf16[2,128,128]{2,1,0:T(8,128)(2,1)} %wo_ref.3) | copy-start | bytes 196612
  102.0 41.6 %copy-start.2 = (bf16[2,512,384]{2,1,0:T(8,128)(2,1)S(1)}, bf16[2,512,384]{2,1,0:T(8,128)(2,1)}, u32[]{:S(2)}) copy-start(bf16[2,512,384]{2,1,0:T(8,128)(2,1)} %constant.21.clone.rows_ref) | copy-start | bytes 2359300
  141.4 3.7 %collective-permute-start.1 = (bf16[128,7,2,128]{3,2,1,0:T(2,128)(2,1)S(1)}, bf16[128,7,2,128]{3,2,1,0:T(2,128)(2,1)S(1)}, u32[]{:S(2)}, u32[]{:S(2)}) collective-permute-start(bf16[128,7,2,128]{3,2,1,0:T(2,128)(2,1)S(1)} %all_to_all.22), channel_id=1, source_target_pairs={{0,16},{16,0},{1,17},{17,1},{2,18},{18,2},{3,19},{19,3},{4,20},{20... | collective-permute-start | bytes 1376264 | tf_op jit(solution)/shard_map/ppermute | solution.py:308
  143.5 1.6 copy-start.3

commit v7 on v6

--- a/solution.py
+++ b/solution.py
@@ -12,7 +12,7 @@
 ROW = ("y1", "y0", "zh", "core")
 CHAN = ("zl", "x")
 TO_CHANNELS = ("x", "zl", "zh", "y1")
-TO_POSITIONS = ("zl", "x", "y1", "zh")
+TO_POSITIONS = ("zl", "y1", "zh", "x")
 SWAP = [(0, 1), (1, 0)]
 ROWS, COLS, C = 21, 42, 128
 T, U = 7, 3
@@ -74,7 +74,7 @@
 
 
 def updated(x_ref, p_ref, gate_ref, w_ref, step):
-    owners = [((zl * 4 + x) * 2 + y1) * 4 + zh for x in range(4) for zl in range(4) for zh in range(4) for y1 in range(2)]
+    owners = [((zl * 2 + y1) * 4 + zh) * 4 + x for x in range(4) for zl in range(4) for zh in range(4) for y1 in range(2)]
     product = jnp.swapaxes(jnp.stack([x_ref[owner].astype(F32) for owner in owners], axis=0), 0, 1)
     blocks = []
     for t in range(T):
@@ -84,18 +84,13 @@
     return blocks
 
 
-def first_kernel(y0_ref, core_ref, p_hbm, w_hbm, msg_ref, gate_ref, flat_ref, p_ref, w_ref, done):
-    copies = [pltpu.make_async_copy(p_hbm, p_ref, done.at[0]), pltpu.make_async_copy(w_hbm, w_ref, done.at[1])]
-    for copy in copies:
-        copy.start()
+def first_kernel(y0_ref, core_ref, p_ref, w_ref, msg_ref, gate_ref, flat_ref):
     blocks = []
-    copies[0].wait()
     for t in range(T):
         rows = [p_ref[U * t + u].astype(F32) for u in range(U)]
         block = jnp.concatenate(rows + [jnp.zeros((2, C), F32)], axis=0)
         flat_ref[t] = block.astype(BF16)
         blocks.append(block)
-    copies[1].wait()
     emit_edges(blocks, w_ref, 0, msg_ref, gate_ref)
 
 
@@ -146,8 +141,9 @@
         jnp.concatenate([product[64 * u : 64 * (u + 1), 128 * high : 128 * (high + 1)] for u in range(U)], axis=1)
         for high in range(4)
     ]
-    packed = dot(jnp.concatenate(wide, axis=0), gather_ref[...], 1, 0)
-    return jnp.swapaxes(packed.reshape(4, 4, 2, 8, 256), 1, 2).reshape(256, 256).astype(BF16)
+    packed = dot(jnp.concatenate(wide, axis=0), gather_ref[...], 1, 0).reshape(4, 4, 2, 8, 256)
+    packed = jnp.swapaxes(packed, 1, 2).reshape(4, 8, 8, 256).astype(BF16)
+    return [packed[s // 2, :, :, 128 * (s % 2) : 128 * (s % 2 + 1)] for s in range(8)]
 
 
 def outgoing_near_kernel(msg_ref, near_ref, spread_ref, gather_ref, left, out_ref, right):
@@ -164,8 +160,7 @@
         fill_right(right, core, lambda m, core=core: near_ref[core, m], table)
     packed = outgoing_products(left, right, gather_ref)
     for s in range(8):
-        high, low = divmod(s, 2)
-        out_ref[s] = packed[64 * high : 64 * (high + 1), 128 * low : 128 * (low + 1)]
+        out_ref[s] = packed[s]
 
 
 def outgoing_far_kernel(y0_ref, left, near_ref, far_ref, spread_ref, gather_ref, out_ref, right):
@@ -177,10 +172,9 @@
         fill_right(right, core, lambda m, core=core: far_ref[core, m], table)
     packed = outgoing_products(left, right, gather_ref)
     for s in range(8):
-        high, low = divmod(s, 2)
         zh, y1 = divmod(s, 2)
-        out_ref[(2 * y1 + y0) * 4 + zh] = near_ref[s]
-        out_ref[(2 * y1 + 1 - y0) * 4 + zh] = packed[64 * high : 64 * (high + 1), 128 * low : 128 * (low + 1)]
+        out_ref[2 * y1 + y0, :, zh] = near_ref[s]
+        out_ref[2 * y1 + 1 - y0, :, zh] = packed[s]
 
 
 def incoming_products(left, right, gather_ref, put):
@@ -193,9 +187,9 @@
             ]
             wide.append(jnp.concatenate(part, axis=1))
     packed = dot(jnp.concatenate(wide, axis=0), gather_ref[...], 1, 0)
-    for pair in range(8):
-        for x in range(2):
-            put(2 * pair + x, packed[64 * pair : 64 * (pair + 1), 128 * x : 128 * (x + 1)])
+    packed = packed.reshape(8, 8, 8, 256)
+    for at in range(16):
+        put(at // 4, at % 4, packed[at // 2, :, :, 128 * (at % 2) : 128 * (at % 2 + 1)])
 
 
 def incoming_part(mine, msg_ref, spread_ref, rows_ref, put_left, put_right):
@@ -236,8 +230,8 @@
     right[:192] = right_own[...]
     left_near[...] = left[y0_ref[0]]
 
-    def put(at, part):
-        far_ref[at] = part.astype(BF16)
+    def put(zl, x, part):
+        far_ref[zl, :, x] = part.astype(BF16)
 
     incoming_products(left[1 - y0_ref[0]], right[...], gather_ref, put)
 
@@ -245,8 +239,8 @@
 def incoming_near_kernel(y0_ref, left, right, far_ref, gather_ref, out_ref):
     other = 1 - y0_ref[0]
 
-    def put(at, part):
-        out_ref[at] = (part + far_ref[other, at].astype(F32)).astype(BF16)
+    def put(zl, x, part):
+        out_ref[zl, :, x] = (part + far_ref[other, zl, :, x].astype(F32)).astype(BF16)
 
     incoming_products(left[...], right[...], gather_ref, put)
 
@@ -255,19 +249,15 @@
 SMEM = pl.BlockSpec(memory_space=pltpu.SMEM)
 
 
-HBM = pl.BlockSpec(memory_space=pl.ANY)
-
-
-def call(kernel, outs, args, name, scratch=(), scalars=0, fetched=0):
+def call(kernel, outs, args, name, scratch=(), scalars=0):
     moved = sum(a.size * a.dtype.itemsize for a in args) + sum(2 * int(np.prod(s)) for s in outs)
     return pl.pallas_call(
         kernel,
         out_shape=[jax.ShapeDtypeStruct(s, BF16) for s in outs],
-        in_specs=[SMEM] * scalars + [VMEM] * (len(args) - scalars - fetched) + [HBM] * fetched,
+        in_specs=[SMEM] * scalars + [VMEM] * (len(args) - scalars),
         out_specs=[VMEM] * len(outs),
-        scratch_shapes=[pltpu.VMEM(s, BF16) for s in scratch]
-        + ([pltpu.SemaphoreType.DMA((fetched,))] if fetched else []),
-        compiler_params=pltpu.CompilerParams(vmem_limit_bytes=(56 if fetched else 48) * 1024 * 1024),
+        scratch_shapes=[pltpu.VMEM(s, BF16) for s in scratch],
+        compiler_params=pltpu.CompilerParams(vmem_limit_bytes=48 * 1024 * 1024),
         cost_estimate=pl.CostEstimate(flops=2_000_000_000, bytes_accessed=moved, transcendentals=0),
         name=name,
     )(*args)
@@ -275,6 +265,7 @@
 
 FLAT = (T, 128, C)
 MSG = (C, T, 2, 128)
+PRODUCT = (4, 8, 4, 8, 128)
 
 
 def shards(pair_rep, in_weights, out_weights):
@@ -284,19 +275,19 @@
 
     msg, gate, flat = call(
         first_kernel, [MSG, FLAT, FLAT], (y0, core, pair_rep, in_weights), "edges",
-        scratch=[pair_rep.shape, in_weights.shape], scalars=2, fetched=2,
+        scalars=2,
     )
     msg = lax.all_to_all(msg, TO_CHANNELS, 0, 0, tiled=True)
     right = msg[:, :4].reshape(C, 8, 128)
     far = lax.ppermute(right, "y0", SWAP)
     near = lax.all_gather(right, "core", axis=0, tiled=True).reshape(2, 16, 64, 128)
     left, near = call(
-        outgoing_near_kernel, [(192, 1024), (8, 64, 128)], (msg.reshape(16, 8, T, 2, 128), near, table, gather),
+        outgoing_near_kernel, [(192, 1024), (8, 8, 8, 128)], (msg.reshape(16, 8, T, 2, 128), near, table, gather),
         "outgoing_near", scratch=[(512, 1024)],
     )
     far = lax.all_gather(far, "core", axis=0, tiled=True).reshape(2, 16, 64, 128)
     (product,) = call(
-        outgoing_far_kernel, [(16, 64, 128)], (y0, left, near, far, table, gather),
+        outgoing_far_kernel, [PRODUCT], (y0, left, near, far, table, gather),
         "outgoing_far", scratch=[(512, 1024)], scalars=1,
     )
     product = lax.all_to_all(product.reshape(128, 8, 128), TO_POSITIONS, 0, 0, tiled=True)
@@ -311,13 +302,13 @@
         "incoming_own", scalars=1,
     )
     far, left, right = call(
-        incoming_far_kernel, [(16, 64, 128), (384, 256), (384, 1024)],
+        incoming_far_kernel, [PRODUCT, (384, 256), (384, 1024)],
         (y0, core, other.reshape(16, 8, T, 2, 128), left, right, table, rows, back),
         "incoming_far", scratch=[(2, 384, 256)], scalars=2,
     )
-    far = lax.all_gather(far.reshape(128, 8, 128), "y0", axis=0, tiled=True).reshape(2, 16, 64, 128)
+    far = lax.all_gather(far.reshape(128, 8, 128), "y0", axis=0, tiled=True).reshape(2, *PRODUCT)
     (product,) = call(
-        incoming_near_kernel, [(16, 64, 128)], (y0, left, right, far, back), "incoming_near", scalars=1
+        incoming_near_kernel, [PRODUCT], (y0, left, right, far, back), "incoming_near", scalars=1
     )
     product = lax.all_to_all(product.reshape(128, 8, 128), TO_POSITIONS, 0, 0, tiled=True)
     (out,) = call(last_kernel, [(ROWS, COLS, C)], (product, flat, gate, out_weights), "update")

time: 186 us -> 185 us (level)
  the two profiles are of different devices: /device:TPU:32 before, /device:TPU:4 now
where the time goes in v7:
time: 185 us; the launch traced here: 184 us
  blocking collectives  165 us (89%)
  Pallas kernels  8.79 us (5%)
  starting transfers between devices  4.81 us (3%)
  waiting for transfers between devices  3.3 us (2%)
  local copies, waits for them, and re-layouts  2.14 us (1%)
    all_to_all x2, blocking collectives, shards(): msg = lax.all_to_all(msg, TO_CHANNELS, 0, 0, tiled=True)  88.3 us
    all_to_all x2, blocking collectives, shards(): lax.all_to_all(product.reshape(128, 8, 128), TO_POSITIONS, 0, 0, tiled=True)  63.5 us
    all_gather x1, blocking collectives, shards(): lax.all_gather(far.reshape(128, 8, 128), 'y0', axis=0, tiled=True)  9.02 us
    pallas_call x8, Pallas kernels, call(): pl.pallas_call(kernel, out_shape=[jax.ShapeDtypeStruct(s, BF16) for s in...  8.79 us
  transfers between devices with their start and end apart: 2, of which 2 were waited for; matrix products, arithmetic and copies ran while one was open for 0% of the time, Pallas kernels for 1%

profile of v7, /device:TPU:4, one launch (start us, length us, event | category | flops | bytes accessed | tf_op | source)
XLA Modules:
  0.0 184.3 jit_solution(14003884259307341654)
XLA Ops:
  0.0 0.0 copy-start
  0.0 1.0 copy-done
  1.0 0.0 copy-start.2
  1.0 0.9 copy-done.2
  1.9 1.5 edges.1
  3.4 51.2 %all_to_all.20 = bf16[128,7,2,128]{3,2,1,0:T(2,128)(2,1)S(1)} all-to-all(bf16[128,7,2,128]{3,2,1,0:T(2,128)(2,1)S(1)} %get-tuple-element.18), channel_id=1, replica_groups=mesh['y1'=2,'y0'=2,'zh'=4,'core'=2,'zl'=4,'x'=4] {'x','zl','zh','y1'}, dimensions={0} | all-to-all | bytes 917504 | tf_op jit(solution)/shard_map/all_to_all | solution.py:280
  54.6 0.2 slice.4
  54.8 0.0 copy-start.6
  54.8 0.0 copy-start.7
  54.8 2.7 %collective-permute-start = (bf16[128,8,128]{2,1,0:T(8,128)(2,1)S(1)}, bf16[128,8,128]{2,1,0:T(8,128)(2,1)S(1)}, u32[]{:S(2)}, u32[]{:S(2)}) collective-permute-start(bf16[128,8,128]{2,1,0:T(8,128)(2,1)S(1)} %bitcast.21), channel_id=1, source_target_pairs={{0,128},{128,0},{1,129},{129,1},{2,130},{130,2},{3,131},{131,3},{4... | collective-permute-start | bytes 786440 | tf_op jit(solution)/shard_map/ppermute | solution.py:282
  57.5 2.2 %all_gather.9 = bf16[256,8,128]{2,1,0:T(8,128)(2,1)S(1)} all-gather(bf16[128,8,128]{2,1,0:T(8,128)(2,1)S(1)} %bitcast.22), channel_id=1, replica_groups=mesh['y1'=2,'y0'=2,'zh'=4,'core'=2,'zl'=4,'x'=4] {'core'}, dimensions={0}, use_global_device_ids=true | all-gather | bytes 786432 | tf_op jit(solution)/shard_map/all_gather | solution.py:283
  59.7 0.0 copy-done.6
  59.7 0.0 copy-done.7
  59.7 1.3 outgoing_near.1
  61.0 2.2 %collective-permute-done = bf16[128,8,128]{2,1,0:T(8,128)(2,1)S(1)} collective-permute-done((bf16[128,8,128]{2,1,0:T(8,128)(2,1)S(1)}, bf16[128,8,128]{2,1,0:T(8,128)(2,1)S(1)}, u32[]{:S(2)}, u32[]{:S(2)}) %collective-permute-start) | collective-permute-done | bytes 262176 | tf_op jit(solution)/shard_map/ppermute | solution.py:282
  63.2 2.2 %all_gather.10 = bf16[256,8,128]{2,1,0:T(8,128)(2,1)S(1)} all-gather(bf16[128,8,128]{2,1,0:T(8,128)(2,1)S(1)} %collective-permute-done), channel_id=1, replica_groups=mesh['y1'=2,'y0'=2,'zh'=4,'core'=2,'zl'=4,'x'=4] {'core'}, dimensions={0}, use_global_device_ids=true | all-gather | bytes 786432 | tf_op jit(solution)/shard_map/all_gather | solution.py:288
  65.4 1.1 outgoing_far.1
  66.5 0.0 copy-start.1
  66.5 0.0 copy-start.3
  66.5 32.4 %all_to_all.21.x_ref = bf16[128,8,128]{2,1,0:T(8,128)(2,1)S(1)} all-to-all(bf16[128,8,128]{2,1,0:T(8,128)(2,1)S(1)} %bitcast.19), channel_id=1, replica_groups=mesh['y1'=2,'y0'=2,'zh'=4,'core'=2,'zl'=4,'x'=4] {'zl','y1','zh','x'}, dimensions={0} | all-to-all | bytes 524288 | tf_op jit(solution)/shard_map/all_to_all | solution.py:293
  98.9 0.0 copy-done.1
  98.9 0.0 copy-done.3
  98.9 1.7 update_edges.1
  100.6 0.0 copy-start.4
  100.6 37.1 %all_to_all.22 = bf16[128,7,2,128]{3,2,1,0:T(2,128)(2,1)S(1)} all-to-all(bf16[128,7,2,128]{3,2,1,0:T(2,128)(2,1)S(1)} %get-tuple-element.23), channel_id=1, replica_groups=mesh['y1'=2,'y0'=2,'zh'=4,'core'=2,'zl'=4,'x'=4] {'x','zl','zh','y1'}, dimensions={0} | all-to-all | bytes 917504 | tf_op jit(solution)/shard_map/all_to_all | solution.py:297
  137.7 2.1 %collective-permute-start.1 = (bf16[128,7,2,128]{3,2,1,0:T(2,128)(2,1)S(1)}, bf16[128,7,2,128]{3,2,1,0:T(2,128)(2,1)S(1)}, u32[]{:S(2)}, u32[]{:S(2)}) collective-permute-start(bf16[128,7,2,128]{3,2,1,0:T(2,128)(2,1)S(1)} %all_to_all.22), channel_id=1, source_target_pairs={{0,16},{16,0},{1,17},{17,1},{2,18},{18,2},{3,19},{19,3},{4,20},{20... | collective-permute-start | bytes 1376264 | tf_op jit(solution)/shard_map/ppermute | solution.py:299
  139.8 0.0 copy-done.4
  139.8 0.0 copy-start.5
  139.8 0.5 incoming_own.1
  140.3 1.1 collective-permute-done.1
  141.4 0.0 copy-done.5
  141.4 1.0 incoming_far.1
  142.4 9.0 %all_gather.11 = bf16[256,8,128]{2,1,0:T(8,128)(2,1)S(1)} all-gather(bf16[128,8,128]{2,1,0:T(8,128)(2,1)S(1)} %bitcast.17), channel_id=1, replica_groups=mesh['y1'=2,'y0'=2,'zh'=4,'core'=2,'zl'=4,'x'=4] {'y0'}, dimensions={0}, use_global_device_ids=true | all-gather | bytes 786432 | tf_op jit(solution)/shard_map/all_gather | solution.py:309
  151.4 0.6 incoming_near.1
  152.1 31.1 %all_to_all.23.x_ref = bf16[128,8,128]{2,1,0:T(8,128)(2,1)S(1)} all-to-all(bf16[128,8,128]{2,1,0:T(8,128)(2,1)S(1)} %bitcast.18), channel_id=1, replica_groups=mesh['y1'=2,'y0'=2,'zh'=4,'core'=2,'zl'=4,'x'=4] {'zl','y1','zh','x'}, dimensions={0} | all-to-all | bytes 524288 | tf_op jit(solution)/shard_map/all_to_all | solution.py:313
  183.1 1.2 update.1
Async XLA Ops:
  0.0 1.0 copy-start
  1.0 0.9 copy-start.2
  54.8 4.9 %copy-start.6 = (bf16[256,384]{1,0:T(8,128)(2,1)S(1)}, bf16[256,384]{1,0:T(8,128)(2,1)}, u32[]{:S(2)}) copy-start(bf16[256,384]{1,0:T(8,128)(2,1)} %constant.18.clone.spread_ref) | copy-start | bytes 589828
  54.8 4.9 %copy-start.7 = (bf16[384,256]{1,0:T(8,128)(2,1)S(1)}, bf16[384,256]{1,0:T(8,128)(2,1)}, u32[]{:S(2)}) copy-start(bf16[384,256]{1,0:T(8,128)(2,1)} %constant.20.clone.gather_ref) | copy-start | bytes 589828
  54.8 8.4 %collective-permute-start = (bf16[128,8,128]{2,1,0:T(8,128)(2,1)S(1)}, bf16[128,8,128]{2,1,0:T(8,128)(2,1)S(1)}, u32[]{:S(2)}, u32[]{:S(2)}) collective-permute-start(bf16[128,8,128]{2,1,0:T(8,128)(2,1)S(1)} %bitcast.21), channel_id=1, source_target_pairs={{0,128},{128,0},{1,129},{129,1},{2,130},{130,2},{3,131},{131,3},{4... | collective-permute-start | bytes 786440 | tf_op jit(solution)/shard_map/ppermute | solution.py:282
  66.5 32.4 %copy-start.1 = (bf16[2,128,640]{2,1,0:T(8,128)(2,1)S(1)}, bf16[2,128,640]{2,1,0:T(8,128)(2,1)}, u32[]{:S(2)}) copy-start(bf16[2,128,640]{2,1,0:T(8,128)(2,1)} %w_ref.3) | copy-start | bytes 983044
  66.5 32.4 %copy-start.3 = (bf16[2,128,128]{2,1,0:T(8,128)(2,1)S(1)}, bf16[2,128,128]{2,1,0:T(8,128)(2,1)}, u32[]{:S(2)}) copy-start(bf16[2,128,128]{2,1,0:T(8,128)(2,1)} %wo_ref.3) | copy-start | bytes 196612
  100.6 39.2 %copy-start.4 = (bf16[2,512,384]{2,1,0:T(8,128)(2,1)S(1)}, bf16[2,512,384]{2,1,0:T(8,128)(2,1)}, u32[]{:S(2)}) copy-start(bf16[2,512,384]{2,1,0:T(8,128)(2,1)} %constant.21.clone.rows_ref) | copy-start | bytes 2359300
  137.7 3.7 %collective-permute-start.1 = (bf16[128,7,2,128]{3,2,1,0:T(2,128)(2,1)S(1)}, bf16[128,7,2,128]{3,2,1,0:T(2,128)(2,1)S(1)}, u32[]{:S(2)}, u32[]{:S(2)}) collective-permute-start(bf16[128,7,2,128]{3,2,1,0:T(2,128)(2,1)S(1)} %all_to_all.22), channel_id=1, source_target_pairs={{0,16},{16,0},{1,17},{17,1},{2,18},{18,2},{3,19},{19,3},{4,20},{20... | collective-permute-start | bytes 1376264 | tf_op jit(solution)/shard_map/ppermute | solution.py:299
  139.8 1.6 copy-start.5

commit v8 on v7

--- a/solution.py
+++ b/solution.py
@@ -8,11 +8,12 @@
 from jax.experimental.pallas import tpu as pltpu
 from jax.sharding import Mesh, PartitionSpec as P
 
-PARTS = (("y1", 2), ("y0", 2), ("zh", 4), ("core", 2), ("zl", 4), ("x", 4))
+PARTS = (("y1", 2), ("y0", 2), ("zh", 4), ("core", 2), ("zl", 4), ("x1", 2), ("x0", 2))
+SIZE = dict(PARTS)
 ROW = ("y1", "y0", "zh", "core")
-CHAN = ("zl", "x")
-TO_CHANNELS = ("x", "zl", "zh", "y1")
-TO_POSITIONS = ("zl", "y1", "zh", "x")
+CHAN = ("zl", "x1", "x0")
+TO_CHANNELS = (("x1", "x0", "zl", "zh", "y1"), ("x1", "zl", "zh", "y1", "y0"))
+TO_POSITIONS = (("zl", "y1", "zh", "x1", "x0"), ("zl", "y1", "y0", "zh", "x1"))
 SWAP = [(0, 1), (1, 0)]
 ROWS, COLS, C = 21, 42, 128
 T, U = 7, 3
@@ -73,9 +74,13 @@
     msg_ref[...] = jnp.swapaxes(both, 0, 1).astype(BF16).reshape(C, T, 2, 128)
 
 
+def owners(step):
+    order = np.arange(C).reshape([SIZE[name] for name in TO_POSITIONS[step]])
+    return order.transpose([TO_POSITIONS[step].index(name) for name in TO_CHANNELS[step]]).reshape(-1).tolist()
+
+
 def updated(x_ref, p_ref, gate_ref, w_ref, step):
-    owners = [((zl * 2 + y1) * 4 + zh) * 4 + x for x in range(4) for zl in range(4) for zh in range(4) for y1 in range(2)]
-    product = jnp.swapaxes(jnp.stack([x_ref[owner].astype(F32) for owner in owners], axis=0), 0, 1)
+    product = jnp.swapaxes(jnp.stack([x_ref[owner].astype(F32) for owner in owners(step)], axis=0), 0, 1)
     blocks = []
     for t in range(T):
         normed = layer_norm(product[t + 1], 0).astype(BF16)
@@ -84,7 +89,7 @@
     return blocks
 
 
-def first_kernel(y0_ref, core_ref, p_ref, w_ref, msg_ref, gate_ref, flat_ref):
+def first_kernel(y0_ref, x0_ref, core_ref, p_ref, w_ref, msg_ref, gate_ref, flat_ref):
     blocks = []
     for t in range(T):
         rows = [p_ref[U * t + u].astype(F32) for u in range(U)]
@@ -109,24 +114,26 @@
             out_ref[U * t + u] = block[COLS * u : COLS * (u + 1)].astype(BF16)
 
 
-def fan(get, count, table):
-    wide = []
-    for zl in range(4):
-        for first in range(0, 4, count):
-            wide.append(jnp.concatenate([get(4 * x + zl) for x in range(first, first + count)], axis=1))
+def fan(get, groups, table):
+    wide = [jnp.concatenate([get(at) for at in group], axis=1) for group in groups]
     return dot(jnp.concatenate(wide, axis=0), table, 1, 0)
 
 
+PAIRS = [(8 * x1 + zl, 8 * x1 + 4 + zl) for zl in range(4) for x1 in range(2)]
+NEXT_PAIRS = [(zl, 4 + zl) for zl in range(4)]
+NEXT_QUADS = [(2 * y1, 4 + 2 * y1, 2 * y1 + 1, 5 + 2 * y1) for y1 in range(2)]
+
+
 def right_of(ref, at):
-    return ref[at, :, :4].reshape(64, 128)
+    return ref[at, :, :4].reshape(-1, 128)
 
 
 def left_of(ref, at):
-    return ref[at, :, 3:].reshape(64, 128)
+    return ref[at, :, 3:].reshape(-1, 128)
 
 
 def fill_right(right, core, get, table):
-    part = fan(get, 2, table).astype(BF16)
+    part = fan(get, PAIRS, table).astype(BF16)
     for pair in range(8):
         for v in range(U):
             for high in range(4):
@@ -148,7 +155,7 @@
 
 def outgoing_near_kernel(msg_ref, near_ref, spread_ref, gather_ref, left, out_ref, right):
     table = spread_ref[...]
-    part = fan(lambda at: left_of(msg_ref, at), 2, table).astype(BF16)
+    part = fan(lambda at: left_of(msg_ref, at), PAIRS, table).astype(BF16)
     for pair in range(8):
         for u in range(U):
             left[64 * u : 64 * (u + 1), 128 * pair : 128 * (pair + 1)] = part[
@@ -177,72 +184,60 @@
         out_ref[2 * y1 + 1 - y0, :, zh] = packed[s]
 
 
-def incoming_products(left, right, gather_ref, put):
-    product = dot(left, right, 0, 0).astype(BF16)
-    wide = []
-    for pair in range(8):
+def fill_incoming_left(left, at, get, rows):
+    part = pltpu.roll(fan(get, NEXT_QUADS, rows).reshape(32, 8, U * 128), 7, 1)
+    at_t = lax.broadcasted_iota(jnp.int32, part.shape, 1)
+    part = jnp.where(at_t < T, part, 0).reshape(256, U * 128).astype(BF16)
+    for u in range(U):
         for y1 in range(2):
-            part = [
-                product[128 * y1 + 32 * w : 128 * y1 + 32 * (w + 1), 128 * pair : 128 * (pair + 1)] for w in range(U)
+            left[at + 128 * u : at + 128 * (u + 1), 128 * y1 : 128 * (y1 + 1)] = part[
+                128 * y1 : 128 * (y1 + 1), 128 * u : 128 * (u + 1)
             ]
-            wide.append(jnp.concatenate(part, axis=1))
-    packed = dot(jnp.concatenate(wide, axis=0), gather_ref[...], 1, 0)
-    packed = packed.reshape(8, 8, 8, 256)
-    for at in range(16):
-        put(at // 4, at % 4, packed[at // 2, :, :, 128 * (at % 2) : 128 * (at % 2 + 1)])
-
-
-def incoming_part(mine, msg_ref, spread_ref, rows_ref, put_left, put_right):
-    lefts = pltpu.roll(fan(lambda m: left_of(msg_ref, m), 4, rows_ref[mine]).reshape(32, 8, U * 128), 7, 1)
-    at_t = lax.broadcasted_iota(jnp.int32, lefts.shape, 1)
-    lefts = jnp.where(at_t < T, lefts, 0).reshape(256, U * 128).astype(BF16)
-    rights = fan(lambda m: right_of(msg_ref, m), 2, spread_ref[...]).astype(BF16)
+
+
+def fill_incoming_right(right, at, get, table):
+    part = fan(get, NEXT_PAIRS, table).astype(BF16)
     for u in range(U):
         for zl in range(4):
-            put_left(u, zl, lefts[64 * zl : 64 * (zl + 1), 128 * u : 128 * (u + 1)])
-        for pair in range(8):
-            put_right(u, pair, rights[64 * pair : 64 * (pair + 1), 128 * u : 128 * (u + 1)])
+            right[at + 128 * u : at + 128 * (u + 1), 128 * zl : 128 * (zl + 1)] = part[
+                128 * zl : 128 * (zl + 1), 128 * u : 128 * (u + 1)
+            ]
+
+
+def incoming_products(left, right, gather_ref):
+    product = dot(left[...], right[...], 0, 0).astype(BF16)
+    wide = []
+    for zl in range(4):
+        for y1 in range(2):
+            part = [product[128 * y1 + 32 * w : 128 * y1 + 32 * (w + 1), 128 * zl : 128 * (zl + 1)] for w in range(U)]
+            wide.append(jnp.concatenate(part, axis=1))
+    packed = dot(jnp.concatenate(wide, axis=0), gather_ref[...], 1, 0).reshape(4, 4, 2, 8, 256).astype(BF16)
+    return [packed[at // 2, ..., 128 * (at % 2) : 128 * (at % 2 + 1)] for at in range(8)]
 
 
 def incoming_own_kernel(core_ref, msg_ref, spread_ref, rows_ref, left, right):
-    def put_left(u, zl, part):
-        y1, y = divmod(zl, 2)
-        left[y, 64 * u : 64 * (u + 1), 128 * y1 : 128 * (y1 + 1)] = part
-
-    def put_right(u, pair, part):
-        right[64 * u : 64 * (u + 1), 128 * pair : 128 * (pair + 1)] = part
-
-    incoming_part(core_ref[0], msg_ref, spread_ref, rows_ref, put_left, put_right)
-
-
-def incoming_far_kernel(
-    y0_ref, core_ref, msg_ref, left_own, right_own, spread_ref, rows_ref, gather_ref, far_ref, left_near, right, left
-):
-    def put_left(u, zl, part):
-        y1, y = divmod(zl, 2)
-        left[y, 192 + 64 * u : 192 + 64 * (u + 1), 128 * y1 : 128 * (y1 + 1)] = part
-
-    def put_right(u, pair, part):
-        right[192 + 64 * u : 192 + 64 * (u + 1), 128 * pair : 128 * (pair + 1)] = part
-
-    incoming_part(core_ref[0], msg_ref, spread_ref, rows_ref, put_left, put_right)
-    left[:, :192] = left_own[...]
-    right[:192] = right_own[...]
-    left_near[...] = left[y0_ref[0]]
-
-    def put(zl, x, part):
-        far_ref[zl, :, x] = part.astype(BF16)
-
-    incoming_products(left[1 - y0_ref[0]], right[...], gather_ref, put)
-
-
-def incoming_near_kernel(y0_ref, left, right, far_ref, gather_ref, out_ref):
-    other = 1 - y0_ref[0]
-
-    def put(zl, x, part):
-        out_ref[zl, :, x] = (part + far_ref[other, zl, :, x].astype(F32)).astype(BF16)
-
-    incoming_products(left[...], right[...], gather_ref, put)
+    fill_incoming_left(left, 0, lambda at: left_of(msg_ref, at), rows_ref[core_ref[0]])
+    fill_incoming_right(right, 0, lambda at: right_of(msg_ref, at), spread_ref[...])
+
+
+def incoming_near_kernel(core_ref, msg_ref, left_own, right_own, spread_ref, rows_ref, gather_ref, right, out_ref, left):
+    left[:384] = left_own[...]
+    right[:384] = right_own[...]
+    fill_incoming_left(left, 384, lambda at: left_of(msg_ref, at), rows_ref[core_ref[0]])
+    fill_incoming_right(right, 384, lambda at: right_of(msg_ref, at), spread_ref[...])
+    packed = incoming_products(left, right, gather_ref)
+    for at in range(8):
+        out_ref[at] = packed[at]
+
+
+def incoming_far_kernel(x0_ref, core_ref, far_ref, right, near_ref, rows_ref, gather_ref, out_ref, left):
+    x0, core = x0_ref[0], core_ref[0]
+    for at, k_core in ((0, core), (384, 1 - core)):
+        fill_incoming_left(left, at, lambda m, k_core=k_core: far_ref[k_core, m], rows_ref[core])
+    packed = incoming_products(left, right, gather_ref)
+    for at in range(8):
+        out_ref[at // 2, :, :, x0, at % 2] = near_ref[at]
+        out_ref[at // 2, :, :, 1 - x0, at % 2] = packed[at]
 
 
 VMEM = pl.BlockSpec(memory_space=pltpu.VMEM)
@@ -266,18 +261,19 @@
 FLAT = (T, 128, C)
 MSG = (C, T, 2, 128)
 PRODUCT = (4, 8, 4, 8, 128)
+NEXT_PRODUCT = (4, 4, 2, 2, 2, 8, 128)
 
 
 def shards(pair_rep, in_weights, out_weights):
     table, back = jnp.asarray(spread(), BF16), jnp.asarray(spread().T, BF16)
     gather = jnp.asarray(gather_rows(), BF16)
-    y0, core = (lax.axis_index(name).astype(jnp.int32)[None] for name in ("y0", "core"))
+    y0, x0, core = (lax.axis_index(name).astype(jnp.int32)[None] for name in ("y0", "x0", "core"))
 
     msg, gate, flat = call(
-        first_kernel, [MSG, FLAT, FLAT], (y0, core, pair_rep, in_weights), "edges",
-        scalars=2,
-    )
-    msg = lax.all_to_all(msg, TO_CHANNELS, 0, 0, tiled=True)
+        first_kernel, [MSG, FLAT, FLAT], (y0, x0, core, pair_rep, in_weights), "edges",
+        scalars=3,
+    )
+    msg = lax.all_to_all(msg, TO_CHANNELS[0], 0, 0, tiled=True)
     right = msg[:, :4].reshape(C, 8, 128)
     far = lax.ppermute(right, "y0", SWAP)
     near = lax.all_gather(right, "core", axis=0, tiled=True).reshape(2, 16, 64, 128)
@@ -290,27 +286,29 @@
         outgoing_far_kernel, [PRODUCT], (y0, left, near, far, table, gather),
         "outgoing_far", scratch=[(512, 1024)], scalars=1,
     )
-    product = lax.all_to_all(product.reshape(128, 8, 128), TO_POSITIONS, 0, 0, tiled=True)
+    product = lax.all_to_all(product.reshape(128, 8, 128), TO_POSITIONS[0], 0, 0, tiled=True)
     msg, gate, flat = call(
         middle_kernel, [MSG, FLAT, FLAT], (product, flat, gate, out_weights, in_weights), "update_edges"
     )
-    msg = lax.all_to_all(msg, TO_CHANNELS, 0, 0, tiled=True)
+    msg = lax.all_to_all(msg, TO_CHANNELS[1], 0, 0, tiled=True)
     rows = jnp.asarray(spread_rows(), BF16)
+    far = lax.ppermute(msg[:, 3:].reshape(C, 8, 128), "x0", SWAP)
     other = lax.ppermute(msg, "core", SWAP)
     left, right = call(
-        incoming_own_kernel, [(2, 192, 256), (192, 1024)], (core, msg.reshape(16, 8, T, 2, 128), table, rows),
+        incoming_own_kernel, [(384, 256), (384, 512)], (core, msg.reshape(8, 16, T, 2, 128), table, rows),
         "incoming_own", scalars=1,
     )
-    far, left, right = call(
-        incoming_far_kernel, [PRODUCT, (384, 256), (384, 1024)],
-        (y0, core, other.reshape(16, 8, T, 2, 128), left, right, table, rows, back),
-        "incoming_far", scratch=[(2, 384, 256)], scalars=2,
-    )
-    far = lax.all_gather(far.reshape(128, 8, 128), "y0", axis=0, tiled=True).reshape(2, *PRODUCT)
+    right, near = call(
+        incoming_near_kernel, [(768, 512), (8, 4, 2, 8, 128)],
+        (core, other.reshape(8, 16, T, 2, 128), left, right, table, rows, back),
+        "incoming_near", scratch=[(768, 256)], scalars=1,
+    )
+    far = lax.all_gather(far, "core", axis=0, tiled=True).reshape(2, 8, 128, 128)
     (product,) = call(
-        incoming_near_kernel, [PRODUCT], (y0, left, right, far, back), "incoming_near", scalars=1
-    )
-    product = lax.all_to_all(product.reshape(128, 8, 128), TO_POSITIONS, 0, 0, tiled=True)
+        incoming_far_kernel, [NEXT_PRODUCT], (x0, core, far, right, near, rows, back),
+        "incoming_far", scratch=[(768, 256)], scalars=2,
+    )
+    product = lax.all_to_all(product.reshape(128, 8, 128), TO_POSITIONS[1], 0, 0, tiled=True)
     (out,) = call(last_kernel, [(ROWS, COLS, C)], (product, flat, gate, out_weights), "update")
     return out
 

time: 185 us -> 189 us (1.022)
  the two profiles are of different devices: /device:TPU:4 before, /device:TPU:32 now
where the time goes in v8:
time: 189 us; the launch traced here: 188 us
  blocking collectives  160 us (85%)
  waiting for transfers between devices  9.07 us (5%)
  Pallas kernels  9.05 us (5%)
  starting transfers between devices  7.87 us (4%)
  local copies, waits for them, and re-layouts  2.32 us (1%)
    all_to_all x1, blocking collectives, shards(): msg = lax.all_to_all(msg, TO_CHANNELS[0], 0, 0, tiled=True)  54.2 us
    all_to_all x1, blocking collectives, shards(): msg = lax.all_to_all(msg, TO_CHANNELS[1], 0, 0, tiled=True)  40.1 us
    all_to_all x1, blocking collectives, shards(): lax.all_to_all(product.reshape(128, 8, 128), TO_POSITIONS[1], 0, 0, tiled...  29.8 us
    all_to_all x1, blocking collectives, shards(): lax.all_to_all(product.reshape(128, 8, 128), TO_POSITIONS[0], 0, 0, tiled...  29.1 us
    pallas_call x8, Pallas kernels, call(): pl.pallas_call(kernel, out_shape=[jax.ShapeDtypeStruct(s, BF16) for s in...  9.05 us
    ppermute x1, waiting for transfers between devices, shards(): far = lax.ppermute(msg[:, 3:].reshape(C, 8, 128), 'x0', SWAP)  6.87 us
  transfers between devices with their start and end apart: 3, of which 2 were waited for; matrix products, arithmetic and copies ran while one was open for 0% of the time, Pallas kernels for 1%

profile of v8, /device:TPU:32, one launch (start us, length us, event | category | flops | bytes accessed | tf_op | source)
XLA Modules:
  0.0 188.4 jit_solution(5491698119232654231)
XLA Ops:
  0.0 0.0 copy-start
  0.0 1.0 copy-done
  1.0 0.0 copy-start.2
  1.0 0.9 copy-done.2
  1.9 1.5 edges.1
  3.4 54.2 %all_to_all.20 = bf16[128,7,2,128]{3,2,1,0:T(2,128)(2,1)S(1)} all-to-all(bf16[128,7,2,128]{3,2,1,0:T(2,128)(2,1)S(1)} %get-tuple-element.17), channel_id=1, replica_groups=mesh['y1'=2,'y0'=2,'zh'=4,'core'=2,'zl'=4,'x1'=2,'x0'=2] {'x1','x0','zl'..., dimensions={0} | all-to-all | bytes 917504 | tf_op jit(solution)/shard_map/all_to_all | solution.py:276
  57.6 0.2 slice.8
  57.8 0.0 copy-start.6
  57.8 0.0 copy-start.7
  57.8 2.7 %collective-permute-start = (bf16[128,8,128]{2,1,0:T(8,128)(2,1)S(1)}, bf16[128,8,128]{2,1,0:T(8,128)(2,1)S(1)}, u32[]{:S(2)}, u32[]{:S(2)}) collective-permute-start(bf16[128,8,128]{2,1,0:T(8,128)(2,1)S(1)} %bitcast.21), channel_id=1, source_target_pairs={{0,128},{128,0},{1,129},{129,1},{2,130},{130,2},{3,131},{131,3},{4... | collective-permute-start | bytes 786440 | tf_op jit(solution)/shard_map/ppermute | solution.py:278
  60.6 2.2 %all_gather.9 = bf16[256,8,128]{2,1,0:T(8,128)(2,1)S(1)} all-gather(bf16[128,8,128]{2,1,0:T(8,128)(2,1)S(1)} %bitcast.22), channel_id=1, replica_groups=mesh['y1'=2,'y0'=2,'zh'=4,'core'=2,'zl'=4,'x1'=2,'x0'=2] {'core'}, dimensions={0}, use_global_device_ids=true | all-gather | bytes 786432 | tf_op jit(solution)/shard_map/all_gather | solution.py:279
  62.8 0.0 copy-done.6
  62.8 0.0 copy-done.7
  62.8 1.3 outgoing_near.1
  64.0 2.2 %collective-permute-done = bf16[128,8,128]{2,1,0:T(8,128)(2,1)S(1)} collective-permute-done((bf16[128,8,128]{2,1,0:T(8,128)(2,1)S(1)}, bf16[128,8,128]{2,1,0:T(8,128)(2,1)S(1)}, u32[]{:S(2)}, u32[]{:S(2)}) %collective-permute-start) | collective-permute-done | bytes 262176 | tf_op jit(solution)/shard_map/ppermute | solution.py:278
  66.2 2.2 %all_gather.10 = bf16[256,8,128]{2,1,0:T(8,128)(2,1)S(1)} all-gather(bf16[128,8,128]{2,1,0:T(8,128)(2,1)S(1)} %collective-permute-done), channel_id=1, replica_groups=mesh['y1'=2,'y0'=2,'zh'=4,'core'=2,'zl'=4,'x1'=2,'x0'=2] {'core'}, dimensions={0}, use_global_device_ids=true | all-gather | bytes 786432 | tf_op jit(solution)/shard_map/all_gather | solution.py:284
  68.4 1.1 outgoing_far.1
  69.5 0.0 copy-start.1
  69.5 0.0 copy-start.3
  69.6 29.1 %all_to_all.21.x_ref = bf16[128,8,128]{2,1,0:T(8,128)(2,1)S(1)} all-to-all(bf16[128,8,128]{2,1,0:T(8,128)(2,1)S(1)} %bitcast.19), channel_id=1, replica_groups=mesh['y1'=2,'y0'=2,'zh'=4,'core'=2,'zl'=4,'x1'=2,'x0'=2] {'zl','y1','zh'..., dimensions={0} | all-to-all | bytes 524288 | tf_op jit(solution)/shard_map/all_to_all | solution.py:289
  98.7 0.0 copy-done.1
  98.7 0.0 copy-done.3
  98.7 1.7 update_edges.1
  100.3 0.0 copy-start.4
  100.4 40.1 %all_to_all.22 = bf16[128,7,2,128]{3,2,1,0:T(2,128)(2,1)S(1)} all-to-all(bf16[128,7,2,128]{3,2,1,0:T(2,128)(2,1)S(1)} %get-tuple-element.22), channel_id=1, replica_groups=mesh['y1'=2,'y0'=2,'zh'=4,'core'=2,'zl'=4,'x1'=2,'x0'=2] {'x1','zl','zh'..., dimensions={0} | all-to-all | bytes 917504 | tf_op jit(solution)/shard_map/all_to_all | solution.py:293
  140.4 1.9 %collective-permute-start.2 = (bf16[128,7,2,128]{3,2,1,0:T(2,128)(2,1)S(1)}, bf16[128,7,2,128]{3,2,1,0:T(2,128)(2,1)S(1)}, u32[]{:S(2)}, u32[]{:S(2)}) collective-permute-start(bf16[128,7,2,128]{3,2,1,0:T(2,128)(2,1)S(1)} %all_to_all.22), channel_id=1, source_target_pairs={{0,16},{16,0},{1,17},{17,1},{2,18},{18,2},{3,19},{19,3},{4,20},{20... | collective-permute-start | bytes 1376264 | tf_op jit(solution)/shard_map/ppermute | solution.py:296
  142.3 0.2 slice.9
  142.5 3.2 %collective-permute-start.1 = (bf16[128,8,128]{2,1,0:T(8,128)(2,1)S(1)}, bf16[128,8,128]{2,1,0:T(8,128)(2,1)S(1)}, u32[]{:S(2)}, u32[]{:S(2)}) collective-permute-start(bf16[128,8,128]{2,1,0:T(8,128)(2,1)S(1)} %bitcast.23), channel_id=1, source_target_pairs={{0,1},{1,0},{2,3},{3,2},{4,5},{5,4},{6,7},{7,6},{8,9},{9,8},{10,11... | collective-permute-start | bytes 786440 | tf_op jit(solution)/shard_map/ppermute | solution.py:295
  145.8 0.0 copy-done.4
  145.8 0.5 incoming_own.1
  146.2 0.0 copy-start.5
  146.3 6.9 %collective-permute-done.1 = bf16[128,8,128]{2,1,0:T(8,128)(2,1)S(1)} collective-permute-done((bf16[128,8,128]{2,1,0:T(8,128)(2,1)S(1)}, bf16[128,8,128]{2,1,0:T(8,128)(2,1)S(1)}, u32[]{:S(2)}, u32[]{:S(2)}) %collective-permute-start.1) | collective-permute-done | bytes 262176 | tf_op jit(solution)/shard_map/ppermute | solution.py:295
  153.1 2.3 %all_gather.11 = bf16[256,8,128]{2,1,0:T(8,128)(2,1)S(1)} all-gather(bf16[128,8,128]{2,1,0:T(8,128)(2,1)S(1)} %collective-permute-done.1), channel_id=1, replica_groups=mesh['y1'=2,'y0'=2,'zh'=4,'core'=2,'zl'=4,'x1'=2,'x0'=2] {'core'}, dimensions={0}, use_global_device_ids=true | all-gather | bytes 786432 | tf_op jit(solution)/shard_map/all_gather | solution.py:306
  155.5 0.0 collective-permute-done.2
  155.5 0.0 copy-done.5
  155.5 1.0 incoming_near.1
  156.5 0.9 incoming_far.1
  157.4 29.8 %all_to_all.23.x_ref = bf16[128,8,128]{2,1,0:T(8,128)(2,1)S(1)} all-to-all(bf16[128,8,128]{2,1,0:T(8,128)(2,1)S(1)} %bitcast.18), channel_id=1, replica_groups=mesh['y1'=2,'y0'=2,'zh'=4,'core'=2,'zl'=4,'x1'=2,'x0'=2] {'zl','y1','y0'..., dimensions={0} | all-to-all | bytes 524288 | tf_op jit(solution)/shard_map/all_to_all | solution.py:311
  187.2 1.2 update.1
Async XLA Ops:
  0.0 1.0 copy-start
  1.0 0.9 copy-start.2
  57.8 4.9 %copy-start.6 = (bf16[256,384]{1,0:T(8,128)(2,1)S(1)}, bf16[256,384]{1,0:T(8,128)(2,1)}, u32[]{:S(2)}) copy-start(bf16[256,384]{1,0:T(8,128)(2,1)} %constant.20.clone.spread_ref) | copy-start | bytes 589828
  57.8 4.9 %copy-start.7 = (bf16[384,256]{1,0:T(8,128)(2,1)S(1)}, bf16[384,256]{1,0:T(8,128)(2,1)}, u32[]{:S(2)}) copy-start(bf16[384,256]{1,0:T(8,128)(2,1)} %constant.22.clone.gather_ref) | copy-start | bytes 589828
  57.8 8.4 %collective-permute-start = (bf16[128,8,128]{2,1,0:T(8,128)(2,1)S(1)}, bf16[128,8,128]{2,1,0:T(8,128)(2,1)S(1)}, u32[]{:S(2)}, u32[]{:S(2)}) collective-permute-start(bf16[128,8,128]{2,1,0:T(8,128)(2,1)S(1)} %bitcast.21), channel_id=1, source_target_pairs={{0,128},{128,0},{1,129},{129,1},{2,130},{130,2},{3,131},{131,3},{4... | collective-permute-start | bytes 786440 | tf_op jit(solution)/shard_map/ppermute | solution.py:278
  69.5 29.2 %copy-start.1 = (bf16[2,128,640]{2,1,0:T(8,128)(2,1)S(1)}, bf16[2,128,640]{2,1,0:T(8,128)(2,1)}, u32[]{:S(2)}) copy-start(bf16[2,128,640]{2,1,0:T(8,128)(2,1)} %w_ref.3) | copy-start | bytes 983044
  69.5 29.1 %copy-start.3 = (bf16[2,128,128]{2,1,0:T(8,128)(2,1)S(1)}, bf16[2,128,128]{2,1,0:T(8,128)(2,1)}, u32[]{:S(2)}) copy-start(bf16[2,128,128]{2,1,0:T(8,128)(2,1)} %wo_ref.3) | copy-start | bytes 196612
  100.3 45.4 %copy-start.4 = (bf16[2,512,384]{2,1,0:T(8,128)(2,1)S(1)}, bf16[2,512,384]{2,1,0:T(8,128)(2,1)}, u32[]{:S(2)}) copy-start(bf16[2,512,384]{2,1,0:T(8,128)(2,1)} %constant.23.clone.rows_ref) | copy-start | bytes 2359300
  140.4 15.1 %collective-permute-start.2 = (bf16[128,7,2,128]{3,2,1,0:T(2,128)(2,1)S(1)}, bf16[128,7,2,128]{3,2,1,0:T(2,128)(2,1)S(1)}, u32[]{:S(2)}, u32[]{:S(2)}) collective-permute-start(bf16[128,7,2,128]{3,2,1,0:T(2,128)(2,1)S(1)} %all_to_all.22), channel_id=1, source_target_pairs={{0,16},{16,0},{1,17},{17,1},{2,18},{18,2},{3,19},{19,3},{4,20},{20... | collective-permute-start | bytes 1376264 | tf_op jit(solution)/shard_map/ppermute | solution.py:296
  142.5 10.6 %collective-permute-start.1 = (bf16[128,8,128]{2,1,0:T(8,128)(2,1)S(1)}, bf16[128,8,128]{2,1,0:T(8,128)(2,1)S(1)}, u32[]{:S(2)}, u32[]{:S(2)}) collective-permute-start(bf16[128,8,128]{2,1,0:T(8,128)(2,1)S(1)} %bitcast.23), channel_id=1, source_target_pairs={{0,1},{1,0},{2,3},{3,2},{4,5},{5,4},{6,7},{7,6},{8,9},{9,8},{10,11... | collective-permute-start | bytes 786440 | tf_op jit(solution)/shard_map/ppermute | solution.py:295
  146.2 9.2 %copy-start.5 = (bf16[384,256]{1,0:T(8,128)(2,1)S(1)}, bf16[384,256]{1,0:T(8,128)(2,1)}, u32[]{:S(2)}) copy-start(bf16[384,256]{1,0:T(8,128)(2,1)} %constant.21.clone.gather_ref) | copy-start | bytes 589828

commit v9 on v8

--- a/solution.py
+++ b/solution.py
@@ -215,25 +215,19 @@
     return [packed[at // 2, ..., 128 * (at % 2) : 128 * (at % 2 + 1)] for at in range(8)]
 
 
-def incoming_own_kernel(core_ref, msg_ref, spread_ref, rows_ref, left, right):
-    fill_incoming_left(left, 0, lambda at: left_of(msg_ref, at), rows_ref[core_ref[0]])
-    fill_incoming_right(right, 0, lambda at: right_of(msg_ref, at), spread_ref[...])
-
-
-def incoming_near_kernel(core_ref, msg_ref, left_own, right_own, spread_ref, rows_ref, gather_ref, right, out_ref, left):
-    left[:384] = left_own[...]
-    right[:384] = right_own[...]
-    fill_incoming_left(left, 384, lambda at: left_of(msg_ref, at), rows_ref[core_ref[0]])
-    fill_incoming_right(right, 384, lambda at: right_of(msg_ref, at), spread_ref[...])
+def incoming_near_kernel(core_ref, left_ref, right_ref, spread_ref, rows_ref, gather_ref, right, out_ref, left):
+    for k_core in range(2):
+        fill_incoming_left(left, 384 * k_core, lambda at: left_ref[k_core, at], rows_ref[core_ref[0]])
+        fill_incoming_right(right, 384 * k_core, lambda at: right_ref[k_core, at], spread_ref[...])
     packed = incoming_products(left, right, gather_ref)
     for at in range(8):
         out_ref[at] = packed[at]
 
 
-def incoming_far_kernel(x0_ref, core_ref, far_ref, right, near_ref, rows_ref, gather_ref, out_ref, left):
-    x0, core = x0_ref[0], core_ref[0]
-    for at, k_core in ((0, core), (384, 1 - core)):
-        fill_incoming_left(left, at, lambda m, k_core=k_core: far_ref[k_core, m], rows_ref[core])
+def incoming_far_kernel(x0_ref, core_ref, left_ref, right, near_ref, rows_ref, gather_ref, out_ref, left):
+    x0 = x0_ref[0]
+    for k_core in range(2):
+        fill_incoming_left(left, 384 * k_core, lambda at: left_ref[k_core, at], rows_ref[core_ref[0]])
     packed = incoming_products(left, right, gather_ref)
     for at in range(8):
         out_ref[at // 2, :, :, x0, at % 2] = near_ref[at]
@@ -244,8 +238,8 @@
 SMEM = pl.BlockSpec(memory_space=pltpu.SMEM)
 
 
-def call(kernel, outs, args, name, scratch=(), scalars=0):
-    moved = sum(a.size * a.dtype.itemsize for a in args) + sum(2 * int(np.prod(s)) for s in outs)
+def call(kernel, outs, args, name, scratch=(), scalars=0, flops=2_000_000_000):
+    moved = flops // 1000
     return pl.pallas_call(
         kernel,
         out_shape=[jax.ShapeDtypeStruct(s, BF16) for s in outs],
@@ -253,7 +247,7 @@
         out_specs=[VMEM] * len(outs),
         scratch_shapes=[pltpu.VMEM(s, BF16) for s in scratch],
         compiler_params=pltpu.CompilerParams(vmem_limit_bytes=48 * 1024 * 1024),
-        cost_estimate=pl.CostEstimate(flops=2_000_000_000, bytes_accessed=moved, transcendentals=0),
+        cost_estimate=pl.CostEstimate(flops=flops, bytes_accessed=moved, transcendentals=0),
         name=name,
     )(*args)
 
@@ -292,16 +286,13 @@
     )
     msg = lax.all_to_all(msg, TO_CHANNELS[1], 0, 0, tiled=True)
     rows = jnp.asarray(spread_rows(), BF16)
-    far = lax.ppermute(msg[:, 3:].reshape(C, 8, 128), "x0", SWAP)
-    other = lax.ppermute(msg, "core", SWAP)
-    left, right = call(
-        incoming_own_kernel, [(384, 256), (384, 512)], (core, msg.reshape(8, 16, T, 2, 128), table, rows),
-        "incoming_own", scalars=1,
-    )
+    left, right = msg[:, 3:].reshape(C, 8, 128), msg[:, :4].reshape(C, 8, 128)
+    far = lax.ppermute(left, "x0", SWAP)
+    left = lax.all_gather(left, "core", axis=0, tiled=True).reshape(2, 8, 128, 128)
+    right = lax.all_gather(right, "core", axis=0, tiled=True).reshape(2, 8, 128, 128)
     right, near = call(
-        incoming_near_kernel, [(768, 512), (8, 4, 2, 8, 128)],
-        (core, other.reshape(8, 16, T, 2, 128), left, right, table, rows, back),
-        "incoming_near", scratch=[(768, 256)], scalars=1,
+        incoming_near_kernel, [(768, 512), (8, 4, 2, 8, 128)], (core, left, right, table, rows, back),
+        "incoming_near", scratch=[(768, 256)], scalars=1, flops=1_000_000,
     )
     far = lax.all_gather(far, "core", axis=0, tiled=True).reshape(2, 8, 128, 128)
     (product,) = call(

time: 189 us -> 185 us (0.979)
  waiting for transfers between devices: 9.07 us -> 2.2 us
  blocking collectives: 160 us -> 165 us
    ppermute x2 -> x1, waiting for transfers between devices: 6.87 us -> 0.01 us  [shards(): far = lax.ppermute(left, 'x0', SWAP)]
    all_gather x0 -> x2, blocking collectives: none -> 4.66 us  [the longest x1 2.48 us: shards(): lax.all_gather(right, 'core', axis=0, tiled=True).reshape(2, 8, 128, 128)]
    ppermute x2 -> x1, starting transfers between devices: 5.15 us -> 3.34 us  [shards(): far = lax.ppermute(left, 'x0', SWAP)]
    pallas_call x8 -> x7, Pallas kernels: 9.05 us -> 8.83 us  [call(): pl.pallas_call(kernel, out_shape=[jax.ShapeDtypeStruct(s, BF16) for s in...]
  transfers between devices with their start and end apart: 3 -> 2, of which waited for: 2 -> 1; matrix products, arithmetic and copies ran while one was open for 0% -> 0% of each run, Pallas kernels for 1% -> 1%
where the time goes in v9:
time: 185 us; the launch traced here: 184 us
  blocking collectives  165 us (89%)
  Pallas kernels  8.83 us (5%)
  starting transfers between devices  6.06 us (3%)
  local copies, waits for them, and re-layouts  2.5 us (1%)
  waiting for transfers between devices  2.2 us (1%)
    all_to_all x1, blocking collectives, shards(): msg = lax.all_to_all(msg, TO_CHANNELS[0], 0, 0, tiled=True)  54.2 us
    all_to_all x1, blocking collectives, shards(): msg = lax.all_to_all(msg, TO_CHANNELS[1], 0, 0, tiled=True)  40 us
    all_to_all x1, blocking collectives, shards(): lax.all_to_all(product.reshape(128, 8, 128), TO_POSITIONS[1], 0, 0, tiled...  30.2 us
    all_to_all x1, blocking collectives, shards(): lax.all_to_all(product.reshape(128, 8, 128), TO_POSITIONS[0], 0, 0, tiled...  29.1 us
    pallas_call x7, Pallas kernels, call(): pl.pallas_call(kernel, out_shape=[jax.ShapeDtypeStruct(s, BF16) for s in...  8.83 us
  transfers between devices with their start and end apart: 2, of which 1 were waited for; matrix products, arithmetic and copies ran while one was open for 0% of the time, Pallas kernels for 1%

profile of v9, /device:TPU:32, one launch (start us, length us, event | category | flops | bytes accessed | tf_op | source)
XLA Modules:
  0.0 184.4 jit_solution(4707350288156665133)
XLA Ops:
  0.0 0.0 copy-start.3
  0.0 1.0 copy-done.3
  1.0 0.0 copy-start.5
  1.0 0.9 copy-done.5
  1.9 1.5 edges.1
  3.4 54.2 %all_to_all.20 = bf16[128,7,2,128]{3,2,1,0:T(2,128)(2,1)S(1)} all-to-all(bf16[128,7,2,128]{3,2,1,0:T(2,128)(2,1)S(1)} %get-tuple-element.15), channel_id=1, replica_groups=mesh['y1'=2,'y0'=2,'zh'=4,'core'=2,'zl'=4,'x1'=2,'x0'=2] {'x1','x0','zl'..., dimensions={0} | all-to-all | bytes 917504 | tf_op jit(solution)/shard_map/all_to_all | solution.py:270
  57.6 0.2 slice.12
  57.8 0.0 copy-start.2
  57.8 0.0 copy-start.7
  57.8 2.7 %collective-permute-start = (bf16[128,8,128]{2,1,0:T(8,128)(2,1)S(1)}, bf16[128,8,128]{2,1,0:T(8,128)(2,1)S(1)}, u32[]{:S(2)}, u32[]{:S(2)}) collective-permute-start(bf16[128,8,128]{2,1,0:T(8,128)(2,1)S(1)} %bitcast.22), channel_id=1, source_target_pairs={{0,128},{128,0},{1,129},{129,1},{2,130},{130,2},{3,131},{131,3},{4... | collective-permute-start | bytes 786440 | tf_op jit(solution)/shard_map/ppermute | solution.py:272
  60.6 2.2 %all_gather.15 = bf16[256,8,128]{2,1,0:T(8,128)(2,1)S(1)} all-gather(bf16[128,8,128]{2,1,0:T(8,128)(2,1)S(1)} %bitcast.23), channel_id=1, replica_groups=mesh['y1'=2,'y0'=2,'zh'=4,'core'=2,'zl'=4,'x1'=2,'x0'=2] {'core'}, dimensions={0}, use_global_device_ids=true | all-gather | bytes 786432 | tf_op jit(solution)/shard_map/all_gather | solution.py:273
  62.8 0.0 copy-done.2
  62.8 0.0 copy-done.7
  62.8 1.3 outgoing_near.1
  64.0 2.2 %collective-permute-done = bf16[128,8,128]{2,1,0:T(8,128)(2,1)S(1)} collective-permute-done((bf16[128,8,128]{2,1,0:T(8,128)(2,1)S(1)}, bf16[128,8,128]{2,1,0:T(8,128)(2,1)S(1)}, u32[]{:S(2)}, u32[]{:S(2)}) %collective-permute-start) | collective-permute-done | bytes 262176 | tf_op jit(solution)/shard_map/ppermute | solution.py:272
  66.2 2.2 %all_gather.16 = bf16[256,8,128]{2,1,0:T(8,128)(2,1)S(1)} all-gather(bf16[128,8,128]{2,1,0:T(8,128)(2,1)S(1)} %collective-permute-done), channel_id=1, replica_groups=mesh['y1'=2,'y0'=2,'zh'=4,'core'=2,'zl'=4,'x1'=2,'x0'=2] {'core'}, dimensions={0}, use_global_device_ids=true | all-gather | bytes 786432 | tf_op jit(solution)/shard_map/all_gather | solution.py:278
  68.4 1.1 outgoing_far.1
  69.5 0.0 copy-start.4
  69.5 0.0 copy-start.6
  69.6 29.1 %all_to_all.21.x_ref = bf16[128,8,128]{2,1,0:T(8,128)(2,1)S(1)} all-to-all(bf16[128,8,128]{2,1,0:T(8,128)(2,1)S(1)} %bitcast.21), channel_id=1, replica_groups=mesh['y1'=2,'y0'=2,'zh'=4,'core'=2,'zl'=4,'x1'=2,'x0'=2] {'zl','y1','zh'..., dimensions={0} | all-to-all | bytes 524288 | tf_op jit(solution)/shard_map/all_to_all | solution.py:283
  98.7 0.0 copy-done.4
  98.7 0.0 copy-done.6
  98.7 1.7 update_edges.1
  100.3 40.0 %all_to_all.22 = bf16[128,7,2,128]{3,2,1,0:T(2,128)(2,1)S(1)} all-to-all(bf16[128,7,2,128]{3,2,1,0:T(2,128)(2,1)S(1)} %get-tuple-element.20), channel_id=1, replica_groups=mesh['y1'=2,'y0'=2,'zh'=4,'core'=2,'zl'=4,'x1'=2,'x0'=2] {'x1','zl','zh'..., dimensions={0} | all-to-all | bytes 917504 | tf_op jit(solution)/shard_map/all_to_all | solution.py:287
  140.3 0.4 fusion
  140.7 0.0 copy-start
  140.7 3.3 %collective-permute-start.1 = (bf16[128,8,128]{2,1,0:T(8,128)(2,1)S(1)}, bf16[128,8,128]{2,1,0:T(8,128)(2,1)S(1)}, u32[]{:S(2)}, u32[]{:S(2)}) collective-permute-start(bf16[128,8,128]{2,1,0:T(8,128)(2,1)S(1)} %bitcast.24), channel_id=1, source_target_pairs={{0,1},{1,0},{2,3},{3,2},{4,5},{5,4},{6,7},{7,6},{8,9},{9,8},{10,11... | collective-permute-start | bytes 786440 | tf_op jit(solution)/shard_map/ppermute | solution.py:290
  144.0 2.2 %all_gather.18 = bf16[256,8,128]{2,1,0:T(8,128)(2,1)S(1)} all-gather(bf16[128,8,128]{2,1,0:T(8,128)(2,1)S(1)} %bitcast.25), channel_id=1, replica_groups=mesh['y1'=2,'y0'=2,'zh'=4,'core'=2,'zl'=4,'x1'=2,'x0'=2] {'core'}, dimensions={0}, use_global_device_ids=true | all-gather | bytes 786432 | tf_op jit(solution)/shard_map/all_gather | solution.py:291
  146.2 0.0 copy-start.1
  146.2 2.5 %all_gather.19 = bf16[256,8,128]{2,1,0:T(8,128)(2,1)S(1)} all-gather(bf16[128,8,128]{2,1,0:T(8,128)(2,1)S(1)} %bitcast.26), channel_id=1, replica_groups=mesh['y1'=2,'y0'=2,'zh'=4,'core'=2,'zl'=4,'x1'=2,'x0'=2] {'core'}, dimensions={0}, use_global_device_ids=true | all-gather | bytes 786432 | tf_op jit(solution)/shard_map/all_gather | solution.py:292
  148.7 0.0 copy-done
  148.7 0.0 copy-done.1
  148.7 1.2 incoming_near.1
  149.9 0.0 collective-permute-done.1
  149.9 2.2 %all_gather.17 = bf16[256,8,128]{2,1,0:T(8,128)(2,1)S(1)} all-gather(bf16[128,8,128]{2,1,0:T(8,128)(2,1)S(1)} %collective-permute-done.1), channel_id=1, replica_groups=mesh['y1'=2,'y0'=2,'zh'=4,'core'=2,'zl'=4,'x1'=2,'x0'=2] {'core'}, dimensions={0}, use_global_device_ids=true | all-gather | bytes 786432 | tf_op jit(solution)/shard_map/all_gather | solution.py:297
  152.1 1.0 incoming_far.1
  153.1 30.2 %all_to_all.23.x_ref = bf16[128,8,128]{2,1,0:T(8,128)(2,1)S(1)} all-to-all(bf16[128,8,128]{2,1,0:T(8,128)(2,1)S(1)} %bitcast.20), channel_id=1, replica_groups=mesh['y1'=2,'y0'=2,'zh'=4,'core'=2,'zl'=4,'x1'=2,'x0'=2] {'zl','y1','y0'..., dimensions={0} | all-to-all | bytes 524288 | tf_op jit(solution)/shard_map/all_to_all | solution.py:302
  183.3 1.2 update.1
Async XLA Ops:
  0.0 1.0 copy-start.3
  1.0 0.9 copy-start.5
  57.8 4.9 %copy-start.2 = (bf16[256,384]{1,0:T(8,128)(2,1)S(1)}, bf16[256,384]{1,0:T(8,128)(2,1)}, u32[]{:S(2)}) copy-start(bf16[256,384]{1,0:T(8,128)(2,1)} %constant.20.clone.spread_ref) | copy-start | bytes 589828
  57.8 4.9 %copy-start.7 = (bf16[384,256]{1,0:T(8,128)(2,1)S(1)}, bf16[384,256]{1,0:T(8,128)(2,1)}, u32[]{:S(2)}) copy-start(bf16[384,256]{1,0:T(8,128)(2,1)} %constant.22.clone.gather_ref) | copy-start | bytes 589828
  57.8 8.4 %collective-permute-start = (bf16[128,8,128]{2,1,0:T(8,128)(2,1)S(1)}, bf16[128,8,128]{2,1,0:T(8,128)(2,1)S(1)}, u32[]{:S(2)}, u32[]{:S(2)}) collective-permute-start(bf16[128,8,128]{2,1,0:T(8,128)(2,1)S(1)} %bitcast.22), channel_id=1, source_target_pairs={{0,128},{128,0},{1,129},{129,1},{2,130},{130,2},{3,131},{131,3},{4... | collective-permute-start | bytes 786440 | tf_op jit(solution)/shard_map/ppermute | solution.py:272
  69.5 29.2 %copy-start.4 = (bf16[2,128,640]{2,1,0:T(8,128)(2,1)S(1)}, bf16[2,128,640]{2,1,0:T(8,128)(2,1)}, u32[]{:S(2)}) copy-start(bf16[2,128,640]{2,1,0:T(8,128)(2,1)} %w_ref.3) | copy-start | bytes 983044
  69.5 29.1 %copy-start.6 = (bf16[2,128,128]{2,1,0:T(8,128)(2,1)S(1)}, bf16[2,128,128]{2,1,0:T(8,128)(2,1)}, u32[]{:S(2)}) copy-start(bf16[2,128,128]{2,1,0:T(8,128)(2,1)} %wo_ref.3) | copy-start | bytes 196612
  140.7 8.0 %copy-start = (bf16[2,512,384]{2,1,0:T(8,128)(2,1)S(1)}, bf16[2,512,384]{2,1,0:T(8,128)(2,1)}, u32[]{:S(2)}) copy-start(bf16[2,512,384]{2,1,0:T(8,128)(2,1)} %constant.23.clone.rows_ref) | copy-start | bytes 2359300
  140.7 9.2 %collective-permute-start.1 = (bf16[128,8,128]{2,1,0:T(8,128)(2,1)S(1)}, bf16[128,8,128]{2,1,0:T(8,128)(2,1)S(1)}, u32[]{:S(2)}, u32[]{:S(2)}) collective-permute-start(bf16[128,8,128]{2,1,0:T(8,128)(2,1)S(1)} %bitcast.24), channel_id=1, source_target_pairs={{0,1},{1,0},{2,3},{3,2},{4,5},{5,4},{6,7},{7,6},{8,9},{9,8},{10,11... | collective-permute-start | bytes 786440 | tf_op jit(solution)/shard_map/ppermute | solution.py:290
  146.2 2.5 %copy-start.1 = (bf16[384,256]{1,0:T(8,128)(2,1)S(1)}, bf16[384,256]{1,0:T(8,128)(2,1)}, u32[]{:S(2)}) copy-start(bf16[384,256]{1,0:T(8,128)(2,1)} %constant.21.clone.gather_ref) | copy-start | bytes 589828

commit v10 on v9

--- a/solution.py
+++ b/solution.py
@@ -286,9 +286,11 @@
     )
     msg = lax.all_to_all(msg, TO_CHANNELS[1], 0, 0, tiled=True)
     rows = jnp.asarray(spread_rows(), BF16)
-    left, right = msg[:, 3:].reshape(C, 8, 128), msg[:, :4].reshape(C, 8, 128)
+    left = msg[:, 3:].reshape(C, 8, 128)
     far = lax.ppermute(left, "x0", SWAP)
     left = lax.all_gather(left, "core", axis=0, tiled=True).reshape(2, 8, 128, 128)
+    msg, left = lax.optimization_barrier((msg, left))
+    right = msg[:, :4].reshape(C, 8, 128)
     right = lax.all_gather(right, "core", axis=0, tiled=True).reshape(2, 8, 128, 128)
     right, near = call(
         incoming_near_kernel, [(768, 512), (8, 4, 2, 8, 128)], (core, left, right, table, rows, back),

time: 185 us -> 185 us (level)
  no operation moved by 1% of the time
where the time goes in v10:
time: 185 us; the launch traced here: 184 us
  blocking collectives  165 us (89%)
  Pallas kernels  8.83 us (5%)
  starting transfers between devices  5.93 us (3%)
  local copies, waits for them, and re-layouts  2.5 us (1%)
  waiting for transfers between devices  2.2 us (1%)
    all_to_all x1, blocking collectives, shards(): msg = lax.all_to_all(msg, TO_CHANNELS[0], 0, 0, tiled=True)  54.2 us
    all_to_all x1, blocking collectives, shards(): msg = lax.all_to_all(msg, TO_CHANNELS[1], 0, 0, tiled=True)  40 us
    all_to_all x1, blocking collectives, shards(): lax.all_to_all(product.reshape(128, 8, 128), TO_POSITIONS[1], 0, 0, tiled...  30.2 us
    all_to_all x1, blocking collectives, shards(): lax.all_to_all(product.reshape(128, 8, 128), TO_POSITIONS[0], 0, 0, tiled...  29.1 us
    pallas_call x7, Pallas kernels, call(): pl.pallas_call(kernel, out_shape=[jax.ShapeDtypeStruct(s, BF16) for s in...  8.83 us
  transfers between devices with their start and end apart: 2, of which 1 were waited for; matrix products, arithmetic and copies ran while one was open for 0% of the time, Pallas kernels for 1%

profile of v10, /device:TPU:32, one launch (start us, length us, event | category | flops | bytes accessed | tf_op | source)
XLA Modules:
  0.0 184.3 jit_solution(12378038023500256442)
XLA Ops:
  0.0 0.0 copy-start.3
  0.0 1.0 copy-done.3
  1.0 0.0 copy-start.5
  1.0 0.9 copy-done.5
  1.9 1.5 edges.1
  3.4 54.2 %all_to_all.20 = bf16[128,7,2,128]{3,2,1,0:T(2,128)(2,1)S(1)} all-to-all(bf16[128,7,2,128]{3,2,1,0:T(2,128)(2,1)S(1)} %get-tuple-element.17), channel_id=1, replica_groups=mesh['y1'=2,'y0'=2,'zh'=4,'core'=2,'zl'=4,'x1'=2,'x0'=2] {'x1','x0','zl'..., dimensions={0} | all-to-all | bytes 917504 | tf_op jit(solution)/shard_map/all_to_all | solution.py:270
  57.6 0.2 slice.12
  57.8 0.0 copy-start.2
  57.8 0.0 copy-start.7
  57.8 2.7 %collective-permute-start = (bf16[128,8,128]{2,1,0:T(8,128)(2,1)S(1)}, bf16[128,8,128]{2,1,0:T(8,128)(2,1)S(1)}, u32[]{:S(2)}, u32[]{:S(2)}) collective-permute-start(bf16[128,8,128]{2,1,0:T(8,128)(2,1)S(1)} %bitcast.24), channel_id=1, source_target_pairs={{0,128},{128,0},{1,129},{129,1},{2,130},{130,2},{3,131},{131,3},{4... | collective-permute-start | bytes 786440 | tf_op jit(solution)/shard_map/ppermute | solution.py:272
  60.6 2.2 %all_gather.15 = bf16[256,8,128]{2,1,0:T(8,128)(2,1)S(1)} all-gather(bf16[128,8,128]{2,1,0:T(8,128)(2,1)S(1)} %bitcast.25), channel_id=1, replica_groups=mesh['y1'=2,'y0'=2,'zh'=4,'core'=2,'zl'=4,'x1'=2,'x0'=2] {'core'}, dimensions={0}, use_global_device_ids=true | all-gather | bytes 786432 | tf_op jit(solution)/shard_map/all_gather | solution.py:273
  62.8 0.0 copy-done.2
  62.8 0.0 copy-done.7
  62.8 1.3 outgoing_near.1
  64.0 2.2 %collective-permute-done = bf16[128,8,128]{2,1,0:T(8,128)(2,1)S(1)} collective-permute-done((bf16[128,8,128]{2,1,0:T(8,128)(2,1)S(1)}, bf16[128,8,128]{2,1,0:T(8,128)(2,1)S(1)}, u32[]{:S(2)}, u32[]{:S(2)}) %collective-permute-start) | collective-permute-done | bytes 262176 | tf_op jit(solution)/shard_map/ppermute | solution.py:272
  66.2 2.2 %all_gather.16 = bf16[256,8,128]{2,1,0:T(8,128)(2,1)S(1)} all-gather(bf16[128,8,128]{2,1,0:T(8,128)(2,1)S(1)} %collective-permute-done), channel_id=1, replica_groups=mesh['y1'=2,'y0'=2,'zh'=4,'core'=2,'zl'=4,'x1'=2,'x0'=2] {'core'}, dimensions={0}, use_global_device_ids=true | all-gather | bytes 786432 | tf_op jit(solution)/shard_map/all_gather | solution.py:278
  68.4 1.1 outgoing_far.1
  69.5 0.0 copy-start.4
  69.5 0.0 copy-start.6
  69.6 29.1 %all_to_all.21.x_ref = bf16[128,8,128]{2,1,0:T(8,128)(2,1)S(1)} all-to-all(bf16[128,8,128]{2,1,0:T(8,128)(2,1)S(1)} %bitcast.21), channel_id=1, replica_groups=mesh['y1'=2,'y0'=2,'zh'=4,'core'=2,'zl'=4,'x1'=2,'x0'=2] {'zl','y1','zh'..., dimensions={0} | all-to-all | bytes 524288 | tf_op jit(solution)/shard_map/all_to_all | solution.py:283
  98.7 0.0 copy-done.4
  98.7 0.0 copy-done.6
  98.7 1.7 update_edges.1
  100.3 40.0 %all_to_all.22 = bf16[128,7,2,128]{3,2,1,0:T(2,128)(2,1)S(1)} all-to-all(bf16[128,7,2,128]{3,2,1,0:T(2,128)(2,1)S(1)} %get-tuple-element.22), channel_id=1, replica_groups=mesh['y1'=2,'y0'=2,'zh'=4,'core'=2,'zl'=4,'x1'=2,'x0'=2] {'x1','zl','zh'..., dimensions={0} | all-to-all | bytes 917504 | tf_op jit(solution)/shard_map/all_to_all | solution.py:287
  140.3 0.2 slice.13
  140.5 3.2 %collective-permute-start.1 = (bf16[128,8,128]{2,1,0:T(8,128)(2,1)S(1)}, bf16[128,8,128]{2,1,0:T(8,128)(2,1)S(1)}, u32[]{:S(2)}, u32[]{:S(2)}) collective-permute-start(bf16[128,8,128]{2,1,0:T(8,128)(2,1)S(1)} %bitcast.22), channel_id=1, source_target_pairs={{0,1},{1,0},{2,3},{3,2},{4,5},{5,4},{6,7},{7,6},{8,9},{9,8},{10,11... | collective-permute-start | bytes 786440 | tf_op jit(solution)/shard_map/ppermute | solution.py:290
  143.7 2.2 %all_gather.18 = bf16[256,8,128]{2,1,0:T(8,128)(2,1)S(1)} all-gather(bf16[128,8,128]{2,1,0:T(8,128)(2,1)S(1)} %bitcast.23), channel_id=1, replica_groups=mesh['y1'=2,'y0'=2,'zh'=4,'core'=2,'zl'=4,'x1'=2,'x0'=2] {'core'}, dimensions={0}, use_global_device_ids=true | all-gather | bytes 786432 | tf_op jit(solution)/shard_map/all_gather | solution.py:291
  145.9 0.0 copy-start
  145.9 0.2 slice.11
  146.1 0.0 copy-start.1
  146.1 2.5 %all_gather.19 = bf16[256,8,128]{2,1,0:T(8,128)(2,1)S(1)} all-gather(bf16[128,8,128]{2,1,0:T(8,128)(2,1)S(1)} %bitcast.26), channel_id=1, replica_groups=mesh['y1'=2,'y0'=2,'zh'=4,'core'=2,'zl'=4,'x1'=2,'x0'=2] {'core'}, dimensions={0}, use_global_device_ids=true | all-gather | bytes 786432 | tf_op jit(solution)/shard_map/all_gather | solution.py:294
  148.6 0.0 copy-done
  148.6 0.0 copy-done.1
  148.6 1.2 incoming_near.1
  149.8 0.0 collective-permute-done.1
  149.8 2.2 %all_gather.17 = bf16[256,8,128]{2,1,0:T(8,128)(2,1)S(1)} all-gather(bf16[128,8,128]{2,1,0:T(8,128)(2,1)S(1)} %collective-permute-done.1), channel_id=1, replica_groups=mesh['y1'=2,'y0'=2,'zh'=4,'core'=2,'zl'=4,'x1'=2,'x0'=2] {'core'}, dimensions={0}, use_global_device_ids=true | all-gather | bytes 786432 | tf_op jit(solution)/shard_map/all_gather | solution.py:299
  152.0 1.0 incoming_far.1
  153.0 30.2 %all_to_all.23.x_ref = bf16[128,8,128]{2,1,0:T(8,128)(2,1)S(1)} all-to-all(bf16[128,8,128]{2,1,0:T(8,128)(2,1)S(1)} %bitcast.20), channel_id=1, replica_groups=mesh['y1'=2,'y0'=2,'zh'=4,'core'=2,'zl'=4,'x1'=2,'x0'=2] {'zl','y1','y0'..., dimensions={0} | all-to-all | bytes 524288 | tf_op jit(solution)/shard_map/all_to_all | solution.py:304
  183.2 1.2 update.1
Async XLA Ops:
  0.0 1.0 copy-start.3
  1.0 0.9 copy-start.5
  57.8 4.9 %copy-start.2 = (bf16[256,384]{1,0:T(8,128)(2,1)S(1)}, bf16[256,384]{1,0:T(8,128)(2,1)}, u32[]{:S(2)}) copy-start(bf16[256,384]{1,0:T(8,128)(2,1)} %constant.20.clone.spread_ref) | copy-start | bytes 589828
  57.8 4.9 %copy-start.7 = (bf16[384,256]{1,0:T(8,128)(2,1)S(1)}, bf16[384,256]{1,0:T(8,128)(2,1)}, u32[]{:S(2)}) copy-start(bf16[384,256]{1,0:T(8,128)(2,1)} %constant.22.clone.gather_ref) | copy-start | bytes 589828
  57.8 8.4 %collective-permute-start = (bf16[128,8,128]{2,1,0:T(8,128)(2,1)S(1)}, bf16[128,8,128]{2,1,0:T(8,128)(2,1)S(1)}, u32[]{:S(2)}, u32[]{:S(2)}) collective-permute-start(bf16[128,8,128]{2,1,0:T(8,128)(2,1)S(1)} %bitcast.24), channel_id=1, source_target_pairs={{0,128},{128,0},{1,129},{129,1},{2,130},{130,2},{3,131},{131,3},{4... | collective-permute-start | bytes 786440 | tf_op jit(solution)/shard_map/ppermute | solution.py:272
  69.5 29.2 %copy-start.4 = (bf16[2,128,640]{2,1,0:T(8,128)(2,1)S(1)}, bf16[2,128,640]{2,1,0:T(8,128)(2,1)}, u32[]{:S(2)}) copy-start(bf16[2,128,640]{2,1,0:T(8,128)(2,1)} %w_ref.3) | copy-start | bytes 983044
  69.5 29.1 %copy-start.6 = (bf16[2,128,128]{2,1,0:T(8,128)(2,1)S(1)}, bf16[2,128,128]{2,1,0:T(8,128)(2,1)}, u32[]{:S(2)}) copy-start(bf16[2,128,128]{2,1,0:T(8,128)(2,1)} %wo_ref.3) | copy-start | bytes 196612
  140.5 9.3 %collective-permute-start.1 = (bf16[128,8,128]{2,1,0:T(8,128)(2,1)S(1)}, bf16[128,8,128]{2,1,0:T(8,128)(2,1)S(1)}, u32[]{:S(2)}, u32[]{:S(2)}) collective-permute-start(bf16[128,8,128]{2,1,0:T(8,128)(2,1)S(1)} %bitcast.22), channel_id=1, source_target_pairs={{0,1},{1,0},{2,3},{3,2},{4,5},{5,4},{6,7},{7,6},{8,9},{9,8},{10,11... | collective-permute-start | bytes 786440 | tf_op jit(solution)/shard_map/ppermute | solution.py:290
  145.9 2.7 %copy-start = (bf16[2,512,384]{2,1,0:T(8,128)(2,1)S(1)}, bf16[2,512,384]{2,1,0:T(8,128)(2,1)}, u32[]{:S(2)}) copy-start(bf16[2,512,384]{2,1,0:T(8,128)(2,1)} %constant.23.clone.rows_ref) | copy-start | bytes 2359300
  146.1 2.5 %copy-start.1 = (bf16[384,256]{1,0:T(8,128)(2,1)S(1)}, bf16[384,256]{1,0:T(8,128)(2,1)}, u32[]{:S(2)}) copy-start(bf16[384,256]{1,0:T(8,128)(2,1)} %constant.21.clone.gather_ref) | copy-start | bytes 589828

commit v11 on v10

--- a/solution.py
+++ b/solution.py
@@ -264,7 +264,7 @@
     y0, x0, core = (lax.axis_index(name).astype(jnp.int32)[None] for name in ("y0", "x0", "core"))
 
     msg, gate, flat = call(
-        first_kernel, [MSG, FLAT, FLAT], (y0, x0, core, pair_rep, in_weights), "edges",
+        first_kernel, [MSG, FLAT, FLAT], (y0, x0, core, pair_rep, in_weights[:1]), "edges",
         scalars=3,
     )
     msg = lax.all_to_all(msg, TO_CHANNELS[0], 0, 0, tiled=True)

time: 185 us -> 184 us (level)
    unnamed x16 -> x14, local copies, waits for them, and re-layouts: 1.96 us -> 0.09 us
where the time goes in v11:
time: 184 us; the launch traced here: 183 us
  blocking collectives  165 us (90%)
  Pallas kernels  8.84 us (5%)
  starting transfers between devices  5.93 us (3%)
  waiting for transfers between devices  2.2 us (1%)
    all_to_all x1, blocking collectives, shards(): msg = lax.all_to_all(msg, TO_CHANNELS[0], 0, 0, tiled=True)  54.2 us
    all_to_all x1, blocking collectives, shards(): msg = lax.all_to_all(msg, TO_CHANNELS[1], 0, 0, tiled=True)  40 us
    all_to_all x1, blocking collectives, shards(): lax.all_to_all(product.reshape(128, 8, 128), TO_POSITIONS[1], 0, 0, tiled...  30.2 us
    all_to_all x1, blocking collectives, shards(): lax.all_to_all(product.reshape(128, 8, 128), TO_POSITIONS[0], 0, 0, tiled...  29.1 us
    pallas_call x7, Pallas kernels, call(): pl.pallas_call(kernel, out_shape=[jax.ShapeDtypeStruct(s, BF16) for s in...  8.84 us
  transfers between devices with their start and end apart: 2, of which 1 were waited for; matrix products, arithmetic and copies ran while one was open for 0% of the time, Pallas kernels for 1%

profile of v11, /device:TPU:32, one launch (start us, length us, event | category | flops | bytes accessed | tf_op | source)
XLA Modules:
  0.0 183.4 jit_solution(3584755940421355366)
XLA Ops:
  0.0 0.0 copy-start.4
  0.0 1.0 slice.12.w_ref
  1.0 0.0 copy-done.4
  1.0 1.5 edges.1
  2.5 54.2 %all_to_all.20 = bf16[128,7,2,128]{3,2,1,0:T(2,128)(2,1)S(1)} all-to-all(bf16[128,7,2,128]{3,2,1,0:T(2,128)(2,1)S(1)} %get-tuple-element.17), channel_id=1, replica_groups=mesh['y1'=2,'y0'=2,'zh'=4,'core'=2,'zl'=4,'x1'=2,'x0'=2] {'x1','x0','zl'..., dimensions={0} | all-to-all | bytes 917504 | tf_op jit(solution)/shard_map/all_to_all | solution.py:270
  56.7 0.2 slice.16
  56.9 0.0 copy-start.2
  56.9 0.0 copy-start.6
  56.9 2.7 %collective-permute-start = (bf16[128,8,128]{2,1,0:T(8,128)(2,1)S(1)}, bf16[128,8,128]{2,1,0:T(8,128)(2,1)S(1)}, u32[]{:S(2)}, u32[]{:S(2)}) collective-permute-start(bf16[128,8,128]{2,1,0:T(8,128)(2,1)S(1)} %bitcast.24), channel_id=1, source_target_pairs={{0,128},{128,0},{1,129},{129,1},{2,130},{130,2},{3,131},{131,3},{4... | collective-permute-start | bytes 786440 | tf_op jit(solution)/shard_map/ppermute | solution.py:272
  59.7 2.2 %all_gather.15 = bf16[256,8,128]{2,1,0:T(8,128)(2,1)S(1)} all-gather(bf16[128,8,128]{2,1,0:T(8,128)(2,1)S(1)} %bitcast.25), channel_id=1, replica_groups=mesh['y1'=2,'y0'=2,'zh'=4,'core'=2,'zl'=4,'x1'=2,'x0'=2] {'core'}, dimensions={0}, use_global_device_ids=true | all-gather | bytes 786432 | tf_op jit(solution)/shard_map/all_gather | solution.py:273
  61.9 0.0 copy-done.2
  61.9 0.0 copy-done.6
  61.9 1.3 outgoing_near.1
  63.1 2.2 %collective-permute-done = bf16[128,8,128]{2,1,0:T(8,128)(2,1)S(1)} collective-permute-done((bf16[128,8,128]{2,1,0:T(8,128)(2,1)S(1)}, bf16[128,8,128]{2,1,0:T(8,128)(2,1)S(1)}, u32[]{:S(2)}, u32[]{:S(2)}) %collective-permute-start) | collective-permute-done | bytes 262176 | tf_op jit(solution)/shard_map/ppermute | solution.py:272
  65.3 2.2 %all_gather.16 = bf16[256,8,128]{2,1,0:T(8,128)(2,1)S(1)} all-gather(bf16[128,8,128]{2,1,0:T(8,128)(2,1)S(1)} %collective-permute-done), channel_id=1, replica_groups=mesh['y1'=2,'y0'=2,'zh'=4,'core'=2,'zl'=4,'x1'=2,'x0'=2] {'core'}, dimensions={0}, use_global_device_ids=true | all-gather | bytes 786432 | tf_op jit(solution)/shard_map/all_gather | solution.py:278
  67.5 1.1 outgoing_far.1
  68.6 0.0 copy-start.3
  68.6 0.0 copy-start.5
  68.7 29.1 %all_to_all.21.x_ref = bf16[128,8,128]{2,1,0:T(8,128)(2,1)S(1)} all-to-all(bf16[128,8,128]{2,1,0:T(8,128)(2,1)S(1)} %bitcast.21), channel_id=1, replica_groups=mesh['y1'=2,'y0'=2,'zh'=4,'core'=2,'zl'=4,'x1'=2,'x0'=2] {'zl','y1','zh'..., dimensions={0} | all-to-all | bytes 524288 | tf_op jit(solution)/shard_map/all_to_all | solution.py:283
  97.8 0.0 copy-done.3
  97.8 0.0 copy-done.5
  97.8 1.7 update_edges.1
  99.4 40.0 %all_to_all.22 = bf16[128,7,2,128]{3,2,1,0:T(2,128)(2,1)S(1)} all-to-all(bf16[128,7,2,128]{3,2,1,0:T(2,128)(2,1)S(1)} %get-tuple-element.22), channel_id=1, replica_groups=mesh['y1'=2,'y0'=2,'zh'=4,'core'=2,'zl'=4,'x1'=2,'x0'=2] {'x1','zl','zh'..., dimensions={0} | all-to-all | bytes 917504 | tf_op jit(solution)/shard_map/all_to_all | solution.py:287
  139.4 0.2 slice.17
  139.6 3.2 %collective-permute-start.1 = (bf16[128,8,128]{2,1,0:T(8,128)(2,1)S(1)}, bf16[128,8,128]{2,1,0:T(8,128)(2,1)S(1)}, u32[]{:S(2)}, u32[]{:S(2)}) collective-permute-start(bf16[128,8,128]{2,1,0:T(8,128)(2,1)S(1)} %bitcast.22), channel_id=1, source_target_pairs={{0,1},{1,0},{2,3},{3,2},{4,5},{5,4},{6,7},{7,6},{8,9},{9,8},{10,11... | collective-permute-start | bytes 786440 | tf_op jit(solution)/shard_map/ppermute | solution.py:290
  142.8 2.2 %all_gather.18 = bf16[256,8,128]{2,1,0:T(8,128)(2,1)S(1)} all-gather(bf16[128,8,128]{2,1,0:T(8,128)(2,1)S(1)} %bitcast.23), channel_id=1, replica_groups=mesh['y1'=2,'y0'=2,'zh'=4,'core'=2,'zl'=4,'x1'=2,'x0'=2] {'core'}, dimensions={0}, use_global_device_ids=true | all-gather | bytes 786432 | tf_op jit(solution)/shard_map/all_gather | solution.py:291
  145.0 0.0 copy-start
  145.0 0.2 slice.15
  145.2 0.0 copy-start.1
  145.2 2.5 %all_gather.19 = bf16[256,8,128]{2,1,0:T(8,128)(2,1)S(1)} all-gather(bf16[128,8,128]{2,1,0:T(8,128)(2,1)S(1)} %bitcast.26), channel_id=1, replica_groups=mesh['y1'=2,'y0'=2,'zh'=4,'core'=2,'zl'=4,'x1'=2,'x0'=2] {'core'}, dimensions={0}, use_global_device_ids=true | all-gather | bytes 786432 | tf_op jit(solution)/shard_map/all_gather | solution.py:294
  147.7 0.0 copy-done
  147.7 0.0 copy-done.1
  147.7 1.2 incoming_near.1
  148.9 0.0 collective-permute-done.1
  148.9 2.2 %all_gather.17 = bf16[256,8,128]{2,1,0:T(8,128)(2,1)S(1)} all-gather(bf16[128,8,128]{2,1,0:T(8,128)(2,1)S(1)} %collective-permute-done.1), channel_id=1, replica_groups=mesh['y1'=2,'y0'=2,'zh'=4,'core'=2,'zl'=4,'x1'=2,'x0'=2] {'core'}, dimensions={0}, use_global_device_ids=true | all-gather | bytes 786432 | tf_op jit(solution)/shard_map/all_gather | solution.py:299
  151.1 1.0 incoming_far.1
  152.1 30.2 %all_to_all.23.x_ref = bf16[128,8,128]{2,1,0:T(8,128)(2,1)S(1)} all-to-all(bf16[128,8,128]{2,1,0:T(8,128)(2,1)S(1)} %bitcast.20), channel_id=1, replica_groups=mesh['y1'=2,'y0'=2,'zh'=4,'core'=2,'zl'=4,'x1'=2,'x0'=2] {'zl','y1','y0'..., dimensions={0} | all-to-all | bytes 524288 | tf_op jit(solution)/shard_map/all_to_all | solution.py:304
  182.2 1.2 update.1
Async XLA Ops:
  0.0 1.0 copy-start.4
  56.9 4.9 %copy-start.2 = (bf16[256,384]{1,0:T(8,128)(2,1)S(1)}, bf16[256,384]{1,0:T(8,128)(2,1)}, u32[]{:S(2)}) copy-start(bf16[256,384]{1,0:T(8,128)(2,1)} %constant.20.clone.spread_ref) | copy-start | bytes 589828
  56.9 4.9 %copy-start.6 = (bf16[384,256]{1,0:T(8,128)(2,1)S(1)}, bf16[384,256]{1,0:T(8,128)(2,1)}, u32[]{:S(2)}) copy-start(bf16[384,256]{1,0:T(8,128)(2,1)} %constant.22.clone.gather_ref) | copy-start | bytes 589828
  56.9 8.4 %collective-permute-start = (bf16[128,8,128]{2,1,0:T(8,128)(2,1)S(1)}, bf16[128,8,128]{2,1,0:T(8,128)(2,1)S(1)}, u32[]{:S(2)}, u32[]{:S(2)}) collective-permute-start(bf16[128,8,128]{2,1,0:T(8,128)(2,1)S(1)} %bitcast.24), channel_id=1, source_target_pairs={{0,128},{128,0},{1,129},{129,1},{2,130},{130,2},{3,131},{131,3},{4... | collective-permute-start | bytes 786440 | tf_op jit(solution)/shard_map/ppermute | solution.py:272
  68.6 29.1 %copy-start.3 = (bf16[2,128,640]{2,1,0:T(8,128)(2,1)S(1)}, bf16[2,128,640]{2,1,0:T(8,128)(2,1)}, u32[]{:S(2)}) copy-start(bf16[2,128,640]{2,1,0:T(8,128)(2,1)} %w_ref.1) | copy-start | bytes 983044
  68.6 29.1 %copy-start.5 = (bf16[2,128,128]{2,1,0:T(8,128)(2,1)S(1)}, bf16[2,128,128]{2,1,0:T(8,128)(2,1)}, u32[]{:S(2)}) copy-start(bf16[2,128,128]{2,1,0:T(8,128)(2,1)} %wo_ref.3) | copy-start | bytes 196612
  139.6 9.3 %collective-permute-start.1 = (bf16[128,8,128]{2,1,0:T(8,128)(2,1)S(1)}, bf16[128,8,128]{2,1,0:T(8,128)(2,1)S(1)}, u32[]{:S(2)}, u32[]{:S(2)}) collective-permute-start(bf16[128,8,128]{2,1,0:T(8,128)(2,1)S(1)} %bitcast.22), channel_id=1, source_target_pairs={{0,1},{1,0},{2,3},{3,2},{4,5},{5,4},{6,7},{7,6},{8,9},{9,8},{10,11... | collective-permute-start | bytes 786440 | tf_op jit(solution)/shard_map/ppermute | solution.py:290
  145.0 2.7 %copy-start = (bf16[2,512,384]{2,1,0:T(8,128)(2,1)S(1)}, bf16[2,512,384]{2,1,0:T(8,128)(2,1)}, u32[]{:S(2)}) copy-start(bf16[2,512,384]{2,1,0:T(8,128)(2,1)} %constant.23.clone.rows_ref) | copy-start | bytes 2359300
  145.2 2.5 %copy-start.1 = (bf16[384,256]{1,0:T(8,128)(2,1)S(1)}, bf16[384,256]{1,0:T(8,128)(2,1)}, u32[]{:S(2)}) copy-start(bf16[384,256]{1,0:T(8,128)(2,1)} %constant.21.clone.gather_ref) | copy-start | bytes 589828
